TPU v7x, 512 devices: a whole 4x4x16 slice. The times are simulated.
512 devices in a mesh: seq: 64 (over x, z), head: 8 (over y, core).
Axes of the slice: x: 4, y: 4, z: 16, core: 2. Of those that a mesh axis runs over, the one named last changes fastest.
Arguments:
- tokens: bfloat16 [16384, 5376], P('seq', 'head'), may hold values from -6 to 6
- features: bfloat16 [512, 64, 1152], P('seq'), may hold values from -6 to 6
- starts: int32 [8], replicated, may hold values from 0 to 16128, as said below
- sources: int32 [8], replicated, may hold values from 0 to 56, as said below
- soft_gain: float32 [1152], replicated, may hold values from 0.25 to 1.75
- proj_weight: bfloat16 [1152, 5376], P(None, 'head'), may hold values from -0.1875 to 0.1875
- input_gain: float32 [5376], replicated, may hold values from 0.25 to 1.75
- query_weight: bfloat16 [5376, 2048], P('seq', 'head'), may hold values from -0.078125 to 0.078125
- key_weight: bfloat16 [5376, 1024], P('seq', 'head'), may hold values from -0.078125 to 0.078125
- value_weight: bfloat16 [5376, 1024], P('seq', 'head'), may hold values from -0.078125 to 0.078125
- query_gain: float32 [128], replicated, may hold values from 0.25 to 1.75
- key_gain: float32 [128], replicated, may hold values from 0.25 to 1.75
- out_weight: bfloat16 [2048, 5376], P('seq', 'head'), may hold values from -0.125 to 0.125
- post_gain: float32 [5376], P('head'), may hold values from 0.25 to 1.75
Outputs:
- layer_out: bfloat16 [16384, 5376], P('seq', 'head')
Inputs may be any that keep to these rules, and one draw needn't show every extreme that they name: Image i takes positions starts[i] to starts[i] + 255; the spans are in increasing order of i, do not intersect, and each crosses one boundary between sequence shards. Distinct multiples of 8; image i's patches fill feature rows sources[i] * 8 onward.
All inputs are finite; a program needn't handle non-finite values.
Results may differ from a plain program's by a relative error of at most 0.012.
Values may be sent and summed in bfloat16 or wider, within the bound.
No kernel may reach another device: no remote copies, remote signals or barrier semaphores. Data moves between devices by JAX's collectives and lax.ppermute only.
A program may use at most 64 MiB of HBM per device.

v0:
```python
import jax
import jax.numpy as jnp
from jax import lax
from jax.sharding import PartitionSpec as P

D = 5376
HEAD_DIM = 128
WINDOW = 1024
PATCH_SIDE = 64
POOL = 4
IMG_TOK = 256


EPSILON = 1e-06
QUERY_SCALE = 168.0 ** (-0.5)
ROPE_BASE = 10000.0


def shifted(value, axis, steps):
    count = lax.axis_size(axis)
    leading, last = (max(0, -steps), min(count, count - steps))
    return lax.ppermute(value, axis, [(source, source + steps) for source in range(leading, last)])


def rms_scale(inputs, scale_gain):
    return (
        inputs * lax.rsqrt(jnp.mean(inputs * inputs, axis=-1, keepdims=True) + EPSILON) * scale_gain
    )


def rotate(inputs, positions):
    half_dim = inputs.shape[-1] // 2
    frequency = ROPE_BASE ** (-jnp.arange(half_dim, dtype=jnp.float32) * 2.0 / inputs.shape[-1])
    angles = positions.astype(jnp.float32)[:, None] * frequency[None, :]
    cosine = jnp.cos(angles)[:, None, :]
    sine_part = jnp.sin(angles)[:, None, :]
    first_half = inputs[..., :half_dim]
    second = inputs[..., half_dim:]
    return jnp.concatenate(
        [first_half * cosine - second * sine_part, second * cosine + first_half * sine_part],
        axis=-1,
    )


def image_of(positions, starts):
    inside = (positions[:, None] >= starts[None, :]) & (
        positions[:, None] < starts[None, :] + IMG_TOK
    )
    labels = jnp.arange(1, starts.shape[0] + 1, dtype=jnp.int32)
    return jnp.sum(jnp.where(inside, labels[None, :], 0), axis=1) - 1


def allowed_keys(query_pos, key_pos, starts, total_rows):
    query_img = image_of(query_pos, starts)
    key_img = image_of(key_pos, starts)
    inside = (key_pos >= 0) & (key_pos < total_rows)
    in_window = query_pos[:, None] - key_pos[None, :] < WINDOW
    causal = key_pos[None, :] <= query_pos[:, None]
    same_image = (query_img[:, None] == key_img[None, :]) & (query_img[:, None] >= 0)
    return inside[None, :] & in_window & (causal | same_image)


def attend(queries, key_rows, values, allowed):
    scores = jnp.einsum("qgrd,kgd->grqk", queries, key_rows, preferred_element_type=jnp.float32)
    scores = jnp.where(allowed[None, None], scores, -jnp.inf)
    row_max = jnp.max(scores, axis=-1, keepdims=True)
    weights = jnp.exp(scores - row_max)
    row_sum = jnp.sum(weights, axis=-1)
    mixed_heads = jnp.einsum(
        "grqk,kgd->qgrd", weights.astype(jnp.bfloat16), values, preferred_element_type=jnp.float32
    )
    return (mixed_heads / jnp.transpose(row_sum, (2, 0, 1))[..., None]).astype(jnp.bfloat16)


def body(
    tokens,
    features,
    starts,
    sources,
    soft_gain,
    proj_weight,
    input_gain,
    query_weight,
    key_weight,
    value_weight,
    query_gain,
    key_gain,
    out_weight,
    post_gain,
):
    tok_rows = tokens.shape[0]
    seq_count = lax.axis_size("seq")
    seq_index = lax.axis_index("seq")
    total_rows = seq_count * tok_rows
    image_count = starts.shape[0]
    my_pos = seq_index * tok_rows + jnp.arange(tok_rows, dtype=jnp.int32)
    pooled_side = PATCH_SIDE // POOL
    pool_rows = features.shape[0] // POOL
    block_rows = pool_rows * pooled_side
    shards_each = pooled_side // pool_rows
    patch_grid = features.reshape(pool_rows, POOL, pooled_side, POOL, features.shape[2])
    pooled = jnp.sum(patch_grid, axis=(1, 3), dtype=jnp.float32).reshape(
        block_rows, features.shape[2]
    ) / (POOL * POOL)
    soft = rms_scale(pooled, soft_gain).astype(jnp.bfloat16)
    embedded = jnp.dot(soft, proj_weight, preferred_element_type=jnp.float32).astype(jnp.bfloat16)
    gathered = lax.all_gather(embedded, "seq", axis=0, tiled=True)
    my_image = image_of(my_pos, starts)
    image_ids = jnp.arange(image_count, dtype=jnp.int32)
    row_base = sources // shards_each * (block_rows * shards_each) - starts
    offset_rows = jnp.sum(
        jnp.where(my_image[:, None] == image_ids[None, :], row_base[None, :], 0), axis=1
    )
    row_index = jnp.where(my_image >= 0, offset_rows + my_pos, 0)
    picked = jnp.take(gathered, row_index, axis=0)
    residual = jnp.where((my_image >= 0)[:, None], picked, tokens)
    whole_rows = lax.all_gather(residual, "head", axis=1, tiled=True)
    normed = rms_scale(whole_rows.astype(jnp.float32), input_gain).astype(jnp.bfloat16)

    def add_rows(piece_rows):
        return jnp.dot(normed, piece_rows, preferred_element_type=jnp.float32)

    query_sum = add_rows(lax.all_gather(query_weight, "seq", axis=0, tiled=True))
    key_sum = add_rows(lax.all_gather(key_weight, "seq", axis=0, tiled=True))
    value_sum = add_rows(lax.all_gather(value_weight, "seq", axis=0, tiled=True))
    kv_local = key_weight.shape[1] // HEAD_DIM
    group_size = query_weight.shape[1] // key_weight.shape[1]
    queries = (
        rotate(
            rms_scale(query_sum.reshape(tok_rows, kv_local * group_size, HEAD_DIM), query_gain),
            my_pos,
        )
        * QUERY_SCALE
    )
    queries = queries.astype(jnp.bfloat16).reshape(tok_rows, kv_local, group_size, HEAD_DIM)
    own_keys = (
        rotate(rms_scale(key_sum.reshape(tok_rows, kv_local, HEAD_DIM), key_gain), my_pos)
        .astype(jnp.bfloat16)
        .reshape(tok_rows, kv_local * HEAD_DIM)
    )
    own_values = value_sum.astype(jnp.bfloat16)
    past_count = WINDOW // tok_rows
    key_value = (own_keys, own_values)
    earlier = [
        shifted((key_value[0], key_value[1]), "seq", step_back)
        for step_back in range(past_count, 0, -1)
    ]
    past_keys = jnp.concatenate([entry[0] for entry in earlier], axis=0)
    past_values = jnp.concatenate([entry[1] for entry in earlier], axis=0)
    later = [shifted((key_value[0], key_value[1]), "seq", -1)]
    all_keys = jnp.concatenate([past_keys, own_keys] + [entry[0] for entry in later], axis=0)
    all_values = jnp.concatenate([past_values, own_values] + [entry[1] for entry in later], axis=0)
    key_pos = (seq_index - past_count) * tok_rows + jnp.arange(all_keys.shape[0], dtype=jnp.int32)
    allowed = allowed_keys(my_pos, key_pos, starts, total_rows)
    attended = attend(
        queries,
        all_keys.reshape(-1, kv_local, HEAD_DIM),
        all_values.reshape(-1, kv_local, HEAD_DIM),
        allowed,
    )
    attended = attended.reshape(tok_rows, kv_local * group_size * HEAD_DIM)
    heads_all = lax.all_gather(attended, "head", axis=1, tiled=True)
    projected = jnp.dot(
        heads_all,
        lax.all_gather(out_weight, "seq", axis=0, tiled=True),
        preferred_element_type=jnp.float32,
    )
    squares = lax.psum(jnp.sum(projected * projected, axis=1), "head")
    post = projected * lax.rsqrt(squares[:, None] / D + EPSILON) * post_gain
    return (residual.astype(jnp.float32) + post).astype(jnp.bfloat16)


def solution(mesh):
    return jax.shard_map(
        body,
        mesh=mesh,
        in_specs=(
            P("seq", "head"),
            P("seq", None, None),
            P(),
            P(),
            P(),
            P(None, "head"),
            P(),
            P("seq", "head"),
            P("seq", "head"),
            P("seq", "head"),
            P(),
            P(),
            P("seq", "head"),
            P("head"),
        ),
        out_specs=P("seq", "head"),
        check_vma=False,
    )
```

profile of v0, /device:TPU:1, one launch (start us, length us, event | category | flops | bytes accessed | tf_op | source)
XLA Modules:
  0.0 813.5 jit_solution(580391868668039390)
XLA Ops:
  6.5 3.4 reshape.416
  9.9 2.3 reduce_sum.100
  16.1 138.9 %all-gather.11.cloned.1.call-done = bf16[2048,672]{1,0:T(8,128)(2,1)} async-done(((bf16[32,672]{1,0:T(8,128)(2,1)}), bf16[2048,672]{1,0:T(8,128)(2,1)}) %all-gather.11.cloned.1.call-update) | async-done | bytes 2752528 | tf_op jit(solution)/shard_map/all_gather | solution.py:107
  155.0 3.7 gather_fusion
  161.7 1.4 fusion.11
  163.1 128.6 %all-gather.21.cloned.1.call-done = bf16[64,84,128]{2,1,0:T(8,128)(2,1)} async-done(((bf16[1,84,128]{2,1,0:T(8,128)(2,1)}), bf16[64,84,128]{2,1,0:T(8,128)(2,1)}) %all-gather.21.cloned.1.call-update) | async-done | bytes 1376272 | tf_op jit(solution)/shard_map/all_gather | solution.py:124
  291.6 3.2 reshape.428
  294.9 135.7 %all-gather.19.cloned.1.call-done = bf16[64,84,128]{2,1,0:T(8,128)(2,1)} async-done(((bf16[1,84,128]{2,1,0:T(8,128)(2,1)}), bf16[64,84,128]{2,1,0:T(8,128)(2,1)}) %all-gather.19.cloned.1.call-update) | async-done | bytes 1376272 | tf_op jit(solution)/shard_map/all_gather | solution.py:125
  430.6 2.2 reshape.426
  432.8 140.1 %all-gather.23.cloned.1.call-done = bf16[64,84,256]{2,1,0:T(8,128)(2,1)} async-done(((bf16[1,84,256]{2,1,0:T(8,128)(2,1)}), bf16[64,84,256]{2,1,0:T(8,128)(2,1)}) %all-gather.23.cloned.1.call-update) | async-done | bytes 2752528 | tf_op jit(solution)/shard_map/all_gather | solution.py:123
  572.9 5.1 reshape.430
  578.0 34.9 %all-gather.13.cloned.1.call-done = bf16[256,5376]{0,1:T(8,128)(2,1)} async-done(((bf16[256,672]{0,1:T(8,128)(2,1)}), bf16[256,5376]{0,1:T(8,128)(2,1)}) %all-gather.13.cloned.1.call-update) | async-done | bytes 2752528 | tf_op jit(solution)/shard_map/all_gather | solution.py:117
  612.9 2.7 fusion
  615.6 3.0 multiply_reduce_fusion.3
  619.7 8.1 collective-permute-start.5
  627.8 5.8 collective-permute-start.6
  633.5 4.5 collective-permute-start.7
  638.0 2.3 collective-permute-start.8
  641.6 2.5 multiply_reduce_fusion.1
  644.1 1.8 copy.31
  647.0 3.6 convolution_convert_fusion
  650.8 4.2 collective-permute-start
  658.0 3.7 collective-permute-start.2
  662.6 4.2 collective-permute-start.3
  667.7 1.3 collective-permute-start.4
  669.1 1.8 collective-permute-done.3
  671.8 1.4 collective-permute-done.4
  674.3 1.3 fusion.18
  675.7 78.1 %all-gather.17.cloned.1.call-done = bf16[2048,672]{1,0:T(8,128)(2,1)} async-done(((bf16[32,672]{1,0:T(8,128)(2,1)}), bf16[2048,672]{1,0:T(8,128)(2,1)}) %all-gather.17.cloned.1.call-update) | async-done | bytes 2752528 | tf_op jit(solution)/shard_map/all_gather | solution.py:165
  753.8 36.4 %all-gather.15.cloned.1.call-done = bf16[256,2048]{0,1:T(8,128)(2,1)} async-done(((bf16[256,256]{0,1:T(8,128)(2,1)}), bf16[256,2048]{0,1:T(8,128)(2,1)}) %all-gather.15.cloned.1.call-update) | async-done | bytes 1048592 | tf_op jit(solution)/shard_map/all_gather | solution.py:162
  790.2 3.5 multiply_reduce_fusion
  793.7 12.0 %psum.7 = f32[256]{0:T(256)S(1)} all-reduce(f32[256]{0:T(256)S(1)} %get-tuple-element.21), channel_id=1, replica_groups=mesh['seq'=64,'head'=8] {'head'}, use_global_device_ids=true, to_apply=%region_11.12 | all-reduce | flops 256 | bytes 2048 | tf_op jit(solution)/shard_map/psum | solution.py:168
  (95 shorter events, 18.0 us)
Async XLA Ops:
  6.5 6.0 copy-start
  6.5 5.8 copy-start.6
  6.5 148.5 %all-gather.11.cloned.1.call-start = ((), (), s32[]{:S(2)}) async-start(), calls=%async_computation | async-start | bytes 3194880 | tf_op jit(solution)/shard_map/all_gather | solution.py:107
  9.9 5.9 copy-start.7
  9.9 5.9 copy-start.11
  12.5 146.4 %copy-start.5 = (bf16[256,672]{0,1:T(8,128)(2,1)S(1)}, bf16[256,672]{0,1:T(8,128)(2,1)}, u32[]{:S(2)}) copy-start(bf16[256,672]{0,1:T(8,128)(2,1)} %param.14) | copy-start | bytes 1032196
  13.7 277.9 %all-gather.21.cloned.1.call-start = ((), (), s32[]{:S(2)}) async-start(), calls=%async_computation.5 | async-start | bytes 1464320 | tf_op jit(solution)/shard_map/all_gather | solution.py:124
  14.5 416.1 %all-gather.19.cloned.1.call-start = ((), (), s32[]{:S(2)}) async-start(), calls=%async_computation.4 | async-start | bytes 1464320 | tf_op jit(solution)/shard_map/all_gather | solution.py:125
  15.2 557.7 %all-gather.23.cloned.1.call-start = ((), (), s32[]{:S(2)}) async-start(), calls=%async_computation.6 | async-start | bytes 2928640 | tf_op jit(solution)/shard_map/all_gather | solution.py:123
  15.8 597.1 %all-gather.13.cloned.1.call-start = ((), (), s32[]{:S(2)}) async-start(), calls=%async_computation.1 | async-start | bytes 3096576 | tf_op jit(solution)/shard_map/all_gather | solution.py:117
  159.7 594.1 %all-gather.17.cloned.1.call-start = ((), (), s32[]{:S(2)}) async-start(), calls=%async_computation.3 | async-start | bytes 3194880 | tf_op jit(solution)/shard_map/all_gather | solution.py:165
  160.2 629.9 %all-gather.15.cloned.1.call-start = ((), (), s32[]{:S(2)}) async-start(), calls=%async_computation.2 | async-start | bytes 1179648 | tf_op jit(solution)/shard_map/all_gather | solution.py:162
  572.9 42.7 %copy-start.12 = (f32[5376]{0:T(1024)S(1)}, f32[5376]{0:T(1024)}, u32[]{:S(2)}) copy-start(f32[5376]{0:T(1024)} %param.20) | copy-start | bytes 64516
  612.9 2.7 copy-start.2
  615.6 3.0 copy-start.9
  615.6 26.0 %copy-start.3 = (bf16[5376,256]{1,0:T(8,128)(2,1)S(1)}, bf16[5376,256]{1,0:T(8,128)(2,1)}, u32[]{:S(2)}) copy-start(bf16[5376,256]{1,0:T(8,128)(2,1)} %reshape.430) | copy-start | bytes 8257540
  619.6 26.2 %copy-start.10 = (f32[128]{0:T(128)S(1)}, f32[128]{0:T(128)}, u32[]{:S(2)}) copy-start(f32[128]{0:T(128)} %param.24) | copy-start | bytes 1540
  619.7 31.1 %collective-permute-start.5 = (bf16[256,128]{0,1:T(8,128)(2,1)}, bf16[256,128]{0,1:T(8,128)(2,1)}, u32[]{:S(2)}, u32[]{:S(2)}) collective-permute-start(bf16[256,128]{0,1:T(8,128)(2,1)} %pad_maximum_fusion), channel_id=1, source_target_pairs={{0,32},{8,40},{16,48},{24,56},{32,64},{40,72},{48,80},{56,88},{64,... | collective-permute-start | bytes 196616 | tf_op jit(solution)/shard_map/ppermute | solution.py:22
  627.8 28.1 %collective-permute-start.6 = (bf16[256,128]{0,1:T(8,128)(2,1)}, bf16[256,128]{0,1:T(8,128)(2,1)}, u32[]{:S(2)}, u32[]{:S(2)}) collective-permute-start(bf16[256,128]{0,1:T(8,128)(2,1)} %pad_maximum_fusion), channel_id=1, source_target_pairs={{0,24},{8,32},{16,40},{24,48},{32,56},{40,64},{48,72},{56,80},{64,... | collective-permute-start | bytes 196616 | tf_op jit(solution)/shard_map/ppermute | solution.py:22
  633.5 24.5 %collective-permute-start.7 = (bf16[256,128]{0,1:T(8,128)(2,1)}, bf16[256,128]{0,1:T(8,128)(2,1)}, u32[]{:S(2)}, u32[]{:S(2)}) collective-permute-start(bf16[256,128]{0,1:T(8,128)(2,1)} %pad_maximum_fusion), channel_id=1, source_target_pairs={{0,16},{8,24},{16,32},{24,40},{32,48},{40,56},{48,64},{56,72},{64,... | collective-permute-start | bytes 196616 | tf_op jit(solution)/shard_map/ppermute | solution.py:22
  638.0 24.6 %collective-permute-start.8 = (bf16[256,128]{0,1:T(8,128)(2,1)}, bf16[256,128]{0,1:T(8,128)(2,1)}, u32[]{:S(2)}, u32[]{:S(2)}) collective-permute-start(bf16[256,128]{0,1:T(8,128)(2,1)} %pad_maximum_fusion), channel_id=1, source_target_pairs={{0,8},{8,16},{16,24},{24,32},{32,40},{40,48},{48,56},{56,64},{64,7... | collective-permute-start | bytes 196616 | tf_op jit(solution)/shard_map/ppermute | solution.py:22
  640.3 30.6 %collective-permute-start.9 = (bf16[256,128]{0,1:T(8,128)(2,1)}, bf16[256,128]{0,1:T(8,128)(2,1)}, u32[]{:S(2)}, u32[]{:S(2)}) collective-permute-start(bf16[256,128]{0,1:T(8,128)(2,1)} %pad_maximum_fusion), channel_id=1, source_target_pairs={{8,0},{16,8},{24,16},{32,24},{40,32},{48,40},{56,48},{64,56},{72,6... | collective-permute-start | bytes 196616 | tf_op jit(solution)/shard_map/ppermute | solution.py:22
  647.0 3.6 copy-start.4
  650.8 16.9 %collective-permute-start = (bf16[256,128]{1,0:T(8,128)(2,1)S(1)}, bf16[256,128]{1,0:T(8,128)(2,1)S(1)}, u32[]{:S(2)}, u32[]{:S(2)}) collective-permute-start(bf16[256,128]{1,0:T(8,128)(2,1)S(1)} %convolution_convert_fusion), channel_id=1, source_target_pairs={{0,32},{8,40},{16,48},{24,56},{32,64},{40,72},{48,80},{56,88},{64,... | collective-permute-start | bytes 196616 | tf_op jit(solution)/shard_map/ppermute | solution.py:22
  655.9 13.1 %collective-permute-start.1 = (bf16[256,128]{1,0:T(8,128)(2,1)S(1)}, bf16[256,128]{1,0:T(8,128)(2,1)S(1)}, u32[]{:S(2)}, u32[]{:S(2)}) collective-permute-start(bf16[256,128]{1,0:T(8,128)(2,1)S(1)} %convolution_convert_fusion), channel_id=1, source_target_pairs={{0,24},{8,32},{16,40},{24,48},{32,56},{40,64},{48,72},{56,80},{64,... | collective-permute-start | bytes 196616 | tf_op jit(solution)/shard_map/ppermute | solution.py:22
  658.0 11.0 %collective-permute-start.2 = (bf16[256,128]{1,0:T(8,128)(2,1)S(1)}, bf16[256,128]{1,0:T(8,128)(2,1)S(1)}, u32[]{:S(2)}, u32[]{:S(2)}) collective-permute-start(bf16[256,128]{1,0:T(8,128)(2,1)S(1)} %convolution_convert_fusion), channel_id=1, source_target_pairs={{0,16},{8,24},{16,32},{24,40},{32,48},{40,56},{48,64},{56,72},{64,... | collective-permute-start | bytes 196616 | tf_op jit(solution)/shard_map/ppermute | solution.py:22
  662.6 8.3 %collective-permute-start.3 = (bf16[256,128]{1,0:T(8,128)(2,1)S(1)}, bf16[256,128]{1,0:T(8,128)(2,1)S(1)}, u32[]{:S(2)}, u32[]{:S(2)}) collective-permute-start(bf16[256,128]{1,0:T(8,128)(2,1)S(1)} %convolution_convert_fusion), channel_id=1, source_target_pairs={{0,8},{8,16},{16,24},{24,32},{32,40},{40,48},{48,56},{56,64},{64,7... | collective-permute-start | bytes 196616 | tf_op jit(solution)/shard_map/ppermute | solution.py:22
  667.7 5.4 collective-permute-start.4
  675.6 130.1 %copy-start.1 = (bf16[256,672]{0,1:T(8,128)(2,1)S(1)}, bf16[256,672]{0,1:T(8,128)(2,1)}, u32[]{:S(2)}) copy-start(bf16[256,672]{0,1:T(8,128)(2,1)} %select_select_fusion) | copy-start | bytes 1032196
  675.6 130.1 %copy-start.8 = (f32[672]{0:T(1024)S(1)}, f32[672]{0:T(1024)}, u32[]{:S(2)}) copy-start(f32[672]{0:T(1024)} %param.27) | copy-start | bytes 8068
Sparse Core Ops, SparseCore 0:
  13.8 141.1 all-gather.10
  157.9 133.6 all-gather.20
  294.6 135.9 all-gather.18
  433.4 139.4 all-gather.22
  574.8 38.0 all-gather.12
  615.7 138.0 all-gather.16
  755.9 34.2 all-gather.14
where the time goes:
time: 815 us; the launch traced here: 814 us
  waiting for transfers between devices  698 us (86%)
  starting transfers between devices  37 us (5%)
  local copies, waits for them, and re-layouts  24.1 us (3%)
  matrix products  15.8 us (2%)
  between operations  13.9 us (2%)
  other arithmetic  12.5 us (2%)
  blocking collectives  12 us (1%)
    all_gather x1, waiting for transfers between devices, body(): lax.all_gather(query_weight, 'seq', axis=0, tiled=True)  140 us
    all_gather x1, waiting for transfers between devices, body(): gathered = lax.all_gather(embedded, 'seq', axis=0, tiled=True)  139 us
    all_gather x1, waiting for transfers between devices, body(): lax.all_gather(value_weight, 'seq', axis=0, tiled=True)  136 us
    all_gather x1, waiting for transfers between devices, body(): key_sum = add_rows(lax.all_gather(key_weight, 'seq', axis=0, tiled=True))  129 us
    all_gather x1, waiting for transfers between devices, body(): lax.all_gather(out_weight, 'seq', axis=0, tiled=True)  78.1 us
    ppermute x10, starting transfers between devices, shifted(): lax.ppermute(value, axis, [(source, source + steps) for source in range(l...  36.7 us
    all_gather x1, waiting for transfers between devices, body(): heads_all = lax.all_gather(attended, 'head', axis=1, tiled=True)  36.4 us
    all_gather x1, waiting for transfers between devices, body(): whole_rows = lax.all_gather(residual, 'head', axis=1, tiled=True)  34.9 us
  transfers between devices with their start and end apart: 17, of which 9 were waited for; matrix products, arithmetic and copies ran while one was open for 5% of the time, Pallas kernels for 0%

commit v1 on v0

v1 whole, which is shorter than its diff:
```python
import jax
import jax.numpy as jnp
from jax import lax
from jax.sharding import Mesh
from jax.sharding import PartitionSpec as P

D = 5376
HEAD_DIM = 128
WINDOW = 1024
PATCH_SIDE = 64
POOL = 4
IMG_TOK = 256
SEQ = ("x", "z")
HEAD = ("y", "core")


EPSILON = 1e-06
QUERY_SCALE = 168.0 ** (-0.5)
ROPE_BASE = 10000.0


def shifted(value, axis, steps):
    count = lax.axis_size(axis)
    leading, last = (max(0, -steps), min(count, count - steps))
    return lax.ppermute(value, axis, [(source, source + steps) for source in range(leading, last)])


def rms_scale(inputs, scale_gain):
    return (
        inputs * lax.rsqrt(jnp.mean(inputs * inputs, axis=-1, keepdims=True) + EPSILON) * scale_gain
    )


def rotate(inputs, positions):
    half_dim = inputs.shape[-1] // 2
    frequency = ROPE_BASE ** (-jnp.arange(half_dim, dtype=jnp.float32) * 2.0 / inputs.shape[-1])
    angles = positions.astype(jnp.float32)[:, None] * frequency[None, :]
    cosine = jnp.cos(angles)[:, None, :]
    sine_part = jnp.sin(angles)[:, None, :]
    first_half = inputs[..., :half_dim]
    second = inputs[..., half_dim:]
    return jnp.concatenate(
        [first_half * cosine - second * sine_part, second * cosine + first_half * sine_part],
        axis=-1,
    )


def image_of(positions, starts):
    inside = (positions[:, None] >= starts[None, :]) & (
        positions[:, None] < starts[None, :] + IMG_TOK
    )
    labels = jnp.arange(1, starts.shape[0] + 1, dtype=jnp.int32)
    return jnp.sum(jnp.where(inside, labels[None, :], 0), axis=1) - 1


def allowed_keys(query_pos, key_pos, starts, total_rows):
    query_img = image_of(query_pos, starts)
    key_img = image_of(key_pos, starts)
    inside = (key_pos >= 0) & (key_pos < total_rows)
    in_window = query_pos[:, None] - key_pos[None, :] < WINDOW
    causal = key_pos[None, :] <= query_pos[:, None]
    same_image = (query_img[:, None] == key_img[None, :]) & (query_img[:, None] >= 0)
    return inside[None, :] & in_window & (causal | same_image)


def attend(queries, key_rows, values, allowed):
    scores = jnp.einsum("qgrd,kgd->grqk", queries, key_rows, preferred_element_type=jnp.float32)
    scores = jnp.where(allowed[None, None], scores, -jnp.inf)
    row_max = jnp.max(scores, axis=-1, keepdims=True)
    weights = jnp.exp(scores - row_max)
    row_sum = jnp.sum(weights, axis=-1)
    mixed_heads = jnp.einsum(
        "grqk,kgd->qgrd", weights.astype(jnp.bfloat16), values, preferred_element_type=jnp.float32
    )
    return (mixed_heads / jnp.transpose(row_sum, (2, 0, 1))[..., None]).astype(jnp.bfloat16)


def exchange(value, axes, count):
    spread = jnp.broadcast_to(value[None], (count, *value.shape))
    return lax.all_to_all(spread, axes, 0, 0, tiled=True)


def body(
    tokens,
    features,
    starts,
    sources,
    soft_gain,
    proj_weight,
    input_gain,
    query_weight,
    key_weight,
    value_weight,
    query_gain,
    key_gain,
    out_weight,
    post_gain,
):
    tok_rows, width = tokens.shape
    x_count = lax.axis_size("x")
    z_count = lax.axis_size("z")
    head_count = lax.axis_size("y") * lax.axis_size("core")
    seq_count = x_count * z_count
    x_index = lax.axis_index("x")
    z_index = lax.axis_index("z")
    head_index = lax.axis_index(HEAD)
    seq_index = lax.axis_index(SEQ)
    total_rows = seq_count * tok_rows
    rows_in = query_weight.shape[0]
    rows_out = out_weight.shape[0]

    qkv_local = jnp.concatenate([query_weight, key_weight, value_weight], axis=1)
    qkv_x = lax.all_gather(qkv_local, "x", axis=0, tiled=True)
    qkv_zx = lax.all_gather(qkv_x, "z", axis=0, tiled=True)
    out_x = lax.all_gather(out_weight, "x", axis=0, tiled=True)
    out_zx = lax.all_gather(out_x, "z", axis=0, tiled=True)

    image_count = starts.shape[0]
    vis = features.shape[2]
    pooled_side = PATCH_SIDE // POOL
    pool_rows = features.shape[0] // POOL
    block_rows = pool_rows * pooled_side
    shards_each = pooled_side // pool_rows
    patch_grid = features.reshape(pool_rows, POOL, pooled_side, POOL, vis)
    pooled = jnp.sum(patch_grid, axis=(1, 3), dtype=jnp.float32).reshape(block_rows, vis) / (
        POOL * POOL
    )
    soft = rms_scale(pooled, soft_gain).astype(jnp.bfloat16)
    vis_part = vis // head_count
    soft_part = lax.dynamic_slice_in_dim(soft, head_index * vis_part, vis_part, 1)
    soft_z = exchange(soft_part, "z", z_count).reshape(z_count * block_rows, vis_part)
    frame_pos = (
        (jnp.arange(x_count, dtype=jnp.int32)[:, None] * z_count + z_index) * tok_rows
        + jnp.arange(tok_rows, dtype=jnp.int32)[None, :]
    ).reshape(-1)
    frame_image = image_of(frame_pos, starts)
    row_base = sources // shards_each * (block_rows * shards_each) - starts
    image_ids = jnp.arange(image_count, dtype=jnp.int32)
    frame_row = jnp.sum(
        jnp.where(frame_image[:, None] == image_ids[None, :], row_base[None, :], 0), axis=1
    )
    frame_row = jnp.where(frame_image >= 0, frame_row + frame_pos, -1)
    here = x_index * (z_count * block_rows) + jnp.arange(z_count * block_rows, dtype=jnp.int32)
    chosen = (frame_row[:, None] == here[None, :]).astype(jnp.bfloat16)
    chosen = chosen.reshape(x_count, tok_rows, z_count * block_rows)
    frames = jnp.einsum("sk,xps->xkp", soft_z, chosen, preferred_element_type=jnp.float32)
    frames = lax.all_to_all(frames.astype(jnp.bfloat16), "x", 0, 0, tiled=True)
    mine = jnp.sum(frames.astype(jnp.float32), axis=0).astype(jnp.bfloat16)
    soft_rows = exchange(mine, HEAD, head_count).reshape(vis, tok_rows)
    embedded = lax.dot_general(
        soft_rows, proj_weight, (((0,), (0,)), ((), ())), preferred_element_type=jnp.float32
    ).astype(jnp.bfloat16)
    my_pos = seq_index * tok_rows + jnp.arange(tok_rows, dtype=jnp.int32)
    my_image = image_of(my_pos, starts)
    residual = jnp.where((my_image >= 0)[:, None], embedded, tokens)

    whole = exchange(residual, HEAD, head_count).astype(jnp.float32)
    mean_square = jnp.sum(whole * whole, axis=(0, 2), keepdims=True) / D
    gains = input_gain.reshape(head_count, 1, width)
    normed = (whole * lax.rsqrt(mean_square + EPSILON) * gains).astype(jnp.bfloat16)

    qkv_weight = (
        qkv_zx.reshape(z_count, x_count, rows_in, -1)
        .transpose(1, 0, 2, 3)
        .reshape(head_count, width, -1)
    )
    qkv = jnp.einsum("hqk,hkn->qn", normed, qkv_weight, preferred_element_type=jnp.float32)
    kv_local = key_weight.shape[1] // HEAD_DIM
    group_size = query_weight.shape[1] // key_weight.shape[1]
    q_width = query_weight.shape[1]
    k_width = key_weight.shape[1]
    query_sum = qkv[:, :q_width]
    key_sum = qkv[:, q_width : q_width + k_width]
    value_sum = qkv[:, q_width + k_width :]
    queries = (
        rotate(
            rms_scale(query_sum.reshape(tok_rows, kv_local * group_size, HEAD_DIM), query_gain),
            my_pos,
        )
        * QUERY_SCALE
    )
    queries = queries.astype(jnp.bfloat16).reshape(tok_rows, kv_local, group_size, HEAD_DIM)
    own_keys = (
        rotate(rms_scale(key_sum.reshape(tok_rows, kv_local, HEAD_DIM), key_gain), my_pos)
        .astype(jnp.bfloat16)
        .reshape(tok_rows, k_width)
    )
    own = jnp.concatenate([own_keys, value_sum.astype(jnp.bfloat16)], axis=1)
    past_count = WINDOW // tok_rows
    pieces = [shifted(own, SEQ, step) for step in range(past_count, 0, -1)]
    pieces += [own, shifted(own, SEQ, -1)]
    window = jnp.concatenate(pieces, axis=0)
    key_pos = (seq_index - past_count) * tok_rows + jnp.arange(window.shape[0], dtype=jnp.int32)
    allowed = allowed_keys(my_pos, key_pos, starts, total_rows)
    attended = attend(
        queries,
        window[:, :k_width].reshape(-1, kv_local, HEAD_DIM),
        window[:, k_width:].reshape(-1, kv_local, HEAD_DIM),
        allowed,
    )
    attended = attended.reshape(tok_rows, kv_local * group_size * HEAD_DIM)
    heads_all = exchange(attended, HEAD, head_count)
    heads_weight = (
        out_zx.reshape(z_count, x_count, rows_out, width)
        .transpose(1, 0, 2, 3)
        .reshape(head_count, q_width, width)
    )
    projected = jnp.einsum(
        "hqk,hkn->qn", heads_all, heads_weight, preferred_element_type=jnp.float32
    )
    squares = jnp.sum(exchange(jnp.sum(projected * projected, axis=1), HEAD, head_count), axis=0)
    post = projected * lax.rsqrt(squares[:, None] / D + EPSILON) * post_gain
    return (residual.astype(jnp.float32) + post).astype(jnp.bfloat16)


def solution(mesh):
    split = Mesh(mesh.devices.reshape(4, 16, 4, 2), ("x", "z", "y", "core"))
    return jax.shard_map(
        body,
        mesh=split,
        in_specs=(
            P(SEQ, HEAD),
            P(SEQ, None, None),
            P(),
            P(),
            P(),
            P(None, HEAD),
            P(),
            P(SEQ, HEAD),
            P(SEQ, HEAD),
            P(SEQ, HEAD),
            P(),
            P(),
            P(SEQ, HEAD),
            P(HEAD),
        ),
        out_specs=P(SEQ, HEAD),
        check_vma=False,
    )
```

time: 815 us -> 255 us (0.31)
  waiting for transfers between devices: 698 us -> 75.7 us
  blocking collectives: 12 us -> 37.5 us
  starting transfers between devices: 37 us -> 57.6 us
  local copies, waits for them, and re-layouts: 24.1 us -> 41.8 us
    all_gather x7 -> x2, waiting for transfers between devices: 693 us -> 0.02 us  [the longest x1 0.01 us: body(): qkv_zx = lax.all_gather(qkv_x, 'z', axis=0, tiled=True)]
    all_to_all x0 -> x4, waiting for transfers between devices: none -> 55.7 us  [exchange(): return lax.all_to_all(spread, axes, 0, 0, tiled=True)]
    all_to_all x0 -> x4, starting transfers between devices: none -> 40.4 us  [exchange(): return lax.all_to_all(spread, axes, 0, 0, tiled=True)]
    reshape x0 -> x3, local copies, waits for them, and re-layouts: none -> 21.6 us  [the longest x1 8.92 us: body(): qkv_zx.reshape(z_count, x_count, rows_in, -1).transpose(1, 0, 2, 3)]
    all_gather x0 -> x2, blocking collectives: none -> 21.6 us  [the longest x1 10.9 us: body(): out_x = lax.all_gather(out_weight, 'x', axis=0, tiled=True)]
    ppermute x10 -> x5, starting transfers between devices: 36.7 us -> 17.2 us  [shifted(): lax.ppermute(value, axis, [(source, source + steps) for source in range(l...]
    ppermute x10 -> x5, waiting for transfers between devices: 3.21 us -> 20 us  [shifted(): lax.ppermute(value, axis, [(source, source + steps) for source in range(l...]
    all_to_all x0 -> x2, blocking collectives: none -> 15.9 us  [the longest x1 8.11 us: body(): frames = lax.all_to_all(frames.astype(jnp.bfloat16), 'x', 0, 0, tiled=True)]
  transfers between devices with their start and end apart: 17 -> 11, of which waited for: 9 -> 7; matrix products, arithmetic and copies ran while one was open for 5% -> 24% of each run, Pallas kernels for 0% -> 0%
where the time goes in v1:
time: 255 us; the launch traced here: 252 us
  waiting for transfers between devices  75.7 us (30%)
  starting transfers between devices  57.6 us (23%)
  local copies, waits for them, and re-layouts  41.8 us (16%)
  blocking collectives  37.5 us (15%)
  between operations  13.8 us (5%)
  matrix products  13.3 us (5%)
  other arithmetic  12.5 us (5%)
    all_to_all x4, waiting for transfers between devices, exchange(): return lax.all_to_all(spread, axes, 0, 0, tiled=True)  55.7 us
    all_to_all x4, starting transfers between devices, exchange(): return lax.all_to_all(spread, axes, 0, 0, tiled=True)  40.4 us
    ppermute x5, waiting for transfers between devices, shifted(): lax.ppermute(value, axis, [(source, source + steps) for source in range(l...  20 us
    ppermute x5, starting transfers between devices, shifted(): lax.ppermute(value, axis, [(source, source + steps) for source in range(l...  17.2 us
    all_gather x1, blocking collectives, body(): out_x = lax.all_gather(out_weight, 'x', axis=0, tiled=True)  10.9 us
    all_gather x1, blocking collectives, body(): qkv_x = lax.all_gather(qkv_local, 'x', axis=0, tiled=True)  10.7 us
    reshape x1, local copies, waits for them, and re-layouts, body(): qkv_zx.reshape(z_count, x_count, rows_in, -1).transpose(1, 0, 2, 3)  8.92 us
    reshape x1, local copies, waits for them, and re-layouts, body(): qkv_weight = qkv_zx.reshape(z_count, x_count, rows_in, -1).transpose(1, 0...  8.9 us
  transfers between devices with their start and end apart: 11, of which 7 were waited for; matrix products, arithmetic and copies ran while one was open for 24% of the time, Pallas kernels for 0%

profile of v1, /device:TPU:1, one launch (start us, length us, event | category | flops | bytes accessed | tf_op | source)
XLA Modules:
  0.0 252.3 jit_solution(5185182241604811078)
XLA Ops:
  7.5 10.7 %all-gather = bf16[4,84,512]{2,1,0:T(8,128)(2,1)S(1)} all-gather(bf16[1,84,512]{2,1,0:T(8,128)(2,1)S(1)} %maximum_bitcast_fusion), channel_id=1, replica_groups=mesh['x'=4,'z'=16,'y'=4,'core'=2] {'x'}, dimensions={0}, use_global_device_ids=true | all-gather | bytes 430080 | tf_op jit(solution)/shard_map/all_gather | solution.py:113
  19.1 3.3 %reshape.472 = f32[2,4,16,4,1152]{4,3,2,1,0:T(4,128)} reshape(bf16[8,64,1152]{2,1,0:T(8,128)(2,1)} %param.15) | data formatting | bytes 3538944 | tf_op jit(solution)/shard_map/convert_element_type | solution.py:125
  22.4 2.2 reduce_sum.132
  26.4 15.7 %all-to-all-start = ((bf16[16,32,144]{2,1,0:T(8,128)(2,1)}), bf16[16,32,144]{2,1,0:T(8,128)(2,1)S(1)}, u32[]{:S(2)}, u32[]{:S(2)}) async-start(bf16[16,32,144]{2,1,0:T(8,128)(2,1)} %broadcast_in_dim.78), calls=%async_computation | async-start | bytes 524288 | tf_op jit(solution)/shard_map/all_to_all | solution.py:80
  42.5 14.0 %all-to-all-done = bf16[16,32,144]{2,1,0:T(8,128)(2,1)S(1)} async-done(((bf16[16,32,144]{2,1,0:T(8,128)(2,1)}), bf16[16,32,144]{2,1,0:T(8,128)(2,1)S(1)}, u32[]{:S(2)}, u32[]{:S(2)}) %all-to-all-start) | async-done | bytes 147488 | tf_op jit(solution)/shard_map/all_to_all | solution.py:80
  57.1 8.1 %all_to_all.31 = bf16[4,144,256]{2,1,0:T(8,128)(2,1)S(1)} all-to-all(bf16[4,144,256]{2,1,0:T(8,128)(2,1)S(1)} %fusion.25), channel_id=1, replica_groups=mesh['x'=4,'z'=16,'y'=4,'core'=2] {'x'}, dimensions={0} | all-to-all | bytes 589824 | tf_op jit(solution)/shard_map/all_to_all | solution.py:147
  66.2 14.8 %all-to-all-start.2 = ((bf16[8,144,256]{2,1,0:T(8,128)(2,1)}), bf16[8,144,256]{2,1,0:T(8,128)(2,1)S(1)}, u32[]{:S(2)}, u32[]{:S(2)}) async-start(bf16[8,144,256]{2,1,0:T(8,128)(2,1)} %broadcast_in_dim.79), calls=%async_computation.2 | async-start | bytes 1179648 | tf_op jit(solution)/shard_map/all_to_all | solution.py:80
  81.0 10.1 %all-to-all-done.2 = bf16[8,144,256]{2,1,0:T(8,128)(2,1)S(1)} async-done(((bf16[8,144,256]{2,1,0:T(8,128)(2,1)}), bf16[8,144,256]{2,1,0:T(8,128)(2,1)S(1)}, u32[]{:S(2)}, u32[]{:S(2)}) %all-to-all-start.2) | async-done | bytes 589856 | tf_op jit(solution)/shard_map/all_to_all | solution.py:80
  91.7 1.7 broadcast_in_dim.80
  93.5 5.3 %all-to-all-start.3 = ((bf16[8,256,672]{1,2,0:T(8,128)(2,1)}), bf16[8,256,672]{1,2,0:T(8,128)(2,1)}, u32[]{:S(2)}, u32[]{:S(2)}) async-start(bf16[8,256,672]{1,2,0:T(8,128)(2,1)} %broadcast_in_dim.80), calls=%async_computation.3 | async-start | bytes 5505024 | tf_op jit(solution)/shard_map/all_to_all | solution.py:80
  98.8 10.9 %all_gather.14 = bf16[128,672]{1,0:T(8,128)(2,1)} all-gather(bf16[32,672]{1,0:T(8,128)(2,1)S(1)} %copy-done.1), channel_id=1, replica_groups=mesh['x'=4,'z'=16,'y'=4,'core'=2] {'x'}, dimensions={0}, use_global_device_ids=true | all-gather | bytes 215040 | tf_op jit(solution)/shard_map/all_gather | solution.py:115
  110.5 1.4 fusion.17
  111.9 20.3 %all-to-all-done.3 = bf16[8,256,672]{1,2,0:T(8,128)(2,1)} async-done(((bf16[8,256,672]{1,2,0:T(8,128)(2,1)}), bf16[8,256,672]{1,2,0:T(8,128)(2,1)}, u32[]{:S(2)}, u32[]{:S(2)}) %all-to-all-start.3) | async-done | bytes 2752544 | tf_op jit(solution)/shard_map/all_to_all | solution.py:80
  132.3 2.5 fusion
  134.8 8.9 %reshape.466 = bf16[16,4,84,512]{3,2,1,0:T(8,128)(2,1)} reshape(bf16[5376,512]{1,0:T(8,128)(2,1)} %all-gather.4.cloned.1.call-done) | data formatting | bytes 11010048 | tf_op jit(solution)/shard_map/reshape | solution.py:163
  143.8 5.8 %copy.56 = bf16[4,16,84,512]{3,2,1,0:T(8,128)(2,1)} copy(bf16[4,16,84,512]{3,2,0,1:T(8,128)(2,1)} %bitcast.76) | data formatting | bytes 11010048 | tf_op jit(solution)/shard_map/transpose | solution.py:164
  149.5 8.9 %reshape.467 = bf16[8,672,512]{2,1,0:T(8,128)(2,1)} reshape(bf16[4,16,84,512]{3,2,1,0:T(8,128)(2,1)} %copy.56) | data formatting | bytes 11010048 | tf_op jit(solution)/shard_map/reshape | solution.py:165
  158.4 6.6 %fusion.18 = f32[256,512]{1,0:T(8,128)S(1)} fusion(bf16[8,672,512]{2,1,0:T(8,128)(2,1)} %reshape.467, bf16[8,256,672]{1,2,0:T(8,128)(2,1)} %all-to-all-done.3, f32[8,672]{1,0:T(8,128)S(1)} %mul.255, f32[256]{0:T(256)S(1)} %add_rsqrt_fusion.3), kind=kOutput, calls=%fused_computation.22 | convolution fusion | flops 1414791168 | bytes 8804352 | tf_op jit(solution)/shard_map/hqk,hkn->qn/dot_general | solution.py:167
  166.0 5.2 %collective-permute-start = (bf16[256,256]{1,0:T(8,128)(2,1)S(1)}, bf16[256,256]{1,0:T(8,128)(2,1)}, u32[]{:S(2)}, u32[]{:S(2)}) collective-permute-start(bf16[256,256]{1,0:T(8,128)(2,1)S(1)} %pad_maximum_fusion), channel_id=1, source_target_pairs={{0,32},{8,40},{16,48},{24,56},{32,64},{40,72},{48,80},{56,88},{64,... | collective-permute-start | bytes 393224 | tf_op jit(solution)/shard_map/ppermute | solution.py:25
  171.2 3.8 %collective-permute-start.1 = (bf16[256,256]{1,0:T(8,128)(2,1)S(1)}, bf16[256,256]{1,0:T(8,128)(2,1)}, u32[]{:S(2)}, u32[]{:S(2)}) collective-permute-start(bf16[256,256]{1,0:T(8,128)(2,1)S(1)} %pad_maximum_fusion), channel_id=1, source_target_pairs={{0,24},{8,32},{16,40},{24,48},{32,56},{40,64},{48,72},{56,80},{64,... | collective-permute-start | bytes 393224 | tf_op jit(solution)/shard_map/ppermute | solution.py:25
  175.0 2.9 %collective-permute-start.2 = (bf16[256,256]{1,0:T(8,128)(2,1)S(1)}, bf16[256,256]{1,0:T(8,128)(2,1)}, u32[]{:S(2)}, u32[]{:S(2)}) collective-permute-start(bf16[256,256]{1,0:T(8,128)(2,1)S(1)} %pad_maximum_fusion), channel_id=1, source_target_pairs={{0,16},{8,24},{16,32},{24,40},{32,48},{40,56},{48,64},{56,72},{64,... | collective-permute-start | bytes 393224 | tf_op jit(solution)/shard_map/ppermute | solution.py:25
  177.9 3.8 %collective-permute-start.3 = (bf16[256,256]{1,0:T(8,128)(2,1)S(1)}, bf16[256,256]{1,0:T(8,128)(2,1)}, u32[]{:S(2)}, u32[]{:S(2)}) collective-permute-start(bf16[256,256]{1,0:T(8,128)(2,1)S(1)} %pad_maximum_fusion), channel_id=1, source_target_pairs={{0,8},{8,16},{16,24},{24,32},{32,40},{40,48},{48,56},{56,64},{64,7... | collective-permute-start | bytes 393224 | tf_op jit(solution)/shard_map/ppermute | solution.py:25
  181.7 1.5 collective-permute-start.4
  185.1 6.4 %collective-permute-done.1 = bf16[256,256]{1,0:T(8,128)(2,1)} collective-permute-done((bf16[256,256]{1,0:T(8,128)(2,1)S(1)}, bf16[256,256]{1,0:T(8,128)(2,1)}, u32[]{:S(2)}, u32[]{:S(2)}) %collective-permute-start.1) | collective-permute-done | bytes 131104 | tf_op jit(solution)/shard_map/ppermute | solution.py:25
  192.4 9.1 %collective-permute-done.2 = bf16[256,256]{1,0:T(8,128)(2,1)} collective-permute-done((bf16[256,256]{1,0:T(8,128)(2,1)S(1)}, bf16[256,256]{1,0:T(8,128)(2,1)}, u32[]{:S(2)}, u32[]{:S(2)}) %collective-permute-start.2) | collective-permute-done | bytes 131104 | tf_op jit(solution)/shard_map/ppermute | solution.py:25
  202.4 4.5 %collective-permute-done.3 = bf16[256,256]{1,0:T(8,128)(2,1)} collective-permute-done((bf16[256,256]{1,0:T(8,128)(2,1)S(1)}, bf16[256,256]{1,0:T(8,128)(2,1)}, u32[]{:S(2)}, u32[]{:S(2)}) %collective-permute-start.3) | collective-permute-done | bytes 131104 | tf_op jit(solution)/shard_map/ppermute | solution.py:25
  211.7 4.7 %all-to-all-start.4 = ((bf16[8,256,256]{2,1,0:T(8,128)(2,1)}), bf16[8,256,256]{2,1,0:T(8,128)(2,1)S(1)}, u32[]{:S(2)}, u32[]{:S(2)}) async-start(bf16[8,256,256]{2,1,0:T(8,128)(2,1)} %broadcast_in_dim.90), calls=%async_computation.4 | async-start | bytes 2097152 | tf_op jit(solution)/shard_map/all_to_all | solution.py:80
  216.3 3.8 %copy.62 = bf16[16,4,32,672]{3,2,0,1:T(8,128)(2,1)} copy(bf16[16,4,32,672]{3,2,1,0:T(8,128)(2,1)} %bitcast.77) | data formatting | bytes 5505024 | tf_op jit(solution)/shard_map/reshape | solution.py:204
  220.2 11.3 %all-to-all-done.4 = bf16[8,256,256]{2,1,0:T(8,128)(2,1)S(1)} async-done(((bf16[8,256,256]{2,1,0:T(8,128)(2,1)}), bf16[8,256,256]{2,1,0:T(8,128)(2,1)S(1)}, u32[]{:S(2)}, u32[]{:S(2)}) %all-to-all-start.4) | async-done | bytes 1048608 | tf_op jit(solution)/shard_map/all_to_all | solution.py:80
  231.5 4.1 %multiply_reduce_fusion = (f32[256]{0:T(256)S(1)}, f32[256,672]{0,1:T(8,128)}) fusion(bf16[8,256,256]{2,1,0:T(8,128)(2,1)S(1)} %all-to-all-done.4, bf16[8,256,672]{2,1,0:T(8,128)(2,1)} %bitcast.78), kind=kOutput, calls=%fused_computation.33 | convolution fusion | flops 704986880 | bytes 4490240 | tf_op jit(solution)/shard_map/hqk,hkn->qn/dot_general | solution.py:208
  235.5 7.8 %all_to_all.32 = f32[8,1,256]{2,1,0:T(1,128)S(1)} all-to-all(f32[8,1,256]{2,1,0:T(1,128)S(1)} %broadcast_in_dim.91), channel_id=1, replica_groups=mesh['x'=4,'z'=16,'y'=4,'core'=2] {'y','core'}, dimensions={0} | all-to-all | bytes 16384 | tf_op jit(solution)/shard_map/all_to_all | solution.py:80
  243.4 2.0 add_convert_fusion
  (90 shorter events, 16.4 us)
Async XLA Ops:
  6.5 84.6 %copy-start = (bf16[1152,672]{0,1:T(8,128)(2,1)S(1)}, bf16[1152,672]{0,1:T(8,128)(2,1)}, u32[]{:S(2)}) copy-start(bf16[1152,672]{0,1:T(8,128)(2,1)} %param.19) | copy-start | bytes 4644868
  6.5 128.3 %all-gather.4.cloned.1.call-start = ((), (), s32[]{:S(2)}) async-start(), calls=%async_computation.6 | async-start | bytes 5849088 | tf_op jit(solution)/shard_map/all_gather | solution.py:114
  19.1 23.1 %copy-start.3 = (s32[8]{0:T(128)S(1)}, s32[8]{0:T(128)}, u32[]{:S(2)}) copy-start(s32[8]{0:T(128)} %param.16) | copy-start | bytes 100
  19.1 23.1 %copy-start.7 = (s32[8]{0:T(128)S(1)}, s32[8]{0:T(128)}, u32[]{:S(2)}) copy-start(s32[8]{0:T(128)} %param.17) | copy-start | bytes 100
  24.6 66.5 %copy-start.8 = (bf16[256,672]{0,1:T(8,128)(2,1)S(1)}, bf16[256,672]{0,1:T(8,128)(2,1)}, u32[]{:S(2)}) copy-start(bf16[256,672]{0,1:T(8,128)(2,1)} %param.14) | copy-start | bytes 1032196
  26.4 30.1 %all-to-all-start = ((bf16[16,32,144]{2,1,0:T(8,128)(2,1)}), bf16[16,32,144]{2,1,0:T(8,128)(2,1)S(1)}, u32[]{:S(2)}, u32[]{:S(2)}) async-start(bf16[16,32,144]{2,1,0:T(8,128)(2,1)} %broadcast_in_dim.78), calls=%async_computation | async-start | bytes 524288 | tf_op jit(solution)/shard_map/all_to_all | solution.py:80
  66.2 25.0 %all-to-all-start.2 = ((bf16[8,144,256]{2,1,0:T(8,128)(2,1)}), bf16[8,144,256]{2,1,0:T(8,128)(2,1)S(1)}, u32[]{:S(2)}, u32[]{:S(2)}) async-start(bf16[8,144,256]{2,1,0:T(8,128)(2,1)} %broadcast_in_dim.79), calls=%async_computation.2 | async-start | bytes 1179648 | tf_op jit(solution)/shard_map/all_to_all | solution.py:80
  93.5 5.3 %copy-start.1 = (bf16[32,672]{1,0:T(8,128)(2,1)S(1)}, bf16[32,672]{1,0:T(8,128)(2,1)}, u32[]{:S(2)}) copy-start(bf16[32,672]{1,0:T(8,128)(2,1)} %param.26) | copy-start | bytes 129028
  93.5 16.2 %copy-start.2 = (f32[5376]{0:T(1024)S(1)}, f32[5376]{0:T(1024)}, u32[]{:S(2)}) copy-start(f32[5376]{0:T(1024)} %param.20) | copy-start | bytes 64516
  93.5 38.8 %all-to-all-start.3 = ((bf16[8,256,672]{1,2,0:T(8,128)(2,1)}), bf16[8,256,672]{1,2,0:T(8,128)(2,1)}, u32[]{:S(2)}, u32[]{:S(2)}) async-start(bf16[8,256,672]{1,2,0:T(8,128)(2,1)} %broadcast_in_dim.80), calls=%async_computation.3 | async-start | bytes 5505024 | tf_op jit(solution)/shard_map/all_to_all | solution.py:80
  98.8 117.5 %all-gather.6.cloned.1.call-start = ((), (), s32[]{:S(2)}) async-start(), calls=%async_computation.7 | async-start | bytes 3342336 | tf_op jit(solution)/shard_map/all_gather | solution.py:116
  158.4 6.8 %copy-start.5 = (f32[128]{0:T(128)S(1)}, f32[128]{0:T(128)}, u32[]{:S(2)}) copy-start(f32[128]{0:T(128)} %param.25) | copy-start | bytes 1540
  158.4 25.4 %copy-start.6 = (f32[128]{0:T(128)S(1)}, f32[128]{0:T(128)}, u32[]{:S(2)}) copy-start(f32[128]{0:T(128)} %param.24) | copy-start | bytes 1540
  166.0 18.1 %collective-permute-start = (bf16[256,256]{1,0:T(8,128)(2,1)S(1)}, bf16[256,256]{1,0:T(8,128)(2,1)}, u32[]{:S(2)}, u32[]{:S(2)}) collective-permute-start(bf16[256,256]{1,0:T(8,128)(2,1)S(1)} %pad_maximum_fusion), channel_id=1, source_target_pairs={{0,32},{8,40},{16,48},{24,56},{32,64},{40,72},{48,80},{56,88},{64,... | collective-permute-start | bytes 393224 | tf_op jit(solution)/shard_map/ppermute | solution.py:25
  171.2 20.3 %collective-permute-start.1 = (bf16[256,256]{1,0:T(8,128)(2,1)S(1)}, bf16[256,256]{1,0:T(8,128)(2,1)}, u32[]{:S(2)}, u32[]{:S(2)}) collective-permute-start(bf16[256,256]{1,0:T(8,128)(2,1)S(1)} %pad_maximum_fusion), channel_id=1, source_target_pairs={{0,24},{8,32},{16,40},{24,48},{32,56},{40,64},{48,72},{56,80},{64,... | collective-permute-start | bytes 393224 | tf_op jit(solution)/shard_map/ppermute | solution.py:25
  175.0 26.4 %collective-permute-start.2 = (bf16[256,256]{1,0:T(8,128)(2,1)S(1)}, bf16[256,256]{1,0:T(8,128)(2,1)}, u32[]{:S(2)}, u32[]{:S(2)}) collective-permute-start(bf16[256,256]{1,0:T(8,128)(2,1)S(1)} %pad_maximum_fusion), channel_id=1, source_target_pairs={{0,16},{8,24},{16,32},{24,40},{32,48},{40,56},{48,64},{56,72},{64,... | collective-permute-start | bytes 393224 | tf_op jit(solution)/shard_map/ppermute | solution.py:25
  177.9 28.9 %collective-permute-start.3 = (bf16[256,256]{1,0:T(8,128)(2,1)S(1)}, bf16[256,256]{1,0:T(8,128)(2,1)}, u32[]{:S(2)}, u32[]{:S(2)}) collective-permute-start(bf16[256,256]{1,0:T(8,128)(2,1)S(1)} %pad_maximum_fusion), channel_id=1, source_target_pairs={{0,8},{8,16},{16,24},{24,32},{32,40},{40,48},{48,56},{56,64},{64,7... | collective-permute-start | bytes 393224 | tf_op jit(solution)/shard_map/ppermute | solution.py:25
  181.7 26.1 %collective-permute-start.4 = (bf16[256,256]{1,0:T(8,128)(2,1)S(1)}, bf16[256,256]{1,0:T(8,128)(2,1)}, u32[]{:S(2)}, u32[]{:S(2)}) collective-permute-start(bf16[256,256]{1,0:T(8,128)(2,1)S(1)} %pad_maximum_fusion), channel_id=1, source_target_pairs={{8,0},{16,8},{24,16},{32,24},{40,32},{48,40},{56,48},{64,56},{72,6... | collective-permute-start | bytes 393224 | tf_op jit(solution)/shard_map/ppermute | solution.py:25
  211.7 19.8 %all-to-all-start.4 = ((bf16[8,256,256]{2,1,0:T(8,128)(2,1)}), bf16[8,256,256]{2,1,0:T(8,128)(2,1)S(1)}, u32[]{:S(2)}, u32[]{:S(2)}) async-start(bf16[8,256,256]{2,1,0:T(8,128)(2,1)} %broadcast_in_dim.90), calls=%async_computation.4 | async-start | bytes 2097152 | tf_op jit(solution)/shard_map/all_to_all | solution.py:80
  220.2 23.2 %copy-start.4 = (f32[672]{0:T(1024)S(1)}, f32[672]{0:T(1024)}, u32[]{:S(2)}) copy-start(f32[672]{0:T(1024)} %param.27) | copy-start | bytes 8068
Sparse Core Ops, SparseCore 0:
  19.2 94.4 all-gather.3
  115.8 85.9 all-gather.5

commit v2 on v1

v2 whole, which is shorter than its diff:
```python
import jax
import jax.numpy as jnp
from jax import lax
from jax.experimental import pallas as pl
from jax.experimental.pallas import tpu as pltpu
from jax.sharding import Mesh
from jax.sharding import PartitionSpec as P

D = 5376
HEAD_DIM = 128
WINDOW = 1024
PATCH_SIDE = 64
POOL = 4
IMG_TOK = 256
Z = 16
ROWS_IN = 84
ROWS_OUT = 32
PAD_IN = 96
PAD_ALL = 144
WIDTH = 672

EPSILON = 1e-06
QUERY_SCALE = 168.0 ** (-0.5)
ROPE_BASE = 10000.0

GIVEN_SEQ = ("k", "a", "z")
GIVEN_HEAD = ("y", "core")
SEQ = ("k", "core", "z")
HEAD = ("y", "a")


def swapped(value):
    return lax.ppermute(value, ("a", "core"), [(0, 0), (1, 2), (2, 1), (3, 3)])


def from_half(value, flip):
    pairs = []
    for k in range(2):
        for a in range(2):
            for core in range(2):
                pairs.append(((k * 2 + a) * 2 + core, ((k ^ flip) * 2 + core) * 2 + a))
    return lax.ppermute(value, ("k", "a", "core"), pairs)


def shifted(value, steps):
    pairs = []
    for source in range(4 * Z):
        target = source + steps
        if 0 <= target < 4 * Z:
            place = [
                ((shard // (2 * Z)) * Z + shard % Z) * 2 + shard // Z % 2
                for shard in (source, target)
            ]
            pairs.append((place[0], place[1]))
    return lax.ppermute(value, ("k", "z", "core"), pairs)


def exchange(value, axes, count):
    spread = jnp.broadcast_to(value[None], (count, *value.shape))
    return lax.all_to_all(spread, axes, 0, 0, tiled=True)


def rms_scale(inputs, scale_gain):
    return (
        inputs * lax.rsqrt(jnp.mean(inputs * inputs, axis=-1, keepdims=True) + EPSILON) * scale_gain
    )


def image_of(positions, starts):
    inside = (positions[:, None] >= starts[None, :]) & (
        positions[:, None] < starts[None, :] + IMG_TOK
    )
    labels = jnp.arange(1, starts.shape[0] + 1, dtype=jnp.int32)
    return jnp.sum(jnp.where(inside, labels[None, :], 0), axis=1) - 1


def allowed_keys(query_pos, key_pos, starts, total_rows):
    query_img = image_of(query_pos, starts)
    key_img = image_of(key_pos, starts)
    inside = (key_pos >= 0) & (key_pos < total_rows)
    in_window = query_pos[:, None] - key_pos[None, :] < WINDOW
    causal = key_pos[None, :] <= query_pos[:, None]
    same_image = (query_img[:, None] == key_img[None, :]) & (query_img[:, None] >= 0)
    return inside[None, :] & in_window & (causal | same_image)


def attend(queries, key_rows, values, allowed):
    scores = jnp.einsum("qgrd,kgd->grqk", queries, key_rows, preferred_element_type=jnp.float32)
    scores = jnp.where(allowed[None, None], scores, -jnp.inf)
    row_max = jnp.max(scores, axis=-1, keepdims=True)
    weights = jnp.exp(scores - row_max)
    row_sum = jnp.sum(weights, axis=-1)
    mixed_heads = jnp.einsum(
        "grqk,kgd->qgrd", weights.astype(jnp.bfloat16), values, preferred_element_type=jnp.float32
    )
    return (mixed_heads / jnp.transpose(row_sum, (2, 0, 1))[..., None]).astype(jnp.bfloat16)


def add_part(whole_ref, gain_ref, weight_ref, block, start, squares):
    for shard in range(8):
        block[shard * ROWS_IN : (shard + 1) * ROWS_IN, :] = weight_ref[shard, 0, :ROWS_IN, :]
    part = whole_ref[0].astype(jnp.float32)
    scaled = (part * gain_ref[0]).astype(jnp.bfloat16)
    product = lax.dot_general(
        scaled, block[...], (((0,), (0,)), ((), ())), preferred_element_type=jnp.float32
    )
    return start + product, squares + jnp.sum(part * part, axis=0, keepdims=True)


def first_kernel(core_ref, whole_ref, gain_ref, weight_ref, total_ref, squares_ref, block):
    @pl.when(pl.program_id(0) == 0)
    def _():
        total_ref[...] = jnp.zeros_like(total_ref)
        squares_ref[...] = jnp.zeros_like(squares_ref)

    total_ref[...], squares_ref[...] = add_part(
        whole_ref, gain_ref, weight_ref, block, total_ref[...], squares_ref[...]
    )


def second_kernel(
    core_ref, whole_ref, gain_ref, weight_ref, start_ref, square_ref, cos_ref, sin_ref,
    query_gain_ref, key_gain_ref, query_ref, pair_ref, block, total, squares,
):
    step = pl.program_id(0)

    @pl.when(step == 0)
    def _():
        total[...] = start_ref[...]
        squares[...] = square_ref[...]

    total[...], squares[...] = add_part(
        whole_ref, gain_ref, weight_ref, block, total[...], squares[...]
    )

    @pl.when(step == pl.num_programs(0) - 1)
    def _():
        inverse = lax.rsqrt(squares[...] / D + EPSILON)
        inverse = jnp.transpose(jnp.broadcast_to(inverse, (HEAD_DIM, inverse.shape[1])))

        def head(index):
            return total[:, index * HEAD_DIM : (index + 1) * HEAD_DIM] * inverse

        def turned(rows, gain):
            mean_square = jnp.mean(rows * rows, axis=-1, keepdims=True)
            rows = rows * lax.rsqrt(mean_square + EPSILON) * gain
            return rows * cos_ref[...] + pltpu.roll(rows, HEAD_DIM // 2, 1) * sin_ref[...]

        for index in range(2):
            query_ref[:, index * HEAD_DIM : (index + 1) * HEAD_DIM] = (
                turned(head(index), query_gain_ref[...]) * QUERY_SCALE
            ).astype(jnp.bfloat16)
        pair_ref[:, :HEAD_DIM] = turned(head(2), key_gain_ref[...]).astype(jnp.bfloat16)
        pair_ref[:, HEAD_DIM:] = head(3).astype(jnp.bfloat16)


def own_block(step, core):
    return step // 2 * 4 + core[0] * 2 + step % 2


def other_block(step, core):
    return step // 2 * 4 + (1 - core[0]) * 2 + step % 2


def qkv_specs(block_of, width, rows):
    return [
        pl.BlockSpec((1, width, rows), lambda step, core: (block_of(step, core), 0, 0)),
        pl.BlockSpec((1, width, 1), lambda step, core: (block_of(step, core), 0, 0)),
        pl.BlockSpec((8, 1, PAD_IN, 512), lambda step, core: (step % 2, step // 2, 0, 0)),
    ]


def project_first(core, whole, gain, weights):
    count, width, rows = whole.shape
    fixed = lambda step, core: (0, 0)
    return pl.pallas_call(
        first_kernel,
        grid_spec=pltpu.PrefetchScalarGridSpec(
            num_scalar_prefetch=1,
            grid=(count // 2,),
            in_specs=qkv_specs(own_block, width, rows),
            out_specs=[pl.BlockSpec((rows, 512), fixed), pl.BlockSpec((1, rows), fixed)],
            scratch_shapes=[pltpu.VMEM((width, 512), jnp.bfloat16)],
        ),
        out_shape=[
            jax.ShapeDtypeStruct((rows, 512), jnp.float32),
            jax.ShapeDtypeStruct((1, rows), jnp.float32),
        ],
        compiler_params=pltpu.CompilerParams(vmem_limit_bytes=24 * 2**20),
        cost_estimate=pl.CostEstimate(
            flops=rows * 512 * D, bytes_accessed=5 * 2**20, transcendentals=0
        ),
    )(core, whole, gain, weights)


def project_second(
    core, whole, gain, weights, total, squares, cosine, sine, query_gain, key_gain
):
    count, width, rows = whole.shape
    fixed = lambda step, core: (0, 0)
    return pl.pallas_call(
        second_kernel,
        grid_spec=pltpu.PrefetchScalarGridSpec(
            num_scalar_prefetch=1,
            grid=(count // 2,),
            in_specs=qkv_specs(other_block, width, rows)
            + [
                pl.BlockSpec((rows, 512), fixed),
                pl.BlockSpec((1, rows), fixed),
                pl.BlockSpec((rows, HEAD_DIM), fixed),
                pl.BlockSpec((rows, HEAD_DIM), fixed),
                pl.BlockSpec((1, HEAD_DIM), fixed),
                pl.BlockSpec((1, HEAD_DIM), fixed),
            ],
            out_specs=[pl.BlockSpec((rows, 256), fixed), pl.BlockSpec((rows, 256), fixed)],
            scratch_shapes=[
                pltpu.VMEM((width, 512), jnp.bfloat16),
                pltpu.VMEM((rows, 512), jnp.float32),
                pltpu.VMEM((1, rows), jnp.float32),
            ],
        ),
        out_shape=[
            jax.ShapeDtypeStruct((rows, 256), jnp.bfloat16),
            jax.ShapeDtypeStruct((rows, 256), jnp.bfloat16),
        ],
        compiler_params=pltpu.CompilerParams(vmem_limit_bytes=24 * 2**20),
        cost_estimate=pl.CostEstimate(
            flops=rows * 512 * D, bytes_accessed=5 * 2**20, transcendentals=0
        ),
    )(
        core, whole, gain, weights, total, squares, cosine, sine,
        query_gain[None, :], key_gain[None, :],
    )


def out_kernel(
    core_ref, own_ref, other_ref, along_ref, across_ref, result_ref, squares_ref, total
):
    step = pl.program_id(0)

    @pl.when(step == 0)
    def _():
        total[...] = jnp.zeros_like(total)

    for heads_ref, weight_ref in ((own_ref, along_ref), (other_ref, across_ref)):
        left = weight_ref[:, 0, :ROWS_OUT, :].reshape(8 * ROWS_OUT, 512)
        right = weight_ref[:, 0, ROWS_OUT:, :]
        right = jnp.concatenate([right[:, :, :256], right[:, :, 256:]], axis=1)
        right = right.reshape(8 * ROWS_OUT, 256)
        heads = heads_ref[0]
        for first, part in ((0, left), (512, right)):
            total[first : first + part.shape[1], :] += lax.dot_general(
                part, heads, (((0,), (0,)), ((), ())), preferred_element_type=jnp.float32
            )

    @pl.when(step == pl.num_programs(0) - 1)
    def _():
        result = total[:WIDTH, :]
        result_ref[...] = result
        squares_ref[...] = jnp.sum(result * result, axis=0, keepdims=True)


def project_out(core, heads, along, across):
    count, depth, rows = heads.shape
    fixed = lambda step, core: (0, 0)
    weights = pl.BlockSpec(
        (8, 1, PAD_ALL - PAD_IN, 512), lambda step, core: (step % 2, step // 2, 2, 0)
    )
    return pl.pallas_call(
        out_kernel,
        grid_spec=pltpu.PrefetchScalarGridSpec(
            num_scalar_prefetch=1,
            grid=(count // 2,),
            in_specs=[
                pl.BlockSpec((1, depth, rows), lambda step, core: (own_block(step, core), 0, 0)),
                pl.BlockSpec((1, depth, rows), lambda step, core: (other_block(step, core), 0, 0)),
                weights,
                weights,
            ],
            out_specs=[pl.BlockSpec((WIDTH, rows), fixed), pl.BlockSpec((1, rows), fixed)],
            scratch_shapes=[pltpu.VMEM((768, rows), jnp.float32)],
        ),
        out_shape=[
            jax.ShapeDtypeStruct((WIDTH, rows), jnp.float32),
            jax.ShapeDtypeStruct((1, rows), jnp.float32),
        ],
        compiler_params=pltpu.CompilerParams(vmem_limit_bytes=24 * 2**20),
        cost_estimate=pl.CostEstimate(
            flops=2 * rows * 768 * 2048, bytes_accessed=5 * 2**20, transcendentals=0
        ),
    )(core, heads, heads, along, across)


def body(
    tokens,
    features,
    starts,
    sources,
    soft_gain,
    proj_weight,
    input_gain,
    query_weight,
    key_weight,
    value_weight,
    query_gain,
    key_gain,
    out_weight,
    post_gain,
):
    tok_rows, width = tokens.shape
    head_count = 8
    x_count = 4
    seq_count = x_count * Z
    core_index = lax.axis_index("core")
    z_index = lax.axis_index("z")
    seq_index = lax.axis_index(SEQ)
    total_rows = seq_count * tok_rows

    out_right = jnp.pad(out_weight[:, 512:], ((0, 0), (0, 768 - width)))
    local = jnp.concatenate(
        [
            jnp.pad(
                jnp.concatenate([query_weight, key_weight, value_weight], axis=1),
                ((0, PAD_IN - ROWS_IN), (0, 0)),
            ),
            out_weight[:, :512],
            jnp.concatenate([out_right[:16], out_right[16:]], axis=1),
        ],
        axis=0,
    )
    same_half = from_half(local, 0)
    other_half = from_half(local, 1)
    k_first = lax.axis_index("k") == 0
    both = jnp.stack(
        [
            jnp.where(k_first, same_half, other_half),
            jnp.where(k_first, other_half, same_half),
        ]
    )
    along = lax.all_gather(both, "z", axis=0)
    core = core_index.astype(jnp.int32)[None]

    image_count = starts.shape[0]
    vis = features.shape[2]
    pooled_side = PATCH_SIDE // POOL
    pool_rows = features.shape[0] // POOL
    block_rows = pool_rows * pooled_side
    shards_each = pooled_side // pool_rows
    patch_grid = features.reshape(pool_rows, POOL, pooled_side, POOL, vis)
    pooled = jnp.sum(patch_grid, axis=(1, 3), dtype=jnp.float32).reshape(block_rows, vis) / (
        POOL * POOL
    )
    soft = rms_scale(pooled, soft_gain).astype(jnp.bfloat16)
    vis_part = vis // head_count
    soft_part = lax.dynamic_slice_in_dim(
        soft, lax.axis_index(GIVEN_HEAD) * vis_part, vis_part, 1
    )
    soft_z = exchange(soft_part, "z", Z).reshape(Z * block_rows, vis_part)
    target = jnp.arange(8, dtype=jnp.int32)
    target_k, target_a, target_core = target // 4, target // 2 % 2, target % 2
    target_seq = (target_k * 2 + target_core) * Z + z_index
    frame_pos = (
        target_seq[:, None] * tok_rows + jnp.arange(tok_rows, dtype=jnp.int32)[None, :]
    ).reshape(-1)
    frame_image = image_of(frame_pos, starts)
    row_base = sources // shards_each * (block_rows * shards_each) - starts
    image_ids = jnp.arange(image_count, dtype=jnp.int32)
    frame_row = jnp.sum(
        jnp.where(frame_image[:, None] == image_ids[None, :], row_base[None, :], 0), axis=1
    )
    wanted = (frame_image >= 0) & jnp.repeat(target_a == core_index, tok_rows)
    frame_row = jnp.where(wanted, frame_row + frame_pos, -1)
    x_index = lax.axis_index(("k", "a"))
    here = x_index * (Z * block_rows) + jnp.arange(Z * block_rows, dtype=jnp.int32)
    chosen = (frame_row[:, None] == here[None, :]).astype(jnp.bfloat16)
    chosen = chosen.reshape(8, tok_rows, Z * block_rows)
    frames = jnp.einsum("sk,xps->xkp", soft_z, chosen, preferred_element_type=jnp.float32)
    frames = lax.all_to_all(
        frames.astype(jnp.bfloat16), ("k", "a", "core"), 0, 0, tiled=True
    )
    mine = jnp.sum(frames.astype(jnp.float32), axis=0).astype(jnp.bfloat16)
    soft_rows = exchange(mine, HEAD, head_count).reshape(vis, tok_rows)
    embedded = lax.dot_general(
        swapped(proj_weight), soft_rows, (((0,), (0,)), ((), ())),
        preferred_element_type=jnp.float32,
    ).astype(jnp.bfloat16)
    my_pos = seq_index * tok_rows + jnp.arange(tok_rows, dtype=jnp.int32)
    my_image = image_of(my_pos, starts)
    residual = jnp.where((my_image >= 0)[None, :], embedded, swapped(tokens).T)

    whole = exchange(residual, HEAD, head_count)
    along, residual = lax.optimization_barrier((along, residual))
    across = lax.ppermute(along, "core", [(0, 1), (1, 0)])
    half = HEAD_DIM // 2
    frequency = ROPE_BASE ** (-jnp.arange(half, dtype=jnp.float32) * 2.0 / HEAD_DIM)
    angles = my_pos.astype(jnp.float32)[:, None] * frequency[None, :]
    cosine, sine = jnp.cos(angles), jnp.sin(angles)
    gain_parts = input_gain.reshape(head_count, width, 1)
    total, row_squares = project_first(core, whole, gain_parts, along)
    queries, own = project_second(
        core,
        whole,
        gain_parts,
        across,
        total,
        row_squares,
        jnp.concatenate([cosine, cosine], axis=1),
        jnp.concatenate([-sine, sine], axis=1),
        query_gain,
        key_gain,
    )
    past_count = WINDOW // tok_rows
    pieces = [shifted(own, step) for step in range(past_count, 0, -1)]
    pieces += [own, shifted(own, -1)]
    window = jnp.concatenate(pieces, axis=0)
    key_pos = (seq_index - past_count) * tok_rows + jnp.arange(window.shape[0], dtype=jnp.int32)
    allowed = allowed_keys(my_pos, key_pos, starts, total_rows)
    attended = attend(
        queries.reshape(tok_rows, 1, 2, HEAD_DIM),
        window[:, :HEAD_DIM].reshape(-1, 1, HEAD_DIM),
        window[:, HEAD_DIM:].reshape(-1, 1, HEAD_DIM),
        allowed,
    )
    attended = attended.reshape(tok_rows, 2 * HEAD_DIM).T
    heads_all = exchange(attended, HEAD, head_count)
    projected, squares = project_out(core, heads_all, along, across)
    squares = jnp.sum(exchange(squares, HEAD, head_count), axis=0)
    gain = swapped(post_gain)[:, None]
    post = projected * lax.rsqrt(squares / D + EPSILON) * gain
    result = (residual.astype(jnp.float32) + post).astype(jnp.bfloat16)
    return swapped(result).T


def solution(mesh):
    split = Mesh(mesh.devices.reshape(2, 2, Z, 4, 2), ("k", "a", "z", "y", "core"))
    seq, head = GIVEN_SEQ, GIVEN_HEAD
    return jax.shard_map(
        body,
        mesh=split,
        in_specs=(
            P(seq, head),
            P(seq, None, None),
            P(),
            P(),
            P(),
            P(None, head),
            P(),
            P(seq, head),
            P(seq, head),
            P(seq, head),
            P(),
            P(),
            P(seq, head),
            P(head),
        ),
        out_specs=P(seq, head),
        check_vma=False,
    )
```

time: 255 us -> 254 us (level)
  local copies, waits for them, and re-layouts: 41.8 us -> 16.1 us
  starting transfers between devices: 57.6 us -> 76.8 us
  waiting for transfers between devices: 75.7 us -> 94.2 us
  Pallas kernels: 0 us -> 11.2 us
  matrix products: 13.3 us -> 3.18 us
  other arithmetic: 12.5 us -> 5.86 us
  blocking collectives: 37.5 us -> 31.8 us
    ppermute x5 -> x12, starting transfers between devices: 17.2 us -> 49.2 us  [the longest x5 18.7 us: shifted(): return lax.ppermute(value, ('k', 'z', 'core'), pairs)]
    all_gather x2 -> x0, blocking collectives: 21.6 us -> none  [the longest x1 10.9 us: body(): out_x = lax.all_gather(out_weight, 'x', axis=0, tiled=True)]
    reshape x4 -> x1, local copies, waits for them, and re-layouts: 21.8 us -> 4.17 us  [body(): gain_parts = input_gain.reshape(head_count, width, 1)]
    all_gather x2 -> x1, waiting for transfers between devices: 0.02 us -> 14.1 us  [body(): along = lax.all_gather(both, 'z', axis=0)]
    ppermute x5 -> x12, waiting for transfers between devices: 20 us -> 33.8 us  [the longest x5 15 us: shifted(): return lax.ppermute(value, ('k', 'z', 'core'), pairs)]
    all_to_all x4, starting transfers between devices: 40.4 us -> 27.6 us  [exchange(): return lax.all_to_all(spread, axes, 0, 0, tiled=True)]
    pallas_call x0 -> x3, Pallas kernels: none -> 11.2 us  [the longest x1 4.73 us: project_second(): pl.pallas_call(second_kernel, grid_spec=pltpu.PrefetchScalarGridSpec(num_...]
    dot_general x3 -> x1, matrix products: 11.3 us -> 0.62 us  [body(): lax.dot_general(swapped(proj_weight), soft_rows, (((0,), (0,)), ((), ()))...]
  transfers between devices with their start and end apart: 11 -> 17, of which waited for: 7 -> 11; matrix products, arithmetic and copies ran while one was open for 24% -> 6% of each run, Pallas kernels for 0% -> 1%
where the time goes in v2:
time: 254 us; the launch traced here: 253 us
  waiting for transfers between devices  94.2 us (37%)
  starting transfers between devices  76.8 us (30%)
  blocking collectives  31.8 us (13%)
  local copies, waits for them, and re-layouts  16.1 us (6%)
  between operations  13.9 us (5%)
  Pallas kernels  11.2 us (4%)
  other arithmetic  5.86 us (2%)
  matrix products  3.18 us (1%)
    all_to_all x4, waiting for transfers between devices, exchange(): return lax.all_to_all(spread, axes, 0, 0, tiled=True)  46.2 us
    all_to_all x4, starting transfers between devices, exchange(): return lax.all_to_all(spread, axes, 0, 0, tiled=True)  27.6 us
    ppermute x5, starting transfers between devices, shifted(): return lax.ppermute(value, ('k', 'z', 'core'), pairs)  18.7 us
    all_to_all x1, blocking collectives, exchange(): return lax.all_to_all(spread, axes, 0, 0, tiled=True)  18 us
    ppermute x5, waiting for transfers between devices, shifted(): return lax.ppermute(value, ('k', 'z', 'core'), pairs)  15 us
    ppermute x4, waiting for transfers between devices, swapped(): return lax.ppermute(value, ('a', 'core'), [(0, 0), (1, 2), (2, 1), (3, 3)])  14.7 us
    all_gather x1, waiting for transfers between devices, body(): along = lax.all_gather(both, 'z', axis=0)  14.1 us
    all_to_all x1, blocking collectives, body(): lax.all_to_all(frames.astype(jnp.bfloat16), ('k', 'a', 'core'), 0, 0, til...  13.8 us
  transfers between devices with their start and end apart: 17, of which 11 were waited for; matrix products, arithmetic and copies ran while one was open for 6% of the time, Pallas kernels for 1%

profile of v2, /device:TPU:1, one launch (start us, length us, event | category | flops | bytes accessed | tf_op | source)
XLA Modules:
  0.0 253.1 jit_solution(4798274759949906972)
XLA Ops:
  9.0 4.5 %collective-permute-start = (bf16[144,512]{1,0:T(8,128)(2,1)S(1)}, bf16[144,512]{1,0:T(8,128)(2,1)S(1)}, u32[]{:S(2)}, u32[]{:S(2)}) collective-permute-start(bf16[144,512]{1,0:T(8,128)(2,1)S(1)} %maximum_maximum_fusion), channel_id=1, source_target_pairs={{0,0},{1,128},{128,1},{129,129},{256,256},{257,384},{384,257},{385... | collective-permute-start | bytes 442376 | tf_op jit(solution)/shard_map/ppermute | solution.py:42
  13.5 3.4 %collective-permute-start.1 = (bf16[144,512]{1,0:T(8,128)(2,1)S(1)}, bf16[144,512]{1,0:T(8,128)(2,1)S(1)}, u32[]{:S(2)}, u32[]{:S(2)}) collective-permute-start(bf16[144,512]{1,0:T(8,128)(2,1)S(1)} %maximum_maximum_fusion), channel_id=1, source_target_pairs={{0,256},{1,384},{128,257},{129,385},{256,0},{257,128},{384,1},{385... | collective-permute-start | bytes 442376 | tf_op jit(solution)/shard_map/ppermute | solution.py:42
  17.0 4.2 %collective-permute-done.1 = bf16[144,512]{1,0:T(8,128)(2,1)S(1)} collective-permute-done((bf16[144,512]{1,0:T(8,128)(2,1)S(1)}, bf16[144,512]{1,0:T(8,128)(2,1)S(1)}, u32[]{:S(2)}, u32[]{:S(2)}) %collective-permute-start.1) | collective-permute-done | bytes 147488 | tf_op jit(solution)/shard_map/ppermute | solution.py:42
  25.0 15.4 %all-to-all-start = ((bf16[16,32,144]{2,1,0:T(8,128)(2,1)}), bf16[16,32,144]{2,1,0:T(8,128)(2,1)S(1)}, u32[]{:S(2)}, u32[]{:S(2)}) async-start(bf16[16,32,144]{2,1,0:T(8,128)(2,1)} %broadcast_in_dim.95), calls=%async_computation | async-start | bytes 524288 | tf_op jit(solution)/shard_map/all_to_all | solution.py:60
  40.4 2.3 collective-permute-start.2
  43.1 15.6 %all-to-all-done = bf16[16,32,144]{2,1,0:T(8,128)(2,1)S(1)} async-done(((bf16[16,32,144]{2,1,0:T(8,128)(2,1)}), bf16[16,32,144]{2,1,0:T(8,128)(2,1)S(1)}, u32[]{:S(2)}, u32[]{:S(2)}) %all-to-all-start) | async-done | bytes 147488 | tf_op jit(solution)/shard_map/all_to_all | solution.py:60
  60.0 13.8 %all_to_all.30 = bf16[8,144,256]{2,1,0:T(8,128)(2,1)S(1)} all-to-all(bf16[8,144,256]{2,1,0:T(8,128)(2,1)S(1)} %fusion.16), channel_id=1, replica_groups=mesh['k'=2,'a'=2,'z'=16,'y'=4,'core'=2] {'k','a','core'}, dimensions={0} | all-to-all | bytes 1179648 | tf_op jit(solution)/shard_map/all_to_all | solution.py:378
  74.8 4.6 %all-to-all-start.2 = ((bf16[8,144,256]{2,1,0:T(8,128)(2,1)}), bf16[8,144,256]{2,1,0:T(8,128)(2,1)S(1)}, u32[]{:S(2)}, u32[]{:S(2)}) async-start(bf16[8,144,256]{2,1,0:T(8,128)(2,1)} %broadcast_in_dim.96), calls=%async_computation.2 | async-start | bytes 1179648 | tf_op jit(solution)/shard_map/all_to_all | solution.py:60
  79.4 4.2 %collective-permute-start.3 = (bf16[256,672]{0,1:T(8,128)(2,1)S(1)}, bf16[256,672]{0,1:T(8,128)(2,1)S(1)}, u32[]{:S(2)}, u32[]{:S(2)}) collective-permute-start(bf16[256,672]{0,1:T(8,128)(2,1)S(1)} %copy-done.8), channel_id=1, source_target_pairs={{0,0},{1,128},{128,1},{129,129},{2,2},{3,130},{130,3},{131,131},{4... | collective-permute-start | bytes 1032200 | tf_op jit(solution)/shard_map/ppermute | solution.py:33
  83.7 8.7 %collective-permute-done.3 = bf16[256,672]{0,1:T(8,128)(2,1)S(1)} collective-permute-done((bf16[256,672]{0,1:T(8,128)(2,1)S(1)}, bf16[256,672]{0,1:T(8,128)(2,1)S(1)}, u32[]{:S(2)}, u32[]{:S(2)}) %collective-permute-start.3) | collective-permute-done | bytes 344096 | tf_op jit(solution)/shard_map/ppermute | solution.py:33
  93.0 14.1 %all-gather.3.cloned.1.call-done = bf16[32,144,512]{2,1,0:T(8,128)(2,1)} async-done(((bf16[2,144,512]{2,1,0:T(8,128)(2,1)}), bf16[32,144,512]{2,1,0:T(8,128)(2,1)}) %all-gather.3.cloned.1.call-update) | async-done | bytes 4718608 | tf_op jit(solution)/shard_map/all_gather | solution.py:340
  107.1 10.2 %collective-permute-start.4 = (bf16[16,2,144,512]{3,2,1,0:T(8,128)(2,1)}, bf16[16,2,144,512]{3,2,1,0:T(8,128)(2,1)}, u32[]{:S(2)}, u32[]{:S(2)}) collective-permute-start(bf16[16,2,144,512]{3,2,1,0:T(8,128)(2,1)} %bitcast.73), channel_id=1, source_target_pairs={{0,1},{1,0},{2,3},{3,2},{4,5},{5,4},{6,7},{7,6},{8,9},{9,8},{10,11... | collective-permute-start | bytes 14155784 | tf_op jit(solution)/shard_map/ppermute | solution.py:393
  119.0 4.3 %all-to-all-start.3 = ((bf16[8,672,256]{2,1,0:T(8,128)(2,1)}), bf16[8,672,256]{2,1,0:T(8,128)(2,1)S(1)}, u32[]{:S(2)}, u32[]{:S(2)}) async-start(bf16[8,672,256]{2,1,0:T(8,128)(2,1)} %broadcast_in_dim.98), calls=%async_computation.3 | async-start | bytes 5505024 | tf_op jit(solution)/shard_map/all_to_all | solution.py:60
  123.3 4.2 %reshape.340.gain_ref = f32[8,672,1]{2,1,0:T(8,128)} reshape(f32[5376]{0:T(1024)S(1)} %copy-done.5) | data formatting | bytes 43008 | tf_op jit(solution)/shard_map/reshape | solution.py:398
  128.4 28.8 %all-to-all-done.3.whole_ref = bf16[8,672,256]{2,1,0:T(8,128)(2,1)S(1)} async-done(((bf16[8,672,256]{2,1,0:T(8,128)(2,1)}), bf16[8,672,256]{2,1,0:T(8,128)(2,1)S(1)}, u32[]{:S(2)}, u32[]{:S(2)}) %all-to-all-start.3) | async-done | bytes 2752544 | tf_op jit(solution)/shard_map/all_to_all | solution.py:60
  158.9 2.3 copy-done.1
  161.2 2.8 %shard_map.136 = (f32[256,512]{1,0:T(8,128)S(1)}, f32[1,256]{1,0:T(1,128)S(1)}) custom-call(s32[1]{0:T(128)} %bitcast.9.core_ref, bf16[8,672,256]{2,1,0:T(8,128)(2,1)S(1)} %all-to-all-done.3.whole_ref, f32[8,672,1]{2,1,0:T(8,128)S(1)} %copy-done, bf16[16,2,144,512]{3,2,1,0:T(8,128)(2,1)S(1)} %bitcast.74), custom_call_target="tpu_custom_call" | custom-call | flops 704643072 | bytes 5242880 | tf_op jit(solution)/shard_map/pallas_call | solution.py:176
  164.1 4.7 %shard_map.137 = (bf16[256,256]{1,0:T(8,128)(2,1)S(1)}, bf16[256,256]{1,0:T(8,128)(2,1)S(1)}) custom-call(s32[1]{0:T(128)} %bitcast.9.core_ref, bf16[8,672,256]{2,1,0:T(8,128)(2,1)S(1)} %all-to-all-done.3.whole_ref, f32[8,672,1]{2,1,0:T(8,128)S(1)} %copy-done, bf16[16,2,144,512]{3,2,1,0:T(8,128)(2,1)} %collective-permute-done.4.weight_ref.across_ref, ...), custom_call_target="tpu_custom_call" | custom-call | flops 704643072 | bytes 5242880 | tf_op jit(solution)/shard_map/pallas_call | solution.py:201
  168.8 4.5 %collective-permute-start.5 = (bf16[256,256]{1,0:T(8,128)(2,1)S(1)}, bf16[256,256]{1,0:T(8,128)(2,1)S(1)}, u32[]{:S(2)}, u32[]{:S(2)}) collective-permute-start(bf16[256,256]{1,0:T(8,128)(2,1)S(1)} %get-tuple-element.17), channel_id=1, source_target_pairs={{0,32},{8,40},{16,48},{24,56},{32,64},{40,72},{48,80},{56,88},{64,... | collective-permute-start | bytes 393224 | tf_op jit(solution)/shard_map/ppermute | solution.py:55
  173.4 4.3 %collective-permute-start.6 = (bf16[256,256]{1,0:T(8,128)(2,1)S(1)}, bf16[256,256]{1,0:T(8,128)(2,1)S(1)}, u32[]{:S(2)}, u32[]{:S(2)}) collective-permute-start(bf16[256,256]{1,0:T(8,128)(2,1)S(1)} %get-tuple-element.17), channel_id=1, source_target_pairs={{0,24},{8,32},{16,40},{24,48},{32,56},{40,64},{48,72},{56,80},{64,... | collective-permute-start | bytes 393224 | tf_op jit(solution)/shard_map/ppermute | solution.py:55
  179.1 3.1 %collective-permute-start.7 = (bf16[256,256]{1,0:T(8,128)(2,1)S(1)}, bf16[256,256]{1,0:T(8,128)(2,1)S(1)}, u32[]{:S(2)}, u32[]{:S(2)}) collective-permute-start(bf16[256,256]{1,0:T(8,128)(2,1)S(1)} %get-tuple-element.17), channel_id=1, source_target_pairs={{0,16},{8,24},{16,32},{24,40},{32,48},{40,56},{48,64},{56,72},{64,... | collective-permute-start | bytes 393224 | tf_op jit(solution)/shard_map/ppermute | solution.py:55
  182.2 2.9 %collective-permute-start.8 = (bf16[256,256]{1,0:T(8,128)(2,1)S(1)}, bf16[256,256]{1,0:T(8,128)(2,1)S(1)}, u32[]{:S(2)}, u32[]{:S(2)}) collective-permute-start(bf16[256,256]{1,0:T(8,128)(2,1)S(1)} %get-tuple-element.17), channel_id=1, source_target_pairs={{0,8},{8,16},{16,24},{24,32},{32,40},{40,48},{48,56},{56,64},{64,7... | collective-permute-start | bytes 393224 | tf_op jit(solution)/shard_map/ppermute | solution.py:55
  185.1 3.9 %collective-permute-start.9 = (bf16[256,256]{1,0:T(8,128)(2,1)S(1)}, bf16[256,256]{1,0:T(8,128)(2,1)S(1)}, u32[]{:S(2)}, u32[]{:S(2)}) collective-permute-start(bf16[256,256]{1,0:T(8,128)(2,1)S(1)} %get-tuple-element.17), channel_id=1, source_target_pairs={{8,0},{16,8},{24,16},{32,24},{40,32},{48,40},{56,48},{64,56},{72,6... | collective-permute-start | bytes 393224 | tf_op jit(solution)/shard_map/ppermute | solution.py:55
  189.0 4.5 %collective-permute-done.6 = bf16[256,256]{1,0:T(8,128)(2,1)S(1)} collective-permute-done((bf16[256,256]{1,0:T(8,128)(2,1)S(1)}, bf16[256,256]{1,0:T(8,128)(2,1)S(1)}, u32[]{:S(2)}, u32[]{:S(2)}) %collective-permute-start.6) | collective-permute-done | bytes 131104 | tf_op jit(solution)/shard_map/ppermute | solution.py:55
  193.5 8.2 %collective-permute-done.7 = bf16[256,256]{1,0:T(8,128)(2,1)S(1)} collective-permute-done((bf16[256,256]{1,0:T(8,128)(2,1)S(1)}, bf16[256,256]{1,0:T(8,128)(2,1)S(1)}, u32[]{:S(2)}, u32[]{:S(2)}) %collective-permute-start.7) | collective-permute-done | bytes 131104 | tf_op jit(solution)/shard_map/ppermute | solution.py:55
  201.8 2.2 collective-permute-done.8
  205.9 18.0 %all_to_all.31.own_ref.other_ref = bf16[8,256,256]{2,1,0:T(8,128)(2,1)S(1)} all-to-all(bf16[8,256,256]{2,1,0:T(8,128)(2,1)S(1)} %broadcast_in_dim.105), channel_id=1, replica_groups=mesh['k'=2,'a'=2,'z'=16,'y'=4,'core'=2] {'y','a'}, dimensions={0} | all-to-all | bytes 2097152 | tf_op jit(solution)/shard_map/all_to_all | solution.py:60
  223.9 3.7 %shard_map.138 = (f32[672,256]{1,0:T(8,128)S(1)}, f32[1,256]{1,0:T(1,128)S(1)}) custom-call(s32[1]{0:T(128)} %bitcast.9.core_ref, bf16[8,256,256]{2,1,0:T(8,128)(2,1)S(1)} %all_to_all.31.own_ref.other_ref, bf16[8,256,256]{2,1,0:T(8,128)(2,1)S(1)} %all_to_all.31.own_ref.other_ref, bf16[16,2,144,512]{3,2,1,0:T(8,128)(2,1)S(1)} %bitcast.77, ...), custom_call_target="tpu_custom_call" | custom-call | flops 805306368 | bytes 5242880 | tf_op jit(solution)/shard_map/pallas_call | solution.py:269
  228.2 3.3 %all-to-all-start.5 = ((f32[8,1,256]{2,1,0:T(1,128)}), f32[8,1,256]{2,1,0:T(1,128)S(1)}, u32[]{:S(2)}, u32[]{:S(2)}) async-start(f32[8,1,256]{2,1,0:T(1,128)} %broadcast_in_dim.173), calls=%async_computation.5 | async-start | bytes 16384 | tf_op jit(solution)/shard_map/all_to_all | solution.py:60
  231.6 3.1 %collective-permute-start.10 = (f32[672]{0:T(1024)S(1)}, f32[672]{0:T(1024)S(1)}, u32[]{:S(2)}, u32[]{:S(2)}) collective-permute-start(f32[672]{0:T(1024)S(1)} %copy-done.9), channel_id=1, source_target_pairs={{0,0},{1,128},{128,1},{129,129},{2,2},{3,130},{130,3},{131,131},{4... | collective-permute-start | bytes 8072 | tf_op jit(solution)/shard_map/ppermute | solution.py:33
  237.0 2.8 %collective-permute-start.11 = (bf16[672,256]{1,0:T(8,128)(2,1)S(1)}, bf16[672,256]{1,0:T(8,128)(2,1)S(1)}, u32[]{:S(2)}, u32[]{:S(2)}) collective-permute-start(bf16[672,256]{1,0:T(8,128)(2,1)S(1)} %add_convert_fusion), channel_id=1, source_target_pairs={{0,0},{1,128},{128,1},{129,129},{2,2},{3,130},{130,3},{131,131},{4... | collective-permute-start | bytes 1032200 | tf_op jit(solution)/shard_map/ppermute | solution.py:33
  239.8 5.8 %collective-permute-done.11 = bf16[672,256]{1,0:T(8,128)(2,1)S(1)} collective-permute-done((bf16[672,256]{1,0:T(8,128)(2,1)S(1)}, bf16[672,256]{1,0:T(8,128)(2,1)S(1)}, u32[]{:S(2)}, u32[]{:S(2)}) %collective-permute-start.11) | collective-permute-done | bytes 344096 | tf_op jit(solution)/shard_map/ppermute | solution.py:33
  (95 shorter events, 20.8 us)
Async XLA Ops:
  6.5 15.4 %copy-start.4 = (bf16[8,64,1152]{2,1,0:T(8,128)(2,1)S(1)}, bf16[8,64,1152]{2,1,0:T(8,128)(2,1)}, u32[]{:S(2)}) copy-start(bf16[8,64,1152]{2,1,0:T(8,128)(2,1)} %param.15) | copy-start | bytes 3538948
  6.5 100.5 %all-gather.3.cloned.1.call-start = ((), (), s32[]{:S(2)}) async-start(), calls=%async_computation.6 | async-start | bytes 5013504 | tf_op jit(solution)/shard_map/all_gather | solution.py:340
  9.0 8.0 %collective-permute-start = (bf16[144,512]{1,0:T(8,128)(2,1)S(1)}, bf16[144,512]{1,0:T(8,128)(2,1)S(1)}, u32[]{:S(2)}, u32[]{:S(2)}) collective-permute-start(bf16[144,512]{1,0:T(8,128)(2,1)S(1)} %maximum_maximum_fusion), channel_id=1, source_target_pairs={{0,0},{1,128},{128,1},{129,129},{256,256},{257,384},{384,257},{385... | collective-permute-start | bytes 442376 | tf_op jit(solution)/shard_map/ppermute | solution.py:42
  13.5 7.7 %collective-permute-start.1 = (bf16[144,512]{1,0:T(8,128)(2,1)S(1)}, bf16[144,512]{1,0:T(8,128)(2,1)S(1)}, u32[]{:S(2)}, u32[]{:S(2)}) collective-permute-start(bf16[144,512]{1,0:T(8,128)(2,1)S(1)} %maximum_maximum_fusion), channel_id=1, source_target_pairs={{0,256},{1,384},{128,257},{129,385},{256,0},{257,128},{384,1},{385... | collective-permute-start | bytes 442376 | tf_op jit(solution)/shard_map/ppermute | solution.py:42
  22.0 20.8 %copy-start.6 = (s32[8]{0:T(128)S(1)}, s32[8]{0:T(128)}, u32[]{:S(2)}) copy-start(s32[8]{0:T(128)} %param.16) | copy-start | bytes 100
  22.0 20.8 %copy-start.7 = (s32[8]{0:T(128)S(1)}, s32[8]{0:T(128)}, u32[]{:S(2)}) copy-start(s32[8]{0:T(128)} %param.17) | copy-start | bytes 100
  25.0 33.7 %all-to-all-start = ((bf16[16,32,144]{2,1,0:T(8,128)(2,1)}), bf16[16,32,144]{2,1,0:T(8,128)(2,1)S(1)}, u32[]{:S(2)}, u32[]{:S(2)}) async-start(bf16[16,32,144]{2,1,0:T(8,128)(2,1)} %broadcast_in_dim.95), calls=%async_computation | async-start | bytes 524288 | tf_op jit(solution)/shard_map/all_to_all | solution.py:60
  40.4 52.0 %collective-permute-start.2 = (bf16[1152,672]{0,1:T(8,128)(2,1)}, bf16[1152,672]{0,1:T(8,128)(2,1)S(1)}, u32[]{:S(2)}, u32[]{:S(2)}) collective-permute-start(bf16[1152,672]{0,1:T(8,128)(2,1)} %param.19), channel_id=1, source_target_pairs={{0,0},{1,128},{128,1},{129,129},{2,2},{3,130},{130,3},{131,131},{4... | collective-permute-start | bytes 4644872 | tf_op jit(solution)/shard_map/ppermute | solution.py:33
  58.7 20.6 %copy-start.8 = (bf16[256,672]{0,1:T(8,128)(2,1)S(1)}, bf16[256,672]{0,1:T(8,128)(2,1)}, u32[]{:S(2)}) copy-start(bf16[256,672]{0,1:T(8,128)(2,1)} %param.14) | copy-start | bytes 1032196
  74.8 17.6 %all-to-all-start.2 = ((bf16[8,144,256]{2,1,0:T(8,128)(2,1)}), bf16[8,144,256]{2,1,0:T(8,128)(2,1)S(1)}, u32[]{:S(2)}, u32[]{:S(2)}) async-start(bf16[8,144,256]{2,1,0:T(8,128)(2,1)} %broadcast_in_dim.96), calls=%async_computation.2 | async-start | bytes 1179648 | tf_op jit(solution)/shard_map/all_to_all | solution.py:60
  79.4 13.0 %collective-permute-start.3 = (bf16[256,672]{0,1:T(8,128)(2,1)S(1)}, bf16[256,672]{0,1:T(8,128)(2,1)S(1)}, u32[]{:S(2)}, u32[]{:S(2)}) collective-permute-start(bf16[256,672]{0,1:T(8,128)(2,1)S(1)} %copy-done.8), channel_id=1, source_target_pairs={{0,0},{1,128},{128,1},{129,129},{2,2},{3,130},{130,3},{131,131},{4... | collective-permute-start | bytes 1032200 | tf_op jit(solution)/shard_map/ppermute | solution.py:33
  107.1 57.0 %collective-permute-start.4 = (bf16[16,2,144,512]{3,2,1,0:T(8,128)(2,1)}, bf16[16,2,144,512]{3,2,1,0:T(8,128)(2,1)}, u32[]{:S(2)}, u32[]{:S(2)}) collective-permute-start(bf16[16,2,144,512]{3,2,1,0:T(8,128)(2,1)} %bitcast.73), channel_id=1, source_target_pairs={{0,1},{1,0},{2,3},{3,2},{4,5},{5,4},{6,7},{7,6},{8,9},{9,8},{10,11... | collective-permute-start | bytes 14155784 | tf_op jit(solution)/shard_map/ppermute | solution.py:393
  119.0 4.3 %copy-start.5 = (f32[5376]{0:T(1024)S(1)}, f32[5376]{0:T(1024)}, u32[]{:S(2)}) copy-start(f32[5376]{0:T(1024)} %param.20) | copy-start | bytes 64516
  119.0 38.2 %all-to-all-start.3 = ((bf16[8,672,256]{2,1,0:T(8,128)(2,1)}), bf16[8,672,256]{2,1,0:T(8,128)(2,1)S(1)}, u32[]{:S(2)}, u32[]{:S(2)}) async-start(bf16[8,672,256]{2,1,0:T(8,128)(2,1)} %broadcast_in_dim.98), calls=%async_computation.3 | async-start | bytes 5505024 | tf_op jit(solution)/shard_map/all_to_all | solution.py:60
  157.1 1.8 copy-start
  158.9 2.3 copy-start.1
  161.2 2.8 %copy-start.2 = (f32[128]{0:T(128)S(1)}, f32[128]{0:T(128)}, u32[]{:S(2)}) copy-start(f32[128]{0:T(128)} %param.24) | copy-start | bytes 1540
  161.2 2.8 %copy-start.3 = (f32[128]{0:T(128)S(1)}, f32[128]{0:T(128)}, u32[]{:S(2)}) copy-start(f32[128]{0:T(128)} %param.25) | copy-start | bytes 1540
  168.8 20.2 %collective-permute-start.5 = (bf16[256,256]{1,0:T(8,128)(2,1)S(1)}, bf16[256,256]{1,0:T(8,128)(2,1)S(1)}, u32[]{:S(2)}, u32[]{:S(2)}) collective-permute-start(bf16[256,256]{1,0:T(8,128)(2,1)S(1)} %get-tuple-element.17), channel_id=1, source_target_pairs={{0,32},{8,40},{16,48},{24,56},{32,64},{40,72},{48,80},{56,88},{64,... | collective-permute-start | bytes 393224 | tf_op jit(solution)/shard_map/ppermute | solution.py:55
  173.4 20.1 %collective-permute-start.6 = (bf16[256,256]{1,0:T(8,128)(2,1)S(1)}, bf16[256,256]{1,0:T(8,128)(2,1)S(1)}, u32[]{:S(2)}, u32[]{:S(2)}) collective-permute-start(bf16[256,256]{1,0:T(8,128)(2,1)S(1)} %get-tuple-element.17), channel_id=1, source_target_pairs={{0,24},{8,32},{16,40},{24,48},{32,56},{40,64},{48,72},{56,80},{64,... | collective-permute-start | bytes 393224 | tf_op jit(solution)/shard_map/ppermute | solution.py:55
  179.1 22.7 %collective-permute-start.7 = (bf16[256,256]{1,0:T(8,128)(2,1)S(1)}, bf16[256,256]{1,0:T(8,128)(2,1)S(1)}, u32[]{:S(2)}, u32[]{:S(2)}) collective-permute-start(bf16[256,256]{1,0:T(8,128)(2,1)S(1)} %get-tuple-element.17), channel_id=1, source_target_pairs={{0,16},{8,24},{16,32},{24,40},{32,48},{40,56},{48,64},{56,72},{64,... | collective-permute-start | bytes 393224 | tf_op jit(solution)/shard_map/ppermute | solution.py:55
  182.2 21.8 %collective-permute-start.8 = (bf16[256,256]{1,0:T(8,128)(2,1)S(1)}, bf16[256,256]{1,0:T(8,128)(2,1)S(1)}, u32[]{:S(2)}, u32[]{:S(2)}) collective-permute-start(bf16[256,256]{1,0:T(8,128)(2,1)S(1)} %get-tuple-element.17), channel_id=1, source_target_pairs={{0,8},{8,16},{16,24},{24,32},{32,40},{40,48},{48,56},{56,64},{64,7... | collective-permute-start | bytes 393224 | tf_op jit(solution)/shard_map/ppermute | solution.py:55
  185.1 19.0 %collective-permute-start.9 = (bf16[256,256]{1,0:T(8,128)(2,1)S(1)}, bf16[256,256]{1,0:T(8,128)(2,1)S(1)}, u32[]{:S(2)}, u32[]{:S(2)}) collective-permute-start(bf16[256,256]{1,0:T(8,128)(2,1)S(1)} %get-tuple-element.17), channel_id=1, source_target_pairs={{8,0},{16,8},{24,16},{32,24},{40,32},{48,40},{56,48},{64,56},{72,6... | collective-permute-start | bytes 393224 | tf_op jit(solution)/shard_map/ppermute | solution.py:55
  204.1 19.8 %slice-start = ((s8[4718592]{0:T(1024)(128)(4,1)}), s8[4194304]{0:T(1024)(128)(4,1)S(1)}, s32[]{:S(2)}) async-start(s8[4718592]{0:T(1024)(128)(4,1)} %bitcast.75), calls=%async_computation.7 | async-start | bytes 8388608
  204.7 19.2 %slice-start.1 = ((s8[4718592]{0:T(1024)(128)(4,1)}), s8[524288]{0:T(1024)(128)(4,1)S(1)}, s32[]{:S(2)}) async-start(s8[4718592]{0:T(1024)(128)(4,1)} %bitcast.75), calls=%async_computation.8 | async-start | bytes 1048576
  223.9 7.6 %copy-start.9 = (f32[672]{0:T(1024)S(1)}, f32[672]{0:T(1024)}, u32[]{:S(2)}) copy-start(f32[672]{0:T(1024)} %param.27) | copy-start | bytes 8068
  228.2 8.3 %all-to-all-start.5 = ((f32[8,1,256]{2,1,0:T(1,128)}), f32[8,1,256]{2,1,0:T(1,128)S(1)}, u32[]{:S(2)}, u32[]{:S(2)}) async-start(f32[8,1,256]{2,1,0:T(1,128)} %broadcast_in_dim.173), calls=%async_computation.5 | async-start | bytes 16384 | tf_op jit(solution)/shard_map/all_to_all | solution.py:60
  231.6 5.2 %collective-permute-start.10 = (f32[672]{0:T(1024)S(1)}, f32[672]{0:T(1024)S(1)}, u32[]{:S(2)}, u32[]{:S(2)}) collective-permute-start(f32[672]{0:T(1024)S(1)} %copy-done.9), channel_id=1, source_target_pairs={{0,0},{1,128},{128,1},{129,129},{2,2},{3,130},{130,3},{131,131},{4... | collective-permute-start | bytes 8072 | tf_op jit(solution)/shard_map/ppermute | solution.py:33
  237.0 8.6 %collective-permute-start.11 = (bf16[672,256]{1,0:T(8,128)(2,1)S(1)}, bf16[672,256]{1,0:T(8,128)(2,1)S(1)}, u32[]{:S(2)}, u32[]{:S(2)}) collective-permute-start(bf16[672,256]{1,0:T(8,128)(2,1)S(1)} %add_convert_fusion), channel_id=1, source_target_pairs={{0,0},{1,128},{128,1},{129,129},{2,2},{3,130},{130,3},{131,131},{4... | collective-permute-start | bytes 1032200 | tf_op jit(solution)/shard_map/ppermute | solution.py:33
Sparse Core Ops, SparseCore 0:
  22.1 84.9 all-gather.2

commit v3 on v2

--- a/solution.py
+++ b/solution.py
@@ -18,6 +18,7 @@
 PAD_IN = 96
 PAD_ALL = 144
 WIDTH = 672
+UPPER = 512
 
 EPSILON = 1e-06
 QUERY_SCALE = 168.0 ** (-0.5)
@@ -55,9 +56,9 @@
     return lax.ppermute(value, ("k", "z", "core"), pairs)
 
 
-def exchange(value, axes, count):
+def exchange(value, axes, count, groups=None):
     spread = jnp.broadcast_to(value[None], (count, *value.shape))
-    return lax.all_to_all(spread, axes, 0, 0, tiled=True)
+    return lax.all_to_all(spread, axes, 0, 0, tiled=True, axis_index_groups=groups)
 
 
 def rms_scale(inputs, scale_gain):
@@ -96,10 +97,10 @@
     return (mixed_heads / jnp.transpose(row_sum, (2, 0, 1))[..., None]).astype(jnp.bfloat16)
 
 
-def add_part(whole_ref, gain_ref, weight_ref, block, start, squares):
+def add_part(upper_ref, lower_ref, gain_ref, weight_ref, block, start, squares):
     for shard in range(8):
         block[shard * ROWS_IN : (shard + 1) * ROWS_IN, :] = weight_ref[shard, 0, :ROWS_IN, :]
-    part = whole_ref[0].astype(jnp.float32)
+    part = jnp.concatenate([upper_ref[0], lower_ref[0]], axis=0).astype(jnp.float32)
     scaled = (part * gain_ref[0]).astype(jnp.bfloat16)
     product = lax.dot_general(
         scaled, block[...], (((0,), (0,)), ((), ())), preferred_element_type=jnp.float32
@@ -107,19 +108,21 @@
     return start + product, squares + jnp.sum(part * part, axis=0, keepdims=True)
 
 
-def first_kernel(core_ref, whole_ref, gain_ref, weight_ref, total_ref, squares_ref, block):
+def first_kernel(
+    core_ref, upper_ref, lower_ref, gain_ref, weight_ref, total_ref, squares_ref, block
+):
     @pl.when(pl.program_id(0) == 0)
     def _():
         total_ref[...] = jnp.zeros_like(total_ref)
         squares_ref[...] = jnp.zeros_like(squares_ref)
 
     total_ref[...], squares_ref[...] = add_part(
-        whole_ref, gain_ref, weight_ref, block, total_ref[...], squares_ref[...]
+        upper_ref, lower_ref, gain_ref, weight_ref, block, total_ref[...], squares_ref[...]
     )
 
 
 def second_kernel(
-    core_ref, whole_ref, gain_ref, weight_ref, start_ref, square_ref, cos_ref, sin_ref,
+    core_ref, upper_ref, lower_ref, gain_ref, weight_ref, start_ref, square_ref, cos_ref, sin_ref,
     query_gain_ref, key_gain_ref, query_ref, pair_ref, block, total, squares,
 ):
     step = pl.program_id(0)
@@ -130,7 +133,7 @@
         squares[...] = square_ref[...]
 
     total[...], squares[...] = add_part(
-        whole_ref, gain_ref, weight_ref, block, total[...], squares[...]
+        upper_ref, lower_ref, gain_ref, weight_ref, block, total[...], squares[...]
     )
 
     @pl.when(step == pl.num_programs(0) - 1)
@@ -163,15 +166,20 @@
 
 
 def qkv_specs(block_of, width, rows):
+    def parts(height):
+        return pl.BlockSpec((1, height, rows), lambda step, core: (block_of(step, core), 0, 0))
+
     return [
-        pl.BlockSpec((1, width, rows), lambda step, core: (block_of(step, core), 0, 0)),
+        parts(UPPER),
+        parts(width - UPPER),
         pl.BlockSpec((1, width, 1), lambda step, core: (block_of(step, core), 0, 0)),
         pl.BlockSpec((8, 1, PAD_IN, 512), lambda step, core: (step % 2, step // 2, 0, 0)),
     ]
 
 
-def project_first(core, whole, gain, weights):
-    count, width, rows = whole.shape
+def project_first(core, upper, lower, gain, weights):
+    count, _, rows = upper.shape
+    width = WIDTH
     fixed = lambda step, core: (0, 0)
     return pl.pallas_call(
         first_kernel,
@@ -190,13 +198,14 @@
         cost_estimate=pl.CostEstimate(
             flops=rows * 512 * D, bytes_accessed=5 * 2**20, transcendentals=0
         ),
-    )(core, whole, gain, weights)
+    )(core, upper, lower, gain, weights)
 
 
 def project_second(
-    core, whole, gain, weights, total, squares, cosine, sine, query_gain, key_gain
+    core, upper, lower, gain, weights, total, squares, cosine, sine, query_gain, key_gain
 ):
-    count, width, rows = whole.shape
+    count, _, rows = upper.shape
+    width = WIDTH
     fixed = lambda step, core: (0, 0)
     return pl.pallas_call(
         second_kernel,
@@ -228,7 +237,7 @@
             flops=rows * 512 * D, bytes_accessed=5 * 2**20, transcendentals=0
         ),
     )(
-        core, whole, gain, weights, total, squares, cosine, sine,
+        core, upper, lower, gain, weights, total, squares, cosine, sine,
         query_gain[None, :], key_gain[None, :],
     )
 
@@ -355,7 +364,10 @@
     soft_part = lax.dynamic_slice_in_dim(
         soft, lax.axis_index(GIVEN_HEAD) * vis_part, vis_part, 1
     )
-    soft_z = exchange(soft_part, "z", Z).reshape(Z * block_rows, vis_part)
+    near_groups = [[4 * i + j for j in range(4)] for i in range(Z // 4)]
+    far_groups = [[4 * i + j for i in range(Z // 4)] for j in range(4)]
+    soft_z = exchange(soft_part, "z", 4, near_groups).reshape(4 * block_rows, vis_part)
+    soft_z = exchange(soft_z, "z", 4, far_groups).reshape(Z * block_rows, vis_part)
     target = jnp.arange(8, dtype=jnp.int32)
     target_k, target_a, target_core = target // 4, target // 2 % 2, target % 2
     target_seq = (target_k * 2 + target_core) * Z + z_index
@@ -388,18 +400,20 @@
     my_image = image_of(my_pos, starts)
     residual = jnp.where((my_image >= 0)[None, :], embedded, swapped(tokens).T)
 
-    whole = exchange(residual, HEAD, head_count)
-    along, residual = lax.optimization_barrier((along, residual))
+    upper = exchange(residual[:UPPER], HEAD, head_count)
+    lower = exchange(residual[UPPER:], HEAD, head_count)
+    along, upper = lax.optimization_barrier((along, upper))
     across = lax.ppermute(along, "core", [(0, 1), (1, 0)])
     half = HEAD_DIM // 2
     frequency = ROPE_BASE ** (-jnp.arange(half, dtype=jnp.float32) * 2.0 / HEAD_DIM)
     angles = my_pos.astype(jnp.float32)[:, None] * frequency[None, :]
     cosine, sine = jnp.cos(angles), jnp.sin(angles)
     gain_parts = input_gain.reshape(head_count, width, 1)
-    total, row_squares = project_first(core, whole, gain_parts, along)
+    total, row_squares = project_first(core, upper, lower, gain_parts, along)
     queries, own = project_second(
         core,
-        whole,
+        upper,
+        lower,
         gain_parts,
         across,
         total,
@@ -410,9 +424,8 @@
         key_gain,
     )
     past_count = WINDOW // tok_rows
-    pieces = [shifted(own, step) for step in range(past_count, 0, -1)]
-    pieces += [own, shifted(own, -1)]
-    window = jnp.concatenate(pieces, axis=0)
+    near = jnp.concatenate([shifted(own, 2), shifted(own, 1)], axis=0)
+    window = jnp.concatenate([shifted(near, 2), near, own, shifted(own, -1)], axis=0)
     key_pos = (seq_index - past_count) * tok_rows + jnp.arange(window.shape[0], dtype=jnp.int32)
     allowed = allowed_keys(my_pos, key_pos, starts, total_rows)
     attended = attend(
@@ -422,13 +435,16 @@
         allowed,
     )
     attended = attended.reshape(tok_rows, 2 * HEAD_DIM).T
+    attended, residual = lax.optimization_barrier((attended, residual))
     heads_all = exchange(attended, HEAD, head_count)
     projected, squares = project_out(core, heads_all, along, across)
-    squares = jnp.sum(exchange(squares, HEAD, head_count), axis=0)
-    gain = swapped(post_gain)[:, None]
-    post = projected * lax.rsqrt(squares / D + EPSILON) * gain
-    result = (residual.astype(jnp.float32) + post).astype(jnp.bfloat16)
-    return swapped(result).T
+    given_residual = swapped(residual).astype(jnp.float32)
+    given = swapped(projected.astype(jnp.bfloat16)).astype(jnp.float32)
+    all_squares = exchange(squares, ("a", "y", "core"), 16).reshape(8, 2, tok_rows)
+    from_core = jnp.arange(2, dtype=jnp.int32) == lax.axis_index("a")
+    squares = jnp.sum(jnp.where(from_core[None, :, None], all_squares, 0.0), axis=(0, 1))
+    post = given * lax.rsqrt(squares[None, :] / D + EPSILON) * post_gain[:, None]
+    return (given_residual + post).astype(jnp.bfloat16).T
 
 
 def solution(mesh):

time: 254 us -> 243 us (0.957)
  waiting for transfers between devices: 94.2 us -> 72.5 us
  blocking collectives: 31.8 us -> 44.3 us
  starting transfers between devices: 76.8 us -> 68.8 us
  other arithmetic: 5.86 us -> 9.69 us
    all_gather x1, waiting for transfers between devices: 14.1 us -> 0.01 us  [body(): along = lax.all_gather(both, 'z', axis=0)]
    all_to_all x1, blocking collectives: 18 us -> 30 us  [exchange(): lax.all_to_all(spread, axes, 0, 0, tiled=True, axis_index_groups=groups)]
    ppermute x5 -> x4, starting transfers between devices: 18.7 us -> 10.4 us  [shifted(): return lax.ppermute(value, ('k', 'z', 'core'), pairs)]
    ppermute x1, starting transfers between devices: 10.2 us -> 3.62 us  [body(): across = lax.ppermute(along, 'core', [(0, 1), (1, 0)])]
    all_to_all x4 -> x6, starting transfers between devices: 27.6 us -> 33.8 us  [exchange(): lax.all_to_all(spread, axes, 0, 0, tiled=True, axis_index_groups=groups)]
    ppermute x4, waiting for transfers between devices: 14.7 us -> 8.68 us  [swapped(): return lax.ppermute(value, ('a', 'core'), [(0, 0), (1, 2), (2, 1), (3, 3)])]
    all_to_all x4 -> x6, waiting for transfers between devices: 46.2 us -> 43.7 us  [exchange(): lax.all_to_all(spread, axes, 0, 0, tiled=True, axis_index_groups=groups)]
    unnamed x31 -> x51, local copies, waits for them, and re-layouts: 4.95 us -> 6.42 us
  transfers between devices with their start and end apart: 17 -> 18, of which waited for: 11 -> 10; matrix products, arithmetic and copies ran while one was open for 6% -> 7% of each run, Pallas kernels for 1% -> 3%
where the time goes in v3:
time: 243 us; the launch traced here: 242 us
  waiting for transfers between devices  72.5 us (30%)
  starting transfers between devices  68.8 us (28%)
  blocking collectives  44.3 us (18%)
  local copies, waits for them, and re-layouts  17.9 us (7%)
  between operations  14.1 us (6%)
  Pallas kernels  11.1 us (5%)
  other arithmetic  9.69 us (4%)
  matrix products  3.18 us (1%)
    all_to_all x6, waiting for transfers between devices, exchange(): lax.all_to_all(spread, axes, 0, 0, tiled=True, axis_index_groups=groups)  43.7 us
    all_to_all x6, starting transfers between devices, exchange(): lax.all_to_all(spread, axes, 0, 0, tiled=True, axis_index_groups=groups)  33.8 us
    all_to_all x1, blocking collectives, exchange(): lax.all_to_all(spread, axes, 0, 0, tiled=True, axis_index_groups=groups)  30 us
    ppermute x4, waiting for transfers between devices, shifted(): return lax.ppermute(value, ('k', 'z', 'core'), pairs)  15.9 us
    all_to_all x1, blocking collectives, body(): lax.all_to_all(frames.astype(jnp.bfloat16), ('k', 'a', 'core'), 0, 0, til...  14.3 us
    ppermute x4, starting transfers between devices, swapped(): return lax.ppermute(value, ('a', 'core'), [(0, 0), (1, 2), (2, 1), (3, 3)])  13 us
    ppermute x4, starting transfers between devices, shifted(): return lax.ppermute(value, ('k', 'z', 'core'), pairs)  10.4 us
    ppermute x4, waiting for transfers between devices, swapped(): return lax.ppermute(value, ('a', 'core'), [(0, 0), (1, 2), (2, 1), (3, 3)])  8.68 us
  transfers between devices with their start and end apart: 18, of which 10 were waited for; matrix products, arithmetic and copies ran while one was open for 7% of the time, Pallas kernels for 3%

profile of v3, /device:TPU:1, one launch (start us, length us, event | category | flops | bytes accessed | tf_op | source)
XLA Modules:
  0.0 241.6 jit_solution(4566967421353294265)
XLA Ops:
  9.0 4.5 %collective-permute-start = (bf16[144,512]{1,0:T(8,128)(2,1)S(1)}, bf16[144,512]{1,0:T(8,128)(2,1)S(1)}, u32[]{:S(2)}, u32[]{:S(2)}) collective-permute-start(bf16[144,512]{1,0:T(8,128)(2,1)S(1)} %maximum_maximum_fusion), channel_id=1, source_target_pairs={{0,0},{1,128},{128,1},{129,129},{256,256},{257,384},{384,257},{385... | collective-permute-start | bytes 442376 | tf_op jit(solution)/shard_map/ppermute | solution.py:43
  13.5 3.4 %collective-permute-start.1 = (bf16[144,512]{1,0:T(8,128)(2,1)S(1)}, bf16[144,512]{1,0:T(8,128)(2,1)S(1)}, u32[]{:S(2)}, u32[]{:S(2)}) collective-permute-start(bf16[144,512]{1,0:T(8,128)(2,1)S(1)} %maximum_maximum_fusion), channel_id=1, source_target_pairs={{0,256},{1,384},{128,257},{129,385},{256,0},{257,128},{384,1},{385... | collective-permute-start | bytes 442376 | tf_op jit(solution)/shard_map/ppermute | solution.py:43
  17.0 4.2 %collective-permute-done.1 = bf16[144,512]{1,0:T(8,128)(2,1)S(1)} collective-permute-done((bf16[144,512]{1,0:T(8,128)(2,1)S(1)}, bf16[144,512]{1,0:T(8,128)(2,1)S(1)}, u32[]{:S(2)}, u32[]{:S(2)}) %collective-permute-start.1) | collective-permute-done | bytes 147488 | tf_op jit(solution)/shard_map/ppermute | solution.py:43
  24.9 6.1 %all-to-all-start = ((bf16[4,32,144]{2,1,0:T(8,128)(2,1)}), bf16[4,32,144]{2,1,0:T(8,128)(2,1)S(1)}, u32[]{:S(2)}, u32[]{:S(2)}) async-start(bf16[4,32,144]{2,1,0:T(8,128)(2,1)} %broadcast_in_dim.114), calls=%async_computation | async-start | bytes 131072 | tf_op jit(solution)/shard_map/all_to_all | solution.py:61
  36.4 12.5 %all-to-all-start.1 = ((bf16[4,128,144]{1,2,0:T(8,128)(2,1)}), bf16[4,128,144]{1,2,0:T(8,128)(2,1)S(1)}, u32[]{:S(2)}, u32[]{:S(2)}) async-start(bf16[4,128,144]{1,2,0:T(8,128)(2,1)} %broadcast_in_dim.116), calls=%async_computation.1 | async-start | bytes 294912 | tf_op jit(solution)/shard_map/all_to_all | solution.py:61
  49.0 18.0 %all-to-all-done.1 = bf16[4,128,144]{1,2,0:T(8,128)(2,1)S(1)} async-done(((bf16[4,128,144]{1,2,0:T(8,128)(2,1)}), bf16[4,128,144]{1,2,0:T(8,128)(2,1)S(1)}, u32[]{:S(2)}, u32[]{:S(2)}) %all-to-all-start.1) | async-done | bytes 147488 | tf_op jit(solution)/shard_map/all_to_all | solution.py:61
  68.5 14.3 %all_to_all.40 = bf16[8,144,256]{2,1,0:T(8,128)(2,1)S(1)} all-to-all(bf16[8,144,256]{2,1,0:T(8,128)(2,1)S(1)} %fusion.16), channel_id=1, replica_groups=mesh['k'=2,'a'=2,'z'=16,'y'=4,'core'=2] {'k','a','core'}, dimensions={0} | all-to-all | bytes 1179648 | tf_op jit(solution)/shard_map/all_to_all | solution.py:390
  83.8 4.6 %all-to-all-start.3 = ((bf16[8,144,256]{2,1,0:T(8,128)(2,1)}), bf16[8,144,256]{2,1,0:T(8,128)(2,1)S(1)}, u32[]{:S(2)}, u32[]{:S(2)}) async-start(bf16[8,144,256]{2,1,0:T(8,128)(2,1)} %broadcast_in_dim.121), calls=%async_computation.3 | async-start | bytes 1179648 | tf_op jit(solution)/shard_map/all_to_all | solution.py:61
  88.4 4.2 %collective-permute-start.3 = (bf16[256,672]{0,1:T(8,128)(2,1)S(1)}, bf16[256,672]{0,1:T(8,128)(2,1)S(1)}, u32[]{:S(2)}, u32[]{:S(2)}) collective-permute-start(bf16[256,672]{0,1:T(8,128)(2,1)S(1)} %copy-done.22), channel_id=1, source_target_pairs={{0,0},{1,128},{128,1},{129,129},{2,2},{3,130},{130,3},{131,131},{4... | collective-permute-start | bytes 1032200 | tf_op jit(solution)/shard_map/ppermute | solution.py:34
  92.7 8.7 %collective-permute-done.3 = bf16[256,672]{0,1:T(8,128)(2,1)S(1)} collective-permute-done((bf16[256,672]{0,1:T(8,128)(2,1)S(1)}, bf16[256,672]{0,1:T(8,128)(2,1)S(1)}, u32[]{:S(2)}, u32[]{:S(2)}) %collective-permute-start.3) | collective-permute-done | bytes 344096 | tf_op jit(solution)/shard_map/ppermute | solution.py:34
  102.2 30.0 %all_to_all.41.upper_ref = bf16[8,512,256]{2,1,0:T(8,128)(2,1)} all-to-all(bf16[8,512,256]{2,1,0:T(8,128)(2,1)S(1)} %broadcast_in_dim.122), channel_id=1, replica_groups=mesh['k'=2,'a'=2,'z'=16,'y'=4,'core'=2] {'y','a'}, dimensions={0} | all-to-all | bytes 4194304 | tf_op jit(solution)/shard_map/all_to_all | solution.py:61
  132.3 3.6 %collective-permute-start.4 = (bf16[16,2,144,512]{3,2,1,0:T(8,128)(2,1)}, bf16[16,2,144,512]{3,2,1,0:T(8,128)(2,1)}, u32[]{:S(2)}, u32[]{:S(2)}) collective-permute-start(bf16[16,2,144,512]{3,2,1,0:T(8,128)(2,1)} %bitcast.74), channel_id=1, source_target_pairs={{0,1},{1,0},{2,3},{3,2},{4,5},{5,4},{6,7},{7,6},{8,9},{9,8},{10,11... | collective-permute-start | bytes 14155784 | tf_op jit(solution)/shard_map/ppermute | solution.py:406
  138.1 3.5 %all-to-all-start.5 = ((bf16[8,160,256]{2,1,0:T(8,128)(2,1)}), bf16[8,160,256]{2,1,0:T(8,128)(2,1)S(1)}, u32[]{:S(2)}, u32[]{:S(2)}) async-start(bf16[8,160,256]{2,1,0:T(8,128)(2,1)} %broadcast_in_dim.198), calls=%async_computation.5 | async-start | bytes 1310720 | tf_op jit(solution)/shard_map/all_to_all | solution.py:61
  141.6 3.2 %reshape.348.gain_ref = f32[8,672,1]{2,1,0:T(8,128)S(1)} reshape(f32[5376]{0:T(1024)} %param.20) | data formatting | bytes 43008 | tf_op jit(solution)/shard_map/reshape | solution.py:411
  147.4 5.9 %all-to-all-done.5.lower_ref = bf16[8,160,256]{2,1,0:T(8,128)(2,1)S(1)} async-done(((bf16[8,160,256]{2,1,0:T(8,128)(2,1)}), bf16[8,160,256]{2,1,0:T(8,128)(2,1)S(1)}, u32[]{:S(2)}, u32[]{:S(2)}) %all-to-all-start.5) | async-done | bytes 655392 | tf_op jit(solution)/shard_map/all_to_all | solution.py:61
  153.3 2.3 copy-done
  157.2 2.7 %shard_map.136 = (f32[256,512]{1,0:T(8,128)S(1)}, f32[1,256]{1,0:T(1,128)S(1)}) custom-call(s32[1]{0:T(128)} %bitcast.core_ref, bf16[8,512,256]{2,1,0:T(8,128)(2,1)S(1)} %copy-done.2, bf16[8,160,256]{2,1,0:T(8,128)(2,1)S(1)} %all-to-all-done.5.lower_ref, f32[8,672,1]{2,1,0:T(8,128)S(1)} %reshape.348.gain_ref, bf16[16,2,144,512]{3,2,1,0:T(8,128)(2,1)S(1)} %bitcast.75), custom_call_target="tpu_custom_call" | custom-call | flops 704643072 | bytes 5242880 | tf_op jit(solution)/shard_map/pallas_call | solution.py:184
  160.0 4.7 %shard_map.137 = (bf16[256,256]{1,0:T(8,128)(2,1)S(1)}, bf16[256,256]{1,0:T(8,128)(2,1)S(1)}) custom-call(s32[1]{0:T(128)} %bitcast.core_ref, bf16[8,512,256]{2,1,0:T(8,128)(2,1)S(1)} %copy-done.2, bf16[8,160,256]{2,1,0:T(8,128)(2,1)S(1)} %all-to-all-done.5.lower_ref, f32[8,672,1]{2,1,0:T(8,128)S(1)} %reshape.348.gain_ref, ...), custom_call_target="tpu_custom_call" | custom-call | flops 704643072 | bytes 5242880 | tf_op jit(solution)/shard_map/pallas_call | solution.py:210
  164.7 2.5 %collective-permute-start.5 = (bf16[256,256]{1,0:T(8,128)(2,1)S(1)}, bf16[256,256]{1,0:T(8,128)(2,1)S(1)}, u32[]{:S(2)}, u32[]{:S(2)}) collective-permute-start(bf16[256,256]{1,0:T(8,128)(2,1)S(1)} %get-tuple-element.19), channel_id=1, source_target_pairs={{0,16},{8,24},{16,32},{24,40},{32,48},{40,56},{48,64},{56,72},{64,... | collective-permute-start | bytes 393224 | tf_op jit(solution)/shard_map/ppermute | solution.py:56
  167.2 3.0 %collective-permute-start.6 = (bf16[256,256]{1,0:T(8,128)(2,1)S(1)}, bf16[256,256]{1,0:T(8,128)(2,1)S(1)}, u32[]{:S(2)}, u32[]{:S(2)}) collective-permute-start(bf16[256,256]{1,0:T(8,128)(2,1)S(1)} %get-tuple-element.19), channel_id=1, source_target_pairs={{0,8},{8,16},{16,24},{24,32},{32,40},{40,48},{48,56},{56,64},{64,7... | collective-permute-start | bytes 393224 | tf_op jit(solution)/shard_map/ppermute | solution.py:56
  170.3 2.9 %collective-permute-done.5 = bf16[256,256]{1,0:T(8,128)(2,1)S(1)} collective-permute-done((bf16[256,256]{1,0:T(8,128)(2,1)S(1)}, bf16[256,256]{1,0:T(8,128)(2,1)S(1)}, u32[]{:S(2)}, u32[]{:S(2)}) %collective-permute-start.5) | collective-permute-done | bytes 131104 | tf_op jit(solution)/shard_map/ppermute | solution.py:56
  173.3 6.8 %collective-permute-done.6 = bf16[256,256]{1,0:T(8,128)(2,1)S(1)} collective-permute-done((bf16[256,256]{1,0:T(8,128)(2,1)S(1)}, bf16[256,256]{1,0:T(8,128)(2,1)S(1)}, u32[]{:S(2)}, u32[]{:S(2)}) %collective-permute-start.6) | collective-permute-done | bytes 131104 | tf_op jit(solution)/shard_map/ppermute | solution.py:56
  183.4 2.9 %collective-permute-start.8 = (bf16[256,256]{1,0:T(8,128)(2,1)S(1)}, bf16[256,256]{1,0:T(8,128)(2,1)S(1)}, u32[]{:S(2)}, u32[]{:S(2)}) collective-permute-start(bf16[256,256]{1,0:T(8,128)(2,1)S(1)} %get-tuple-element.19), channel_id=1, source_target_pairs={{8,0},{16,8},{24,16},{32,24},{40,32},{48,40},{56,48},{64,56},{72,6... | collective-permute-start | bytes 393224 | tf_op jit(solution)/shard_map/ppermute | solution.py:56
  186.4 6.2 %collective-permute-done.7 = bf16[512,256]{1,0:T(8,128)(2,1)S(1)} collective-permute-done((bf16[512,256]{1,0:T(8,128)(2,1)S(1)}, bf16[512,256]{1,0:T(8,128)(2,1)S(1)}, u32[]{:S(2)}, u32[]{:S(2)}) %collective-permute-start.7) | collective-permute-done | bytes 262176 | tf_op jit(solution)/shard_map/ppermute | solution.py:56
  195.5 3.7 %all-to-all-start.6 = ((bf16[8,256,256]{2,1,0:T(8,128)(2,1)}), bf16[8,256,256]{2,1,0:T(8,128)(2,1)S(1)}, u32[]{:S(2)}, u32[]{:S(2)}) async-start(bf16[8,256,256]{2,1,0:T(8,128)(2,1)} %broadcast_in_dim.205), calls=%async_computation.6 | async-start | bytes 2097152 | tf_op jit(solution)/shard_map/all_to_all | solution.py:61
  199.2 3.4 %collective-permute-start.9 = (bf16[672,256]{1,0:T(8,128)(2,1)S(1)}, bf16[672,256]{1,0:T(8,128)(2,1)S(1)}, u32[]{:S(2)}, u32[]{:S(2)}) collective-permute-start(bf16[672,256]{1,0:T(8,128)(2,1)S(1)} %copy-done.8), channel_id=1, source_target_pairs={{0,0},{1,128},{128,1},{129,129},{2,2},{3,130},{130,3},{131,131},{4... | collective-permute-start | bytes 1032200 | tf_op jit(solution)/shard_map/ppermute | solution.py:34
  202.6 12.4 %all-to-all-done.6.own_ref.other_ref = bf16[8,256,256]{2,1,0:T(8,128)(2,1)S(1)} async-done(((bf16[8,256,256]{2,1,0:T(8,128)(2,1)}), bf16[8,256,256]{2,1,0:T(8,128)(2,1)S(1)}, u32[]{:S(2)}, u32[]{:S(2)}) %all-to-all-start.6) | async-done | bytes 1048608 | tf_op jit(solution)/shard_map/all_to_all | solution.py:61
  215.0 2.3 copy-done.1
  217.3 3.6 %shard_map.138 = (f32[672,256]{1,0:T(8,128)S(1)}, f32[1,256]{1,0:T(1,128)S(1)}) custom-call(s32[1]{0:T(128)} %bitcast.core_ref, bf16[8,256,256]{2,1,0:T(8,128)(2,1)S(1)} %all-to-all-done.6.own_ref.other_ref, bf16[8,256,256]{2,1,0:T(8,128)(2,1)S(1)} %all-to-all-done.6.own_ref.other_ref, bf16[16,2,144,512]{3,2,1,0:T(8,128)(2,1)S(1)} %bitcast.76, ...), custom_call_target="tpu_custom_call" | custom-call | flops 805306368 | bytes 5242880 | tf_op jit(solution)/shard_map/pallas_call | solution.py:278
  221.0 3.1 %collective-permute-start.10 = (bf16[672,256]{1,0:T(8,128)(2,1)S(1)}, bf16[672,256]{1,0:T(8,128)(2,1)S(1)}, u32[]{:S(2)}, u32[]{:S(2)}) collective-permute-start(bf16[672,256]{1,0:T(8,128)(2,1)S(1)} %convert_element_type.61), channel_id=1, source_target_pairs={{0,0},{1,128},{128,1},{129,129},{2,2},{3,130},{130,3},{131,131},{4... | collective-permute-start | bytes 1032200 | tf_op jit(solution)/shard_map/ppermute | solution.py:34
  224.8 3.4 %all-to-all-start.7 = ((f32[16,1,256]{2,1,0:T(1,128)}), f32[16,1,256]{2,1,0:T(1,128)S(1)}, u32[]{:S(2)}, u32[]{:S(2)}) async-start(f32[16,1,256]{2,1,0:T(1,128)} %broadcast_in_dim.210), calls=%async_computation.7 | async-start | bytes 32768 | tf_op jit(solution)/shard_map/all_to_all | solution.py:61
  228.3 5.4 %all-to-all-done.7 = f32[16,1,256]{2,1,0:T(1,128)S(1)} async-done(((f32[16,1,256]{2,1,0:T(1,128)}), f32[16,1,256]{2,1,0:T(1,128)S(1)}, u32[]{:S(2)}, u32[]{:S(2)}) %all-to-all-start.7) | async-done | bytes 16416 | tf_op jit(solution)/shard_map/all_to_all | solution.py:61
  (128 shorter events, 29.1 us)
Async XLA Ops:
  6.5 15.5 %copy-start.6 = (bf16[8,64,1152]{2,1,0:T(8,128)(2,1)S(1)}, bf16[8,64,1152]{2,1,0:T(8,128)(2,1)}, u32[]{:S(2)}) copy-start(bf16[8,64,1152]{2,1,0:T(8,128)(2,1)} %param.15) | copy-start | bytes 3538948
  6.5 125.7 %all-gather.3.cloned.1.call-start = ((), (), s32[]{:S(2)}) async-start(), calls=%async_computation.8 | async-start | bytes 5013504 | tf_op jit(solution)/shard_map/all_gather | solution.py:349
  9.0 8.0 %collective-permute-start = (bf16[144,512]{1,0:T(8,128)(2,1)S(1)}, bf16[144,512]{1,0:T(8,128)(2,1)S(1)}, u32[]{:S(2)}, u32[]{:S(2)}) collective-permute-start(bf16[144,512]{1,0:T(8,128)(2,1)S(1)} %maximum_maximum_fusion), channel_id=1, source_target_pairs={{0,0},{1,128},{128,1},{129,129},{256,256},{257,384},{384,257},{385... | collective-permute-start | bytes 442376 | tf_op jit(solution)/shard_map/ppermute | solution.py:43
  13.5 7.7 %collective-permute-start.1 = (bf16[144,512]{1,0:T(8,128)(2,1)S(1)}, bf16[144,512]{1,0:T(8,128)(2,1)S(1)}, u32[]{:S(2)}, u32[]{:S(2)}) collective-permute-start(bf16[144,512]{1,0:T(8,128)(2,1)S(1)} %maximum_maximum_fusion), channel_id=1, source_target_pairs={{0,256},{1,384},{128,257},{129,385},{256,0},{257,128},{384,1},{385... | collective-permute-start | bytes 442376 | tf_op jit(solution)/shard_map/ppermute | solution.py:43
  22.0 11.3 %copy-start.11 = (s32[8]{0:T(128)S(1)}, s32[8]{0:T(128)}, u32[]{:S(2)}) copy-start(s32[8]{0:T(128)} %param.16) | copy-start | bytes 100
  22.0 11.3 %copy-start.21 = (s32[8]{0:T(128)S(1)}, s32[8]{0:T(128)}, u32[]{:S(2)}) copy-start(s32[8]{0:T(128)} %param.17) | copy-start | bytes 100
  24.9 10.7 %all-to-all-start = ((bf16[4,32,144]{2,1,0:T(8,128)(2,1)}), bf16[4,32,144]{2,1,0:T(8,128)(2,1)S(1)}, u32[]{:S(2)}, u32[]{:S(2)}) async-start(bf16[4,32,144]{2,1,0:T(8,128)(2,1)} %broadcast_in_dim.114), calls=%async_computation | async-start | bytes 131072 | tf_op jit(solution)/shard_map/all_to_all | solution.py:61
  31.0 70.4 %collective-permute-start.2 = (bf16[1152,672]{0,1:T(8,128)(2,1)}, bf16[1152,672]{0,1:T(8,128)(2,1)S(1)}, u32[]{:S(2)}, u32[]{:S(2)}) collective-permute-start(bf16[1152,672]{0,1:T(8,128)(2,1)} %param.19), channel_id=1, source_target_pairs={{0,0},{1,128},{128,1},{129,129},{2,2},{3,130},{130,3},{131,131},{4... | collective-permute-start | bytes 4644872 | tf_op jit(solution)/shard_map/ppermute | solution.py:34
  33.4 59.2 %copy-start.13 = (s32[8]{0:T(128)}, s32[8]{0:T(128)S(1)}, u32[]{:S(2)}) copy-start(s32[8]{0:T(128)S(1)} %get-tuple-element.33) | copy-start | bytes 100
  33.4 59.2 %copy-start.15 = (s32[8]{0:T(128)}, s32[8]{0:T(128)S(1)}, u32[]{:S(2)}) copy-start(s32[8]{0:T(128)S(1)} %get-tuple-element.36) | copy-start | bytes 100
  36.4 30.7 %all-to-all-start.1 = ((bf16[4,128,144]{1,2,0:T(8,128)(2,1)}), bf16[4,128,144]{1,2,0:T(8,128)(2,1)S(1)}, u32[]{:S(2)}, u32[]{:S(2)}) async-start(bf16[4,128,144]{1,2,0:T(8,128)(2,1)} %broadcast_in_dim.116), calls=%async_computation.1 | async-start | bytes 294912 | tf_op jit(solution)/shard_map/all_to_all | solution.py:61
  67.2 21.2 %copy-start.22 = (bf16[256,672]{0,1:T(8,128)(2,1)S(1)}, bf16[256,672]{0,1:T(8,128)(2,1)}, u32[]{:S(2)}) copy-start(bf16[256,672]{0,1:T(8,128)(2,1)} %param.14) | copy-start | bytes 1032196
  83.8 17.6 %all-to-all-start.3 = ((bf16[8,144,256]{2,1,0:T(8,128)(2,1)}), bf16[8,144,256]{2,1,0:T(8,128)(2,1)S(1)}, u32[]{:S(2)}, u32[]{:S(2)}) async-start(bf16[8,144,256]{2,1,0:T(8,128)(2,1)} %broadcast_in_dim.121), calls=%async_computation.3 | async-start | bytes 1179648 | tf_op jit(solution)/shard_map/all_to_all | solution.py:61
  88.4 13.0 %collective-permute-start.3 = (bf16[256,672]{0,1:T(8,128)(2,1)S(1)}, bf16[256,672]{0,1:T(8,128)(2,1)S(1)}, u32[]{:S(2)}, u32[]{:S(2)}) collective-permute-start(bf16[256,672]{0,1:T(8,128)(2,1)S(1)} %copy-done.22), channel_id=1, source_target_pairs={{0,0},{1,128},{128,1},{129,129},{2,2},{3,130},{130,3},{131,131},{4... | collective-permute-start | bytes 1032200 | tf_op jit(solution)/shard_map/ppermute | solution.py:34
  92.7 9.5 %copy-start.19 = (pred[256]{0:T(512)(128)(4,1)}, pred[256]{0:T(512)(128)(4,1)S(1)}, u32[]{:S(2)}) copy-start(pred[256]{0:T(512)(128)(4,1)S(1)} %broadcast_compare_fusion.1) | copy-start | bytes 772
  102.0 35.1 %copy-start.7 = (bf16[672,256]{1,0:T(8,128)(2,1)}, bf16[672,256]{1,0:T(8,128)(2,1)S(1)}, u32[]{:S(2)}) copy-start(bf16[672,256]{1,0:T(8,128)(2,1)S(1)} %fusion.20) | copy-start | bytes 1032196
  132.3 27.7 %collective-permute-start.4 = (bf16[16,2,144,512]{3,2,1,0:T(8,128)(2,1)}, bf16[16,2,144,512]{3,2,1,0:T(8,128)(2,1)}, u32[]{:S(2)}, u32[]{:S(2)}) collective-permute-start(bf16[16,2,144,512]{3,2,1,0:T(8,128)(2,1)} %bitcast.74), channel_id=1, source_target_pairs={{0,1},{1,0},{2,3},{3,2},{4,5},{5,4},{6,7},{7,6},{8,9},{9,8},{10,11... | collective-permute-start | bytes 14155784 | tf_op jit(solution)/shard_map/ppermute | solution.py:406
  137.2 9.5 %copy-start.12 = (s32[8]{0:T(128)S(1)}, s32[8]{0:T(128)}, u32[]{:S(2)}) copy-start(s32[8]{0:T(128)} %param.16) | copy-start | bytes 100
  137.2 9.5 %copy-start.14 = (s32[8]{0:T(128)S(1)}, s32[8]{0:T(128)}, u32[]{:S(2)}) copy-start(s32[8]{0:T(128)} %copy-done.13) | copy-start | bytes 100
  138.1 15.2 %all-to-all-start.5 = ((bf16[8,160,256]{2,1,0:T(8,128)(2,1)}), bf16[8,160,256]{2,1,0:T(8,128)(2,1)S(1)}, u32[]{:S(2)}, u32[]{:S(2)}) async-start(bf16[8,160,256]{2,1,0:T(8,128)(2,1)} %broadcast_in_dim.198), calls=%async_computation.5 | async-start | bytes 1310720 | tf_op jit(solution)/shard_map/all_to_all | solution.py:61
  160.0 10.3 %copy-start.18 = (s32[256]{0:T(256)S(1)}, s32[256]{0:T(256)}, u32[]{:S(2)}) copy-start(s32[256]{0:T(256)} %copy-done.17) | copy-start | bytes 3076
  160.0 22.0 %copy-start.10 = (s32[256]{0:T(256)S(1)}, s32[256]{0:T(256)}, u32[]{:S(2)}) copy-start(s32[256]{0:T(256)} %copy-done.9) | copy-start | bytes 3076
  160.0 22.0 %copy-start.20 = (pred[256]{0:T(512)(128)(4,1)S(1)}, pred[256]{0:T(512)(128)(4,1)}, u32[]{:S(2)}) copy-start(pred[256]{0:T(512)(128)(4,1)} %copy-done.19) | copy-start | bytes 772
  164.7 8.6 %collective-permute-start.5 = (bf16[256,256]{1,0:T(8,128)(2,1)S(1)}, bf16[256,256]{1,0:T(8,128)(2,1)S(1)}, u32[]{:S(2)}, u32[]{:S(2)}) collective-permute-start(bf16[256,256]{1,0:T(8,128)(2,1)S(1)} %get-tuple-element.19), channel_id=1, source_target_pairs={{0,16},{8,24},{16,32},{24,40},{32,48},{40,56},{48,64},{56,72},{64,... | collective-permute-start | bytes 393224 | tf_op jit(solution)/shard_map/ppermute | solution.py:56
  167.2 12.8 %collective-permute-start.6 = (bf16[256,256]{1,0:T(8,128)(2,1)S(1)}, bf16[256,256]{1,0:T(8,128)(2,1)S(1)}, u32[]{:S(2)}, u32[]{:S(2)}) collective-permute-start(bf16[256,256]{1,0:T(8,128)(2,1)S(1)} %get-tuple-element.19), channel_id=1, source_target_pairs={{0,8},{8,16},{16,24},{24,32},{32,40},{40,48},{48,56},{56,64},{64,7... | collective-permute-start | bytes 393224 | tf_op jit(solution)/shard_map/ppermute | solution.py:56
  180.1 12.5 %collective-permute-start.7 = (bf16[512,256]{1,0:T(8,128)(2,1)S(1)}, bf16[512,256]{1,0:T(8,128)(2,1)S(1)}, u32[]{:S(2)}, u32[]{:S(2)}) collective-permute-start(bf16[512,256]{1,0:T(8,128)(2,1)S(1)} %pad_maximum_fusion.1), channel_id=1, source_target_pairs={{0,16},{8,24},{16,32},{24,40},{32,48},{40,56},{48,64},{56,72},{64,... | collective-permute-start | bytes 786440 | tf_op jit(solution)/shard_map/ppermute | solution.py:56
  183.4 9.2 %collective-permute-start.8 = (bf16[256,256]{1,0:T(8,128)(2,1)S(1)}, bf16[256,256]{1,0:T(8,128)(2,1)S(1)}, u32[]{:S(2)}, u32[]{:S(2)}) collective-permute-start(bf16[256,256]{1,0:T(8,128)(2,1)S(1)} %get-tuple-element.19), channel_id=1, source_target_pairs={{8,0},{16,8},{24,16},{32,24},{40,32},{48,40},{56,48},{64,56},{72,6... | collective-permute-start | bytes 393224 | tf_op jit(solution)/shard_map/ppermute | solution.py:56
  195.4 38.4 %copy-start.16 = (f32[672]{0:T(1024)S(1)}, f32[672]{0:T(1024)}, u32[]{:S(2)}) copy-start(f32[672]{0:T(1024)} %param.27) | copy-start | bytes 8068
  195.5 19.6 %all-to-all-start.6 = ((bf16[8,256,256]{2,1,0:T(8,128)(2,1)}), bf16[8,256,256]{2,1,0:T(8,128)(2,1)S(1)}, u32[]{:S(2)}, u32[]{:S(2)}) async-start(bf16[8,256,256]{2,1,0:T(8,128)(2,1)} %broadcast_in_dim.205), calls=%async_computation.6 | async-start | bytes 2097152 | tf_op jit(solution)/shard_map/all_to_all | solution.py:61
  199.2 34.6 %collective-permute-start.9 = (bf16[672,256]{1,0:T(8,128)(2,1)S(1)}, bf16[672,256]{1,0:T(8,128)(2,1)S(1)}, u32[]{:S(2)}, u32[]{:S(2)}) collective-permute-start(bf16[672,256]{1,0:T(8,128)(2,1)S(1)} %copy-done.8), channel_id=1, source_target_pairs={{0,0},{1,128},{128,1},{129,129},{2,2},{3,130},{130,3},{131,131},{4... | collective-permute-start | bytes 1032200 | tf_op jit(solution)/shard_map/ppermute | solution.py:34
  221.0 12.8 %collective-permute-start.10 = (bf16[672,256]{1,0:T(8,128)(2,1)S(1)}, bf16[672,256]{1,0:T(8,128)(2,1)S(1)}, u32[]{:S(2)}, u32[]{:S(2)}) collective-permute-start(bf16[672,256]{1,0:T(8,128)(2,1)S(1)} %convert_element_type.61), channel_id=1, source_target_pairs={{0,0},{1,128},{128,1},{129,129},{2,2},{3,130},{130,3},{131,131},{4... | collective-permute-start | bytes 1032200 | tf_op jit(solution)/shard_map/ppermute | solution.py:34
  224.8 8.9 %all-to-all-start.7 = ((f32[16,1,256]{2,1,0:T(1,128)}), f32[16,1,256]{2,1,0:T(1,128)S(1)}, u32[]{:S(2)}, u32[]{:S(2)}) async-start(f32[16,1,256]{2,1,0:T(1,128)} %broadcast_in_dim.210), calls=%async_computation.7 | async-start | bytes 32768 | tf_op jit(solution)/shard_map/all_to_all | solution.py:61
  (9 other events, 37.6 us)
Sparse Core Ops, SparseCore 0:
  22.1 82.2 all-gather.2

commit v4 on v3

--- a/solution.py
+++ b/solution.py
@@ -19,6 +19,7 @@
 PAD_ALL = 144
 WIDTH = 672
 UPPER = 512
+VMEM = 56 * 2**20
 
 EPSILON = 1e-06
 QUERY_SCALE = 168.0 ** (-0.5)
@@ -194,7 +195,7 @@
             jax.ShapeDtypeStruct((rows, 512), jnp.float32),
             jax.ShapeDtypeStruct((1, rows), jnp.float32),
         ],
-        compiler_params=pltpu.CompilerParams(vmem_limit_bytes=24 * 2**20),
+        compiler_params=pltpu.CompilerParams(vmem_limit_bytes=VMEM),
         cost_estimate=pl.CostEstimate(
             flops=rows * 512 * D, bytes_accessed=5 * 2**20, transcendentals=0
         ),
@@ -232,7 +233,7 @@
             jax.ShapeDtypeStruct((rows, 256), jnp.bfloat16),
             jax.ShapeDtypeStruct((rows, 256), jnp.bfloat16),
         ],
-        compiler_params=pltpu.CompilerParams(vmem_limit_bytes=24 * 2**20),
+        compiler_params=pltpu.CompilerParams(vmem_limit_bytes=VMEM),
         cost_estimate=pl.CostEstimate(
             flops=rows * 512 * D, bytes_accessed=5 * 2**20, transcendentals=0
         ),
@@ -293,7 +294,7 @@
             jax.ShapeDtypeStruct((WIDTH, rows), jnp.float32),
             jax.ShapeDtypeStruct((1, rows), jnp.float32),
         ],
-        compiler_params=pltpu.CompilerParams(vmem_limit_bytes=24 * 2**20),
+        compiler_params=pltpu.CompilerParams(vmem_limit_bytes=VMEM),
         cost_estimate=pl.CostEstimate(
             flops=2 * rows * 768 * 2048, bytes_accessed=5 * 2**20, transcendentals=0
         ),
@@ -339,14 +340,6 @@
     )
     same_half = from_half(local, 0)
     other_half = from_half(local, 1)
-    k_first = lax.axis_index("k") == 0
-    both = jnp.stack(
-        [
-            jnp.where(k_first, same_half, other_half),
-            jnp.where(k_first, other_half, same_half),
-        ]
-    )
-    along = lax.all_gather(both, "z", axis=0)
     core = core_index.astype(jnp.int32)[None]
 
     image_count = starts.shape[0]
@@ -360,17 +353,21 @@
         POOL * POOL
     )
     soft = rms_scale(pooled, soft_gain).astype(jnp.bfloat16)
-    vis_part = vis // head_count
-    soft_part = lax.dynamic_slice_in_dim(
-        soft, lax.axis_index(GIVEN_HEAD) * vis_part, vis_part, 1
-    )
-    near_groups = [[4 * i + j for j in range(4)] for i in range(Z // 4)]
-    far_groups = [[4 * i + j for i in range(Z // 4)] for j in range(4)]
-    soft_z = exchange(soft_part, "z", 4, near_groups).reshape(4 * block_rows, vis_part)
-    soft_z = exchange(soft_z, "z", 4, far_groups).reshape(Z * block_rows, vis_part)
-    target = jnp.arange(8, dtype=jnp.int32)
-    target_k, target_a, target_core = target // 4, target // 2 % 2, target % 2
-    target_seq = (target_k * 2 + target_core) * Z + z_index
+    vis_part = vis // 4
+    soft, same_half, other_half = lax.optimization_barrier((soft, same_half, other_half))
+    k_first = lax.axis_index("k") == 0
+    both = jnp.stack(
+        [
+            jnp.where(k_first, same_half, other_half),
+            jnp.where(k_first, other_half, same_half),
+        ]
+    )
+    along = lax.all_gather(both, "z", axis=0)
+    soft_part = lax.dynamic_slice_in_dim(soft, lax.axis_index("y") * vis_part, vis_part, 1)
+    soft_z = exchange(soft_part, "z", Z).reshape(Z * block_rows, vis_part)
+    soft_z, proj_weight, tokens = lax.optimization_barrier((soft_z, proj_weight, tokens))
+    target = jnp.arange(x_count, dtype=jnp.int32)
+    target_seq = (target // 2 * 2 + core_index) * Z + z_index
     frame_pos = (
         target_seq[:, None] * tok_rows + jnp.arange(tok_rows, dtype=jnp.int32)[None, :]
     ).reshape(-1)
@@ -380,18 +377,15 @@
     frame_row = jnp.sum(
         jnp.where(frame_image[:, None] == image_ids[None, :], row_base[None, :], 0), axis=1
     )
-    wanted = (frame_image >= 0) & jnp.repeat(target_a == core_index, tok_rows)
-    frame_row = jnp.where(wanted, frame_row + frame_pos, -1)
+    frame_row = jnp.where(frame_image >= 0, frame_row + frame_pos, -1)
     x_index = lax.axis_index(("k", "a"))
     here = x_index * (Z * block_rows) + jnp.arange(Z * block_rows, dtype=jnp.int32)
     chosen = (frame_row[:, None] == here[None, :]).astype(jnp.bfloat16)
-    chosen = chosen.reshape(8, tok_rows, Z * block_rows)
+    chosen = chosen.reshape(x_count, tok_rows, Z * block_rows)
     frames = jnp.einsum("sk,xps->xkp", soft_z, chosen, preferred_element_type=jnp.float32)
-    frames = lax.all_to_all(
-        frames.astype(jnp.bfloat16), ("k", "a", "core"), 0, 0, tiled=True
-    )
+    frames = lax.all_to_all(frames.astype(jnp.bfloat16), ("k", "a"), 0, 0, tiled=True)
     mine = jnp.sum(frames.astype(jnp.float32), axis=0).astype(jnp.bfloat16)
-    soft_rows = exchange(mine, HEAD, head_count).reshape(vis, tok_rows)
+    soft_rows = exchange(mine, "y", 4).reshape(vis, tok_rows)
     embedded = lax.dot_general(
         swapped(proj_weight), soft_rows, (((0,), (0,)), ((), ())),
         preferred_element_type=jnp.float32,
@@ -424,8 +418,11 @@
         key_gain,
     )
     past_count = WINDOW // tok_rows
+    own, residual = lax.optimization_barrier((own, residual))
+    given_residual = swapped(residual)
     near = jnp.concatenate([shifted(own, 2), shifted(own, 1)], axis=0)
     window = jnp.concatenate([shifted(near, 2), near, own, shifted(own, -1)], axis=0)
+    window, given_residual = lax.optimization_barrier((window, given_residual))
     key_pos = (seq_index - past_count) * tok_rows + jnp.arange(window.shape[0], dtype=jnp.int32)
     allowed = allowed_keys(my_pos, key_pos, starts, total_rows)
     attended = attend(
@@ -435,16 +432,14 @@
         allowed,
     )
     attended = attended.reshape(tok_rows, 2 * HEAD_DIM).T
-    attended, residual = lax.optimization_barrier((attended, residual))
     heads_all = exchange(attended, HEAD, head_count)
     projected, squares = project_out(core, heads_all, along, across)
-    given_residual = swapped(residual).astype(jnp.float32)
     given = swapped(projected.astype(jnp.bfloat16)).astype(jnp.float32)
     all_squares = exchange(squares, ("a", "y", "core"), 16).reshape(8, 2, tok_rows)
     from_core = jnp.arange(2, dtype=jnp.int32) == lax.axis_index("a")
     squares = jnp.sum(jnp.where(from_core[None, :, None], all_squares, 0.0), axis=(0, 1))
     post = given * lax.rsqrt(squares[None, :] / D + EPSILON) * post_gain[:, None]
-    return (given_residual + post).astype(jnp.bfloat16).T
+    return (given_residual.astype(jnp.float32) + post).astype(jnp.bfloat16).T
 
 
 def solution(mesh):

time: 243 us -> 252 us (1.037)
  waiting for transfers between devices: 72.5 us -> 78.6 us
  Pallas kernels: 11.1 us -> 16.7 us
  blocking collectives: 44.3 us -> 48.9 us
  starting transfers between devices: 68.8 us -> 64.7 us
  local copies, waits for them, and re-layouts: 17.9 us -> 14.3 us
    all_to_all x1 -> x2, blocking collectives: 30 us -> 48.9 us  [exchange(): lax.all_to_all(spread, axes, 0, 0, tiled=True, axis_index_groups=groups)]
    all_to_all x0 -> x1, waiting for transfers between devices: none -> 17.6 us  [body(): lax.all_to_all(frames.astype(jnp.bfloat16), ('k', 'a'), 0, 0, tiled=True)]
    all_to_all x1 -> x0, blocking collectives: 14.3 us -> none  [body(): lax.all_to_all(frames.astype(jnp.bfloat16), ('k', 'a', 'core'), 0, 0, til...]
    ppermute x4, waiting for transfers between devices: 8.68 us -> 0.49 us  [swapped(): return lax.ppermute(value, ('a', 'core'), [(0, 0), (1, 2), (2, 1), (3, 3)])]
    all_to_all x6 -> x4, starting transfers between devices: 33.8 us -> 27.1 us  [exchange(): lax.all_to_all(spread, axes, 0, 0, tiled=True, axis_index_groups=groups)]
    unnamed x51 -> x23, local copies, waits for them, and re-layouts: 6.42 us -> 1.86 us
    all_to_all x0 -> x1, starting transfers between devices: none -> 3.48 us  [body(): lax.all_to_all(frames.astype(jnp.bfloat16), ('k', 'a'), 0, 0, tiled=True)]
    ppermute x2, waiting for transfers between devices: 4.21 us -> 0.84 us  [from_half(): return lax.ppermute(value, ('k', 'a', 'core'), pairs)]
  transfers between devices with their start and end apart: 18 -> 17, of which waited for: 10 -> 10; matrix products, arithmetic and copies ran while one was open for 7% -> 8% of each run, Pallas kernels for 3% -> 2%
where the time goes in v4:
time: 252 us; the launch traced here: 251 us
  waiting for transfers between devices  78.6 us (31%)
  starting transfers between devices  64.7 us (26%)
  blocking collectives  48.9 us (19%)
  Pallas kernels  16.7 us (7%)
  local copies, waits for them, and re-layouts  14.3 us (6%)
  between operations  13.9 us (6%)
  other arithmetic  9.13 us (4%)
  matrix products  4.83 us (2%)
    all_to_all x2, blocking collectives, exchange(): lax.all_to_all(spread, axes, 0, 0, tiled=True, axis_index_groups=groups)  48.9 us
    all_to_all x4, waiting for transfers between devices, exchange(): lax.all_to_all(spread, axes, 0, 0, tiled=True, axis_index_groups=groups)  44.5 us
    all_to_all x4, starting transfers between devices, exchange(): lax.all_to_all(spread, axes, 0, 0, tiled=True, axis_index_groups=groups)  27.1 us
    all_to_all x1, waiting for transfers between devices, body(): lax.all_to_all(frames.astype(jnp.bfloat16), ('k', 'a'), 0, 0, tiled=True)  17.6 us
    ppermute x4, waiting for transfers between devices, shifted(): return lax.ppermute(value, ('k', 'z', 'core'), pairs)  15.2 us
    ppermute x4, starting transfers between devices, shifted(): return lax.ppermute(value, ('k', 'z', 'core'), pairs)  13.6 us
    ppermute x4, starting transfers between devices, swapped(): return lax.ppermute(value, ('a', 'core'), [(0, 0), (1, 2), (2, 1), (3, 3)])  9.91 us
    ppermute x2, starting transfers between devices, from_half(): return lax.ppermute(value, ('k', 'a', 'core'), pairs)  7.95 us
  transfers between devices with their start and end apart: 17, of which 10 were waited for; matrix products, arithmetic and copies ran while one was open for 8% of the time, Pallas kernels for 2%

profile of v4, /device:TPU:1, one launch (start us, length us, event | category | flops | bytes accessed | tf_op | source)
XLA Modules:
  0.0 251.0 jit_solution(3280086992263267946)
XLA Ops:
  8.9 4.5 %collective-permute-start = (bf16[144,512]{1,0:T(8,128)(2,1)S(1)}, bf16[144,512]{1,0:T(8,128)(2,1)S(1)}, u32[]{:S(2)}, u32[]{:S(2)}) collective-permute-start(bf16[144,512]{1,0:T(8,128)(2,1)S(1)} %maximum_maximum_fusion), channel_id=1, source_target_pairs={{0,0},{1,128},{128,1},{129,129},{256,256},{257,384},{384,257},{385... | collective-permute-start | bytes 442376 | tf_op jit(solution)/shard_map/ppermute | solution.py:44
  13.4 3.4 %collective-permute-start.1 = (bf16[144,512]{1,0:T(8,128)(2,1)S(1)}, bf16[144,512]{1,0:T(8,128)(2,1)S(1)}, u32[]{:S(2)}, u32[]{:S(2)}) collective-permute-start(bf16[144,512]{1,0:T(8,128)(2,1)S(1)} %maximum_maximum_fusion), channel_id=1, source_target_pairs={{0,256},{1,384},{128,257},{129,385},{256,0},{257,128},{384,1},{385... | collective-permute-start | bytes 442376 | tf_op jit(solution)/shard_map/ppermute | solution.py:44
  16.9 2.5 reshape.326
  22.8 15.4 %all-to-all-start = ((bf16[16,32,288]{2,1,0:T(8,128)(2,1)}), bf16[16,32,288]{2,1,0:T(8,128)(2,1)S(1)}, u32[]{:S(2)}, u32[]{:S(2)}) async-start(bf16[16,32,288]{2,1,0:T(8,128)(2,1)} %broadcast_in_dim.104), calls=%async_computation | async-start | bytes 786432 | tf_op jit(solution)/shard_map/all_to_all | solution.py:62
  38.4 23.5 %all-to-all-done = bf16[16,32,288]{2,1,0:T(8,128)(2,1)S(1)} async-done(((bf16[16,32,288]{2,1,0:T(8,128)(2,1)}), bf16[16,32,288]{2,1,0:T(8,128)(2,1)S(1)}, u32[]{:S(2)}, u32[]{:S(2)}) %all-to-all-start) | async-done | bytes 294944 | tf_op jit(solution)/shard_map/all_to_all | solution.py:62
  61.9 4.1 %collective-permute-start.2 = (bf16[1152,672]{0,1:T(8,128)(2,1)S(1)}, bf16[1152,672]{0,1:T(8,128)(2,1)}, u32[]{:S(2)}, u32[]{:S(2)}) collective-permute-start(bf16[1152,672]{0,1:T(8,128)(2,1)S(1)} %copy-done.7), channel_id=1, source_target_pairs={{0,0},{1,128},{128,1},{129,129},{2,2},{3,130},{130,3},{131,131},{4... | collective-permute-start | bytes 4644872 | tf_op jit(solution)/shard_map/ppermute | solution.py:35
  67.7 3.5 %all-to-all-start.1 = ((bf16[4,288,256]{2,1,0:T(8,128)(2,1)}), bf16[4,288,256]{2,1,0:T(8,128)(2,1)S(1)}, u32[]{:S(2)}, u32[]{:S(2)}) async-start(bf16[4,288,256]{2,1,0:T(8,128)(2,1)} %fusion.14), calls=%async_computation.1 | async-start | bytes 1179648 | tf_op jit(solution)/shard_map/all_to_all | solution.py:386
  71.2 1.9 collective-permute-start.3
  73.2 17.6 %all-to-all-done.1 = bf16[4,288,256]{2,1,0:T(8,128)(2,1)S(1)} async-done(((bf16[4,288,256]{2,1,0:T(8,128)(2,1)}), bf16[4,288,256]{2,1,0:T(8,128)(2,1)S(1)}, u32[]{:S(2)}, u32[]{:S(2)}) %all-to-all-start.1) | async-done | bytes 589856 | tf_op jit(solution)/shard_map/all_to_all | solution.py:386
  91.7 4.3 %all-to-all-start.2 = ((bf16[4,288,256]{2,1,0:T(8,128)(2,1)}), bf16[4,288,256]{2,1,0:T(8,128)(2,1)S(1)}, u32[]{:S(2)}, u32[]{:S(2)}) async-start(bf16[4,288,256]{2,1,0:T(8,128)(2,1)} %broadcast_in_dim.108), calls=%async_computation.2 | async-start | bytes 1179648 | tf_op jit(solution)/shard_map/all_to_all | solution.py:62
  96.1 9.4 %all-to-all-done.2 = bf16[4,288,256]{2,1,0:T(8,128)(2,1)S(1)} async-done(((bf16[4,288,256]{2,1,0:T(8,128)(2,1)}), bf16[4,288,256]{2,1,0:T(8,128)(2,1)S(1)}, u32[]{:S(2)}, u32[]{:S(2)}) %all-to-all-start.2) | async-done | bytes 589856 | tf_op jit(solution)/shard_map/all_to_all | solution.py:62
  105.6 2.0 fusion.17
  107.8 30.8 %all_to_all.35.upper_ref = bf16[8,512,256]{2,1,0:T(8,128)(2,1)} all-to-all(bf16[8,512,256]{2,1,0:T(8,128)(2,1)S(1)} %broadcast_in_dim.109), channel_id=1, replica_groups=mesh['k'=2,'a'=2,'z'=16,'y'=4,'core'=2] {'y','a'}, dimensions={0} | all-to-all | bytes 4194304 | tf_op jit(solution)/shard_map/all_to_all | solution.py:62
  138.5 2.6 %collective-permute-start.4 = (bf16[16,2,144,512]{3,2,1,0:T(8,128)(2,1)}, bf16[16,2,144,512]{3,2,1,0:T(8,128)(2,1)}, u32[]{:S(2)}, u32[]{:S(2)}) collective-permute-start(bf16[16,2,144,512]{3,2,1,0:T(8,128)(2,1)} %bitcast.79), channel_id=1, source_target_pairs={{0,1},{1,0},{2,3},{3,2},{4,5},{5,4},{6,7},{7,6},{8,9},{9,8},{10,11... | collective-permute-start | bytes 14155784 | tf_op jit(solution)/shard_map/ppermute | solution.py:400
  142.7 3.5 %all-to-all-start.4 = ((bf16[8,160,256]{2,1,0:T(8,128)(2,1)}), bf16[8,160,256]{2,1,0:T(8,128)(2,1)S(1)}, u32[]{:S(2)}, u32[]{:S(2)}) async-start(bf16[8,160,256]{2,1,0:T(8,128)(2,1)} %broadcast_in_dim.110), calls=%async_computation.4 | async-start | bytes 1310720 | tf_op jit(solution)/shard_map/all_to_all | solution.py:62
  146.2 4.1 %reshape.331.gain_ref = f32[8,672,1]{2,1,0:T(8,128)} reshape(f32[5376]{0:T(1024)S(1)} %copy-done.2) | data formatting | bytes 43008 | tf_op jit(solution)/shard_map/reshape | solution.py:405
  152.0 5.9 %all-to-all-done.4.lower_ref = bf16[8,160,256]{2,1,0:T(8,128)(2,1)S(1)} async-done(((bf16[8,160,256]{2,1,0:T(8,128)(2,1)}), bf16[8,160,256]{2,1,0:T(8,128)(2,1)S(1)}, u32[]{:S(2)}, u32[]{:S(2)}) %all-to-all-start.4) | async-done | bytes 655392 | tf_op jit(solution)/shard_map/all_to_all | solution.py:62
  158.7 5.6 %shard_map.136 = (f32[256,512]{1,0:T(8,128)}, f32[1,256]{1,0:T(1,128)}) custom-call(s32[1]{0:T(128)} %bitcast.core_ref, bf16[8,512,256]{2,1,0:T(8,128)(2,1)} %all_to_all.35.upper_ref, bf16[8,160,256]{2,1,0:T(8,128)(2,1)} %copy-done, f32[8,672,1]{2,1,0:T(8,128)} %reshape.331.gain_ref, bf16[16,2,144,512]{3,2,1,0:T(8,128)(2,1)} %bitcast.80), custom_call_target="tpu_custom_call" | custom-call | flops 704643072 | bytes 5242880 | tf_op jit(solution)/shard_map/pallas_call | solution.py:185
  164.3 6.2 %shard_map.137 = (bf16[256,256]{1,0:T(8,128)(2,1)}, bf16[256,256]{1,0:T(8,128)(2,1)}) custom-call(s32[1]{0:T(128)} %bitcast.core_ref, bf16[8,512,256]{2,1,0:T(8,128)(2,1)} %all_to_all.35.upper_ref, bf16[8,160,256]{2,1,0:T(8,128)(2,1)} %copy-done, f32[8,672,1]{2,1,0:T(8,128)} %reshape.331.gain_ref, ...), custom_call_target="tpu_custom_call" | custom-call | flops 704643072 | bytes 5242880 | tf_op jit(solution)/shard_map/pallas_call | solution.py:211
  170.5 4.2 %collective-permute-start.5 = (bf16[256,256]{1,0:T(8,128)(2,1)}, bf16[256,256]{1,0:T(8,128)(2,1)S(1)}, u32[]{:S(2)}, u32[]{:S(2)}) collective-permute-start(bf16[256,256]{1,0:T(8,128)(2,1)} %get-tuple-element.34), channel_id=1, source_target_pairs={{0,16},{8,24},{16,32},{24,40},{32,48},{40,56},{48,64},{56,72},{64,... | collective-permute-start | bytes 393224 | tf_op jit(solution)/shard_map/ppermute | solution.py:57
  174.7 3.7 %collective-permute-start.6 = (bf16[256,256]{1,0:T(8,128)(2,1)}, bf16[256,256]{1,0:T(8,128)(2,1)S(1)}, u32[]{:S(2)}, u32[]{:S(2)}) collective-permute-start(bf16[256,256]{1,0:T(8,128)(2,1)} %get-tuple-element.34), channel_id=1, source_target_pairs={{0,8},{8,16},{16,24},{24,32},{32,40},{40,48},{48,56},{56,64},{64,7... | collective-permute-start | bytes 393224 | tf_op jit(solution)/shard_map/ppermute | solution.py:57
  178.4 4.0 %collective-permute-done.5 = bf16[256,256]{1,0:T(8,128)(2,1)S(1)} collective-permute-done((bf16[256,256]{1,0:T(8,128)(2,1)}, bf16[256,256]{1,0:T(8,128)(2,1)S(1)}, u32[]{:S(2)}, u32[]{:S(2)}) %collective-permute-start.5) | collective-permute-done | bytes 131104 | tf_op jit(solution)/shard_map/ppermute | solution.py:57
  182.4 3.5 %collective-permute-done.6 = bf16[256,256]{1,0:T(8,128)(2,1)S(1)} collective-permute-done((bf16[256,256]{1,0:T(8,128)(2,1)}, bf16[256,256]{1,0:T(8,128)(2,1)S(1)}, u32[]{:S(2)}, u32[]{:S(2)}) %collective-permute-start.6) | collective-permute-done | bytes 131104 | tf_op jit(solution)/shard_map/ppermute | solution.py:57
  185.9 2.9 %collective-permute-start.7 = (bf16[512,256]{1,0:T(8,128)(2,1)S(1)}, bf16[512,256]{1,0:T(8,128)(2,1)S(1)}, u32[]{:S(2)}, u32[]{:S(2)}) collective-permute-start(bf16[512,256]{1,0:T(8,128)(2,1)S(1)} %pad_maximum_fusion.1), channel_id=1, source_target_pairs={{0,16},{8,24},{16,32},{24,40},{32,48},{40,56},{48,64},{56,72},{64,... | collective-permute-start | bytes 786440 | tf_op jit(solution)/shard_map/ppermute | solution.py:57
  190.2 2.8 %collective-permute-start.8 = (bf16[256,256]{1,0:T(8,128)(2,1)}, bf16[256,256]{1,0:T(8,128)(2,1)S(1)}, u32[]{:S(2)}, u32[]{:S(2)}) collective-permute-start(bf16[256,256]{1,0:T(8,128)(2,1)} %get-tuple-element.34), channel_id=1, source_target_pairs={{8,0},{16,8},{24,16},{32,24},{40,32},{48,40},{56,48},{64,56},{72,6... | collective-permute-start | bytes 393224 | tf_op jit(solution)/shard_map/ppermute | solution.py:57
  193.0 1.9 collective-permute-start.9
  194.9 7.7 %collective-permute-done.7 = bf16[512,256]{1,0:T(8,128)(2,1)S(1)} collective-permute-done((bf16[512,256]{1,0:T(8,128)(2,1)S(1)}, bf16[512,256]{1,0:T(8,128)(2,1)S(1)}, u32[]{:S(2)}, u32[]{:S(2)}) %collective-permute-start.7) | collective-permute-done | bytes 262176 | tf_op jit(solution)/shard_map/ppermute | solution.py:57
  205.9 18.1 %all_to_all.36.own_ref.other_ref = bf16[8,256,256]{2,1,0:T(8,128)(2,1)} all-to-all(bf16[8,256,256]{2,1,0:T(8,128)(2,1)S(1)} %broadcast_in_dim.192), channel_id=1, replica_groups=mesh['k'=2,'a'=2,'z'=16,'y'=4,'core'=2] {'y','a'}, dimensions={0} | all-to-all | bytes 2097152 | tf_op jit(solution)/shard_map/all_to_all | solution.py:62
  224.1 5.0 %shard_map.138 = (f32[672,256]{1,0:T(8,128)}, f32[1,256]{1,0:T(1,128)}) custom-call(s32[1]{0:T(128)} %bitcast.core_ref, bf16[8,256,256]{2,1,0:T(8,128)(2,1)} %all_to_all.36.own_ref.other_ref, bf16[8,256,256]{2,1,0:T(8,128)(2,1)} %all_to_all.36.own_ref.other_ref, bf16[16,2,144,512]{3,2,1,0:T(8,128)(2,1)} %bitcast.81, ...), custom_call_target="tpu_custom_call" | custom-call | flops 805306368 | bytes 5242880 | tf_op jit(solution)/shard_map/pallas_call | solution.py:279
  230.2 2.0 collective-permute-start.10
  233.4 3.9 %all-to-all-start.6 = ((f32[16,1,256]{2,1,0:T(1,128)}), f32[16,1,256]{2,1,0:T(1,128)S(1)}, u32[]{:S(2)}, u32[]{:S(2)}) async-start(f32[16,1,256]{2,1,0:T(1,128)} %broadcast_in_dim.197), calls=%async_computation.6 | async-start | bytes 32768 | tf_op jit(solution)/shard_map/all_to_all | solution.py:62
  237.4 5.7 %all-to-all-done.6 = f32[16,1,256]{2,1,0:T(1,128)S(1)} async-done(((f32[16,1,256]{2,1,0:T(1,128)}), f32[16,1,256]{2,1,0:T(1,128)S(1)}, u32[]{:S(2)}, u32[]{:S(2)}) %all-to-all-start.6) | async-done | bytes 16416 | tf_op jit(solution)/shard_map/all_to_all | solution.py:62
  (93 shorter events, 21.0 us)
Async XLA Ops:
  6.5 132.0 %all-gather.3.cloned.1.call-start = ((), (), s32[]{:S(2)}) async-start(), calls=%async_computation.7 | async-start | bytes 5013504 | tf_op jit(solution)/shard_map/all_gather | solution.py:365
  8.9 11.3 %collective-permute-start = (bf16[144,512]{1,0:T(8,128)(2,1)S(1)}, bf16[144,512]{1,0:T(8,128)(2,1)S(1)}, u32[]{:S(2)}, u32[]{:S(2)}) collective-permute-start(bf16[144,512]{1,0:T(8,128)(2,1)S(1)} %maximum_maximum_fusion), channel_id=1, source_target_pairs={{0,0},{1,128},{128,1},{129,129},{256,256},{257,384},{384,257},{385... | collective-permute-start | bytes 442376 | tf_op jit(solution)/shard_map/ppermute | solution.py:44
  13.4 7.7 %collective-permute-start.1 = (bf16[144,512]{1,0:T(8,128)(2,1)S(1)}, bf16[144,512]{1,0:T(8,128)(2,1)S(1)}, u32[]{:S(2)}, u32[]{:S(2)}) collective-permute-start(bf16[144,512]{1,0:T(8,128)(2,1)S(1)} %maximum_maximum_fusion), channel_id=1, source_target_pairs={{0,256},{1,384},{128,257},{129,385},{256,0},{257,128},{384,1},{385... | collective-permute-start | bytes 442376 | tf_op jit(solution)/shard_map/ppermute | solution.py:44
  19.3 0.8 copy-start.3
  19.9 18.3 %copy-start.4 = (s32[8]{0:T(128)S(1)}, s32[8]{0:T(128)}, u32[]{:S(2)}) copy-start(s32[8]{0:T(128)} %param.16) | copy-start | bytes 100
  19.9 18.3 %copy-start.6 = (s32[8]{0:T(128)S(1)}, s32[8]{0:T(128)}, u32[]{:S(2)}) copy-start(s32[8]{0:T(128)} %param.17) | copy-start | bytes 100
  21.1 40.8 %copy-start.7 = (bf16[1152,672]{0,1:T(8,128)(2,1)S(1)}, bf16[1152,672]{0,1:T(8,128)(2,1)}, u32[]{:S(2)}) copy-start(bf16[1152,672]{0,1:T(8,128)(2,1)} %param.19) | copy-start | bytes 4644868
  22.0 49.2 %copy-start.8 = (bf16[256,672]{0,1:T(8,128)(2,1)S(1)}, bf16[256,672]{0,1:T(8,128)(2,1)}, u32[]{:S(2)}) copy-start(bf16[256,672]{0,1:T(8,128)(2,1)} %param.14) | copy-start | bytes 1032196
  22.8 39.1 %all-to-all-start = ((bf16[16,32,288]{2,1,0:T(8,128)(2,1)}), bf16[16,32,288]{2,1,0:T(8,128)(2,1)S(1)}, u32[]{:S(2)}, u32[]{:S(2)}) async-start(bf16[16,32,288]{2,1,0:T(8,128)(2,1)} %broadcast_in_dim.104), calls=%async_computation | async-start | bytes 786432 | tf_op jit(solution)/shard_map/all_to_all | solution.py:62
  61.9 43.7 %collective-permute-start.2 = (bf16[1152,672]{0,1:T(8,128)(2,1)S(1)}, bf16[1152,672]{0,1:T(8,128)(2,1)}, u32[]{:S(2)}, u32[]{:S(2)}) collective-permute-start(bf16[1152,672]{0,1:T(8,128)(2,1)S(1)} %copy-done.7), channel_id=1, source_target_pairs={{0,0},{1,128},{128,1},{129,129},{2,2},{3,130},{130,3},{131,131},{4... | collective-permute-start | bytes 4644872 | tf_op jit(solution)/shard_map/ppermute | solution.py:35
  67.7 23.1 %all-to-all-start.1 = ((bf16[4,288,256]{2,1,0:T(8,128)(2,1)}), bf16[4,288,256]{2,1,0:T(8,128)(2,1)S(1)}, u32[]{:S(2)}, u32[]{:S(2)}) async-start(bf16[4,288,256]{2,1,0:T(8,128)(2,1)} %fusion.14), calls=%async_computation.1 | async-start | bytes 1179648 | tf_op jit(solution)/shard_map/all_to_all | solution.py:386
  71.2 24.9 %collective-permute-start.3 = (bf16[256,672]{0,1:T(8,128)(2,1)S(1)}, bf16[256,672]{0,1:T(8,128)(2,1)S(1)}, u32[]{:S(2)}, u32[]{:S(2)}) collective-permute-start(bf16[256,672]{0,1:T(8,128)(2,1)S(1)} %copy-done.8), channel_id=1, source_target_pairs={{0,0},{1,128},{128,1},{129,129},{2,2},{3,130},{130,3},{131,131},{4... | collective-permute-start | bytes 1032200 | tf_op jit(solution)/shard_map/ppermute | solution.py:35
  91.7 13.8 %all-to-all-start.2 = ((bf16[4,288,256]{2,1,0:T(8,128)(2,1)}), bf16[4,288,256]{2,1,0:T(8,128)(2,1)S(1)}, u32[]{:S(2)}, u32[]{:S(2)}) async-start(bf16[4,288,256]{2,1,0:T(8,128)(2,1)} %broadcast_in_dim.108), calls=%async_computation.2 | async-start | bytes 1179648 | tf_op jit(solution)/shard_map/all_to_all | solution.py:62
  138.5 7.7 %copy-start.2 = (f32[5376]{0:T(1024)S(1)}, f32[5376]{0:T(1024)}, u32[]{:S(2)}) copy-start(f32[5376]{0:T(1024)} %param.20) | copy-start | bytes 64516
  138.5 25.7 %collective-permute-start.4 = (bf16[16,2,144,512]{3,2,1,0:T(8,128)(2,1)}, bf16[16,2,144,512]{3,2,1,0:T(8,128)(2,1)}, u32[]{:S(2)}, u32[]{:S(2)}) collective-permute-start(bf16[16,2,144,512]{3,2,1,0:T(8,128)(2,1)} %bitcast.79), channel_id=1, source_target_pairs={{0,1},{1,0},{2,3},{3,2},{4,5},{5,4},{6,7},{7,6},{8,9},{9,8},{10,11... | collective-permute-start | bytes 14155784 | tf_op jit(solution)/shard_map/ppermute | solution.py:400
  142.7 15.2 %all-to-all-start.4 = ((bf16[8,160,256]{2,1,0:T(8,128)(2,1)}), bf16[8,160,256]{2,1,0:T(8,128)(2,1)S(1)}, u32[]{:S(2)}, u32[]{:S(2)}) async-start(bf16[8,160,256]{2,1,0:T(8,128)(2,1)} %broadcast_in_dim.110), calls=%async_computation.4 | async-start | bytes 1310720 | tf_op jit(solution)/shard_map/all_to_all | solution.py:62
  157.8 0.9 copy-start
  170.5 33.7 %copy-start.1 = (bf16[256,256]{1,0:T(8,128)(2,1)S(1)}, bf16[256,256]{1,0:T(8,128)(2,1)}, u32[]{:S(2)}) copy-start(bf16[256,256]{1,0:T(8,128)(2,1)} %get-tuple-element.38) | copy-start | bytes 393220
  170.5 12.0 %collective-permute-start.5 = (bf16[256,256]{1,0:T(8,128)(2,1)}, bf16[256,256]{1,0:T(8,128)(2,1)S(1)}, u32[]{:S(2)}, u32[]{:S(2)}) collective-permute-start(bf16[256,256]{1,0:T(8,128)(2,1)} %get-tuple-element.34), channel_id=1, source_target_pairs={{0,16},{8,24},{16,32},{24,40},{32,48},{40,56},{48,64},{56,72},{64,... | collective-permute-start | bytes 393224 | tf_op jit(solution)/shard_map/ppermute | solution.py:57
  174.7 11.2 %collective-permute-start.6 = (bf16[256,256]{1,0:T(8,128)(2,1)}, bf16[256,256]{1,0:T(8,128)(2,1)S(1)}, u32[]{:S(2)}, u32[]{:S(2)}) collective-permute-start(bf16[256,256]{1,0:T(8,128)(2,1)} %get-tuple-element.34), channel_id=1, source_target_pairs={{0,8},{8,16},{16,24},{24,32},{32,40},{40,48},{48,56},{56,64},{64,7... | collective-permute-start | bytes 393224 | tf_op jit(solution)/shard_map/ppermute | solution.py:57
  185.9 16.8 %collective-permute-start.7 = (bf16[512,256]{1,0:T(8,128)(2,1)S(1)}, bf16[512,256]{1,0:T(8,128)(2,1)S(1)}, u32[]{:S(2)}, u32[]{:S(2)}) collective-permute-start(bf16[512,256]{1,0:T(8,128)(2,1)S(1)} %pad_maximum_fusion.1), channel_id=1, source_target_pairs={{0,16},{8,24},{16,32},{24,40},{32,48},{40,56},{48,64},{56,72},{64,... | collective-permute-start | bytes 786440 | tf_op jit(solution)/shard_map/ppermute | solution.py:57
  190.2 13.4 %collective-permute-start.8 = (bf16[256,256]{1,0:T(8,128)(2,1)}, bf16[256,256]{1,0:T(8,128)(2,1)S(1)}, u32[]{:S(2)}, u32[]{:S(2)}) collective-permute-start(bf16[256,256]{1,0:T(8,128)(2,1)} %get-tuple-element.34), channel_id=1, source_target_pairs={{8,0},{16,8},{24,16},{32,24},{40,32},{48,40},{56,48},{64,56},{72,6... | collective-permute-start | bytes 393224 | tf_op jit(solution)/shard_map/ppermute | solution.py:57
  193.0 11.1 %collective-permute-start.9 = (bf16[672,256]{1,0:T(8,128)(2,1)S(1)}, bf16[672,256]{1,0:T(8,128)(2,1)S(1)}, u32[]{:S(2)}, u32[]{:S(2)}) collective-permute-start(bf16[672,256]{1,0:T(8,128)(2,1)S(1)} %fusion.17), channel_id=1, source_target_pairs={{0,0},{1,128},{128,1},{129,129},{2,2},{3,130},{130,3},{131,131},{4... | collective-permute-start | bytes 1032200 | tf_op jit(solution)/shard_map/ppermute | solution.py:35
  224.1 19.2 %copy-start.5 = (f32[672]{0:T(1024)S(1)}, f32[672]{0:T(1024)}, u32[]{:S(2)}) copy-start(f32[672]{0:T(1024)} %param.27) | copy-start | bytes 8068
  230.2 13.1 %collective-permute-start.10 = (bf16[672,256]{1,0:T(8,128)(2,1)S(1)}, bf16[672,256]{1,0:T(8,128)(2,1)S(1)}, u32[]{:S(2)}, u32[]{:S(2)}) collective-permute-start(bf16[672,256]{1,0:T(8,128)(2,1)S(1)} %convert_element_type.60), channel_id=1, source_target_pairs={{0,0},{1,128},{128,1},{129,129},{2,2},{3,130},{130,3},{131,131},{4... | collective-permute-start | bytes 1032200 | tf_op jit(solution)/shard_map/ppermute | solution.py:35
  233.4 9.7 %all-to-all-start.6 = ((f32[16,1,256]{2,1,0:T(1,128)}), f32[16,1,256]{2,1,0:T(1,128)S(1)}, u32[]{:S(2)}, u32[]{:S(2)}) async-start(f32[16,1,256]{2,1,0:T(1,128)} %broadcast_in_dim.197), calls=%async_computation.6 | async-start | bytes 32768 | tf_op jit(solution)/shard_map/all_to_all | solution.py:62
Sparse Core Ops, SparseCore 0:
  22.0 88.5 all-gather.2

commit v5 on v2

--- a/solution.py
+++ b/solution.py
@@ -337,7 +337,6 @@
             jnp.where(k_first, other_half, same_half),
         ]
     )
-    along = lax.all_gather(both, "z", axis=0)
     core = core_index.astype(jnp.int32)[None]
 
     image_count = starts.shape[0]
@@ -356,6 +355,10 @@
         soft, lax.axis_index(GIVEN_HEAD) * vis_part, vis_part, 1
     )
     soft_z = exchange(soft_part, "z", Z).reshape(Z * block_rows, vis_part)
+    soft_z, both = lax.optimization_barrier((soft_z, both))
+    along = lax.all_gather(both, "z", axis=0)
+    proj_weight, tokens = swapped(proj_weight), swapped(tokens)
+    soft_z, proj_weight, tokens = lax.optimization_barrier((soft_z, proj_weight, tokens))
     target = jnp.arange(8, dtype=jnp.int32)
     target_k, target_a, target_core = target // 4, target // 2 % 2, target % 2
     target_seq = (target_k * 2 + target_core) * Z + z_index
@@ -381,15 +384,16 @@
     mine = jnp.sum(frames.astype(jnp.float32), axis=0).astype(jnp.bfloat16)
     soft_rows = exchange(mine, HEAD, head_count).reshape(vis, tok_rows)
     embedded = lax.dot_general(
-        swapped(proj_weight), soft_rows, (((0,), (0,)), ((), ())),
+        proj_weight, soft_rows, (((0,), (0,)), ((), ())),
         preferred_element_type=jnp.float32,
     ).astype(jnp.bfloat16)
     my_pos = seq_index * tok_rows + jnp.arange(tok_rows, dtype=jnp.int32)
     my_image = image_of(my_pos, starts)
-    residual = jnp.where((my_image >= 0)[None, :], embedded, swapped(tokens).T)
+    residual = jnp.where((my_image >= 0)[None, :], embedded, tokens.T)
 
     whole = exchange(residual, HEAD, head_count)
-    along, residual = lax.optimization_barrier((along, residual))
+    given_residual = swapped(residual)
+    along, whole, given_residual = lax.optimization_barrier((along, whole, given_residual))
     across = lax.ppermute(along, "core", [(0, 1), (1, 0)])
     half = HEAD_DIM // 2
     frequency = ROPE_BASE ** (-jnp.arange(half, dtype=jnp.float32) * 2.0 / HEAD_DIM)
@@ -410,9 +414,8 @@
         key_gain,
     )
     past_count = WINDOW // tok_rows
-    pieces = [shifted(own, step) for step in range(past_count, 0, -1)]
-    pieces += [own, shifted(own, -1)]
-    window = jnp.concatenate(pieces, axis=0)
+    near = jnp.concatenate([shifted(own, 2), shifted(own, 1)], axis=0)
+    window = jnp.concatenate([shifted(near, 2), near, own, shifted(own, -1)], axis=0)
     key_pos = (seq_index - past_count) * tok_rows + jnp.arange(window.shape[0], dtype=jnp.int32)
     allowed = allowed_keys(my_pos, key_pos, starts, total_rows)
     attended = attend(
@@ -424,11 +427,12 @@
     attended = attended.reshape(tok_rows, 2 * HEAD_DIM).T
     heads_all = exchange(attended, HEAD, head_count)
     projected, squares = project_out(core, heads_all, along, across)
-    squares = jnp.sum(exchange(squares, HEAD, head_count), axis=0)
-    gain = swapped(post_gain)[:, None]
-    post = projected * lax.rsqrt(squares / D + EPSILON) * gain
-    result = (residual.astype(jnp.float32) + post).astype(jnp.bfloat16)
-    return swapped(result).T
+    given = swapped(projected.astype(jnp.bfloat16)).astype(jnp.float32)
+    all_squares = exchange(squares, ("a", "y", "core"), 16).reshape(8, 2, tok_rows)
+    from_core = jnp.arange(2, dtype=jnp.int32) == lax.axis_index("a")
+    squares = jnp.sum(jnp.where(from_core[None, :, None], all_squares, 0.0), axis=(0, 1))
+    post = given * lax.rsqrt(squares[None, :] / D + EPSILON) * post_gain[:, None]
+    return (given_residual.astype(jnp.float32) + post).astype(jnp.bfloat16).T
 
 
 def solution(mesh):

time: 254 us -> 243 us (0.957)
  starting transfers between devices: 76.8 us -> 67.6 us
  waiting for transfers between devices: 94.2 us -> 90.5 us
    ppermute x4, waiting for transfers between devices: 14.7 us -> 50.9 us  [swapped(): return lax.ppermute(value, ('a', 'core'), [(0, 0), (1, 2), (2, 1), (3, 3)])]
    all_to_all x4, waiting for transfers between devices: 46.2 us -> 15.5 us  [exchange(): return lax.all_to_all(spread, axes, 0, 0, tiled=True)]
    all_gather x1, waiting for transfers between devices: 14.1 us -> 0.01 us  [body(): along = lax.all_gather(both, 'z', axis=0)]
    ppermute x1, starting transfers between devices: 10.2 us -> 1.91 us  [body(): across = lax.ppermute(along, 'core', [(0, 1), (1, 0)])]
    ppermute x5 -> x4, starting transfers between devices: 18.7 us -> 12.4 us  [shifted(): return lax.ppermute(value, ('k', 'z', 'core'), pairs)]
    ppermute x4, starting transfers between devices: 12.4 us -> 18.1 us  [swapped(): return lax.ppermute(value, ('a', 'core'), [(0, 0), (1, 2), (2, 1), (3, 3)])]
    ppermute x5 -> x4, waiting for transfers between devices: 15 us -> 18.8 us  [shifted(): return lax.ppermute(value, ('k', 'z', 'core'), pairs)]
  transfers between devices with their start and end apart: 17 -> 16, of which waited for: 11 -> 9; matrix products, arithmetic and copies ran while one was open for 6% -> 6% of each run, Pallas kernels for 1% -> 1%
where the time goes in v5:
time: 243 us; the launch traced here: 242 us
  waiting for transfers between devices  90.5 us (37%)
  starting transfers between devices  67.6 us (28%)
  blocking collectives  31.8 us (13%)
  local copies, waits for them, and re-layouts  16 us (7%)
  between operations  14 us (6%)
  Pallas kernels  11.1 us (5%)
  other arithmetic  5.91 us (2%)
  matrix products  4.59 us (2%)
    ppermute x4, waiting for transfers between devices, swapped(): return lax.ppermute(value, ('a', 'core'), [(0, 0), (1, 2), (2, 1), (3, 3)])  50.9 us
    all_to_all x4, starting transfers between devices, exchange(): return lax.all_to_all(spread, axes, 0, 0, tiled=True)  28 us
    ppermute x4, waiting for transfers between devices, shifted(): return lax.ppermute(value, ('k', 'z', 'core'), pairs)  18.8 us
    ppermute x4, starting transfers between devices, swapped(): return lax.ppermute(value, ('a', 'core'), [(0, 0), (1, 2), (2, 1), (3, 3)])  18.1 us
    all_to_all x1, blocking collectives, exchange(): return lax.all_to_all(spread, axes, 0, 0, tiled=True)  17.4 us
    all_to_all x4, waiting for transfers between devices, exchange(): return lax.all_to_all(spread, axes, 0, 0, tiled=True)  15.5 us
    all_to_all x1, blocking collectives, body(): lax.all_to_all(frames.astype(jnp.bfloat16), ('k', 'a', 'core'), 0, 0, til...  14.4 us
    ppermute x4, starting transfers between devices, shifted(): return lax.ppermute(value, ('k', 'z', 'core'), pairs)  12.4 us
  transfers between devices with their start and end apart: 16, of which 9 were waited for; matrix products, arithmetic and copies ran while one was open for 6% of the time, Pallas kernels for 1%

profile of v5, /device:TPU:1, one launch (start us, length us, event | category | flops | bytes accessed | tf_op | source)
XLA Modules:
  0.0 241.5 jit_solution(5125364536025904109)
XLA Ops:
  6.5 2.5 %reshape.337 = f32[2,4,16,4,1152]{4,3,2,1,0:T(4,128)S(1)} reshape(bf16[8,64,1152]{2,1,0:T(8,128)(2,1)} %param.15) | data formatting | bytes 3538944 | tf_op jit(solution)/shard_map/convert_element_type | solution.py:349
  11.6 15.7 %all-to-all-start = ((bf16[16,32,144]{2,1,0:T(8,128)(2,1)}), bf16[16,32,144]{2,1,0:T(8,128)(2,1)S(1)}, u32[]{:S(2)}, u32[]{:S(2)}) async-start(bf16[16,32,144]{2,1,0:T(8,128)(2,1)} %broadcast_in_dim.100), calls=%async_computation | async-start | bytes 524288 | tf_op jit(solution)/shard_map/all_to_all | solution.py:60
  27.5 4.0 %collective-permute-start = (bf16[144,512]{1,0:T(8,128)(2,1)S(1)}, bf16[144,512]{1,0:T(8,128)(2,1)S(1)}, u32[]{:S(2)}, u32[]{:S(2)}) collective-permute-start(bf16[144,512]{1,0:T(8,128)(2,1)S(1)} %maximum_maximum_fusion), channel_id=1, source_target_pairs={{0,0},{1,128},{128,1},{129,129},{256,256},{257,384},{384,257},{385... | collective-permute-start | bytes 442376 | tf_op jit(solution)/shard_map/ppermute | solution.py:42
  31.4 3.2 %collective-permute-start.1 = (bf16[144,512]{1,0:T(8,128)(2,1)S(1)}, bf16[144,512]{1,0:T(8,128)(2,1)S(1)}, u32[]{:S(2)}, u32[]{:S(2)}) collective-permute-start(bf16[144,512]{1,0:T(8,128)(2,1)S(1)} %maximum_maximum_fusion), channel_id=1, source_target_pairs={{0,256},{1,384},{128,257},{129,385},{256,0},{257,128},{384,1},{385... | collective-permute-start | bytes 442376 | tf_op jit(solution)/shard_map/ppermute | solution.py:42
  34.7 5.1 %collective-permute-done.1 = bf16[144,512]{1,0:T(8,128)(2,1)S(1)} collective-permute-done((bf16[144,512]{1,0:T(8,128)(2,1)S(1)}, bf16[144,512]{1,0:T(8,128)(2,1)S(1)}, u32[]{:S(2)}, u32[]{:S(2)}) %collective-permute-start.1) | collective-permute-done | bytes 147488 | tf_op jit(solution)/shard_map/ppermute | solution.py:42
  40.7 9.0 %collective-permute-start.2 = (bf16[1152,672]{0,1:T(8,128)(2,1)S(1)}, bf16[1152,672]{0,1:T(8,128)(2,1)}, u32[]{:S(2)}, u32[]{:S(2)}) collective-permute-start(bf16[1152,672]{0,1:T(8,128)(2,1)S(1)} %copy-done.11), channel_id=1, source_target_pairs={{0,0},{1,128},{128,1},{129,129},{2,2},{3,130},{130,3},{131,131},{4... | collective-permute-start | bytes 4644872 | tf_op jit(solution)/shard_map/ppermute | solution.py:33
  49.7 1.9 collective-permute-start.3
  52.1 19.5 %collective-permute-done.3 = bf16[256,672]{0,1:T(8,128)(2,1)S(1)} collective-permute-done((bf16[256,672]{0,1:T(8,128)(2,1)S(1)}, bf16[256,672]{0,1:T(8,128)(2,1)S(1)}, u32[]{:S(2)}, u32[]{:S(2)}) %collective-permute-start.3) | collective-permute-done | bytes 344096 | tf_op jit(solution)/shard_map/ppermute | solution.py:33
  72.9 14.4 %all_to_all.30 = bf16[8,144,256]{2,1,0:T(8,128)(2,1)S(1)} all-to-all(bf16[8,144,256]{2,1,0:T(8,128)(2,1)S(1)} %fusion.16), channel_id=1, replica_groups=mesh['k'=2,'a'=2,'z'=16,'y'=4,'core'=2] {'k','a','core'}, dimensions={0} | all-to-all | bytes 1179648 | tf_op jit(solution)/shard_map/all_to_all | solution.py:381
  88.3 4.5 %all-to-all-start.2 = ((bf16[8,144,256]{2,1,0:T(8,128)(2,1)}), bf16[8,144,256]{2,1,0:T(8,128)(2,1)S(1)}, u32[]{:S(2)}, u32[]{:S(2)}) async-start(bf16[8,144,256]{2,1,0:T(8,128)(2,1)} %broadcast_in_dim.108), calls=%async_computation.2 | async-start | bytes 1179648 | tf_op jit(solution)/shard_map/all_to_all | solution.py:60
  92.9 9.9 %all-to-all-done.2 = bf16[8,144,256]{2,1,0:T(8,128)(2,1)S(1)} async-done(((bf16[8,144,256]{2,1,0:T(8,128)(2,1)}), bf16[8,144,256]{2,1,0:T(8,128)(2,1)S(1)}, u32[]{:S(2)}, u32[]{:S(2)}) %all-to-all-start.2) | async-done | bytes 589856 | tf_op jit(solution)/shard_map/all_to_all | solution.py:60
  102.8 2.0 fusion.19
  106.6 3.8 %all-to-all-start.3 = ((bf16[8,672,256]{2,1,0:T(8,128)(2,1)}), bf16[8,672,256]{2,1,0:T(8,128)(2,1)S(1)}, u32[]{:S(2)}, u32[]{:S(2)}) async-start(bf16[8,672,256]{2,1,0:T(8,128)(2,1)} %broadcast_in_dim.109), calls=%async_computation.3 | async-start | bytes 5505024 | tf_op jit(solution)/shard_map/all_to_all | solution.py:60
  110.3 5.2 %collective-permute-start.4 = (bf16[672,256]{1,0:T(8,128)(2,1)S(1)}, bf16[672,256]{1,0:T(8,128)(2,1)S(1)}, u32[]{:S(2)}, u32[]{:S(2)}) collective-permute-start(bf16[672,256]{1,0:T(8,128)(2,1)S(1)} %fusion.19), channel_id=1, source_target_pairs={{0,0},{1,128},{128,1},{129,129},{2,2},{3,130},{130,3},{131,131},{4... | collective-permute-start | bytes 1032200 | tf_op jit(solution)/shard_map/ppermute | solution.py:33
  115.6 31.4 %collective-permute-done.4 = bf16[672,256]{1,0:T(8,128)(2,1)S(1)} collective-permute-done((bf16[672,256]{1,0:T(8,128)(2,1)S(1)}, bf16[672,256]{1,0:T(8,128)(2,1)S(1)}, u32[]{:S(2)}, u32[]{:S(2)}) %collective-permute-start.4) | collective-permute-done | bytes 344096 | tf_op jit(solution)/shard_map/ppermute | solution.py:33
  147.0 1.9 collective-permute-start.5
  148.9 4.1 %reshape.342.gain_ref = f32[8,672,1]{2,1,0:T(8,128)} reshape(f32[5376]{0:T(1024)S(1)} %copy-done.5) | data formatting | bytes 43008 | tf_op jit(solution)/shard_map/reshape | solution.py:402
  155.7 2.3 copy-done.1
  158.1 2.7 %shard_map.136 = (f32[256,512]{1,0:T(8,128)S(1)}, f32[1,256]{1,0:T(1,128)S(1)}) custom-call(s32[1]{0:T(128)} %bitcast.9.core_ref, bf16[8,672,256]{2,1,0:T(8,128)(2,1)S(1)} %all-to-all-done.3.whole_ref, f32[8,672,1]{2,1,0:T(8,128)S(1)} %copy-done, bf16[16,2,144,512]{3,2,1,0:T(8,128)(2,1)S(1)} %bitcast.75), custom_call_target="tpu_custom_call" | custom-call | flops 704643072 | bytes 5242880 | tf_op jit(solution)/shard_map/pallas_call | solution.py:176
  160.9 4.7 %shard_map.137 = (bf16[256,256]{1,0:T(8,128)(2,1)S(1)}, bf16[256,256]{1,0:T(8,128)(2,1)S(1)}) custom-call(s32[1]{0:T(128)} %bitcast.9.core_ref, bf16[8,672,256]{2,1,0:T(8,128)(2,1)S(1)} %all-to-all-done.3.whole_ref, f32[8,672,1]{2,1,0:T(8,128)S(1)} %copy-done, bf16[16,2,144,512]{3,2,1,0:T(8,128)(2,1)} %collective-permute-done.5.weight_ref.across_ref, ...), custom_call_target="tpu_custom_call" | custom-call | flops 704643072 | bytes 5242880 | tf_op jit(solution)/shard_map/pallas_call | solution.py:201
  165.6 3.7 %collective-permute-start.6 = (bf16[256,256]{1,0:T(8,128)(2,1)S(1)}, bf16[256,256]{1,0:T(8,128)(2,1)S(1)}, u32[]{:S(2)}, u32[]{:S(2)}) collective-permute-start(bf16[256,256]{1,0:T(8,128)(2,1)S(1)} %get-tuple-element.29), channel_id=1, source_target_pairs={{0,16},{8,24},{16,32},{24,40},{32,48},{40,56},{48,64},{56,72},{64,... | collective-permute-start | bytes 393224 | tf_op jit(solution)/shard_map/ppermute | solution.py:55
  169.3 3.1 %collective-permute-start.7 = (bf16[256,256]{1,0:T(8,128)(2,1)S(1)}, bf16[256,256]{1,0:T(8,128)(2,1)S(1)}, u32[]{:S(2)}, u32[]{:S(2)}) collective-permute-start(bf16[256,256]{1,0:T(8,128)(2,1)S(1)} %get-tuple-element.29), channel_id=1, source_target_pairs={{0,8},{8,16},{16,24},{24,32},{32,40},{40,48},{48,56},{56,64},{64,7... | collective-permute-start | bytes 393224 | tf_op jit(solution)/shard_map/ppermute | solution.py:55
  172.4 2.3 collective-permute-done.6
  174.8 5.5 %collective-permute-done.7 = bf16[256,256]{1,0:T(8,128)(2,1)S(1)} collective-permute-done((bf16[256,256]{1,0:T(8,128)(2,1)S(1)}, bf16[256,256]{1,0:T(8,128)(2,1)S(1)}, u32[]{:S(2)}, u32[]{:S(2)}) %collective-permute-start.7) | collective-permute-done | bytes 131104 | tf_op jit(solution)/shard_map/ppermute | solution.py:55
  180.3 2.9 %collective-permute-start.8 = (bf16[512,256]{1,0:T(8,128)(2,1)S(1)}, bf16[512,256]{1,0:T(8,128)(2,1)S(1)}, u32[]{:S(2)}, u32[]{:S(2)}) collective-permute-start(bf16[512,256]{1,0:T(8,128)(2,1)S(1)} %pad_maximum_fusion.1), channel_id=1, source_target_pairs={{0,16},{8,24},{16,32},{24,40},{32,48},{40,56},{48,64},{56,72},{64,... | collective-permute-start | bytes 786440 | tf_op jit(solution)/shard_map/ppermute | solution.py:55
  184.6 2.7 %collective-permute-start.9 = (bf16[256,256]{1,0:T(8,128)(2,1)S(1)}, bf16[256,256]{1,0:T(8,128)(2,1)S(1)}, u32[]{:S(2)}, u32[]{:S(2)}) collective-permute-start(bf16[256,256]{1,0:T(8,128)(2,1)S(1)} %get-tuple-element.29), channel_id=1, source_target_pairs={{8,0},{16,8},{24,16},{32,24},{40,32},{48,40},{56,48},{64,56},{72,6... | collective-permute-start | bytes 393224 | tf_op jit(solution)/shard_map/ppermute | solution.py:55
  187.3 11.0 %collective-permute-done.8 = bf16[512,256]{1,0:T(8,128)(2,1)S(1)} collective-permute-done((bf16[512,256]{1,0:T(8,128)(2,1)S(1)}, bf16[512,256]{1,0:T(8,128)(2,1)S(1)}, u32[]{:S(2)}, u32[]{:S(2)}) %collective-permute-start.8) | collective-permute-done | bytes 262176 | tf_op jit(solution)/shard_map/ppermute | solution.py:55
  200.2 17.4 %all_to_all.31.own_ref.other_ref = bf16[8,256,256]{2,1,0:T(8,128)(2,1)S(1)} all-to-all(bf16[8,256,256]{2,1,0:T(8,128)(2,1)S(1)} %broadcast_in_dim.189), channel_id=1, replica_groups=mesh['k'=2,'a'=2,'z'=16,'y'=4,'core'=2] {'y','a'}, dimensions={0} | all-to-all | bytes 2097152 | tf_op jit(solution)/shard_map/all_to_all | solution.py:60
  217.6 3.7 %shard_map.138 = (f32[672,256]{1,0:T(8,128)S(1)}, f32[1,256]{1,0:T(1,128)S(1)}) custom-call(s32[1]{0:T(128)} %bitcast.9.core_ref, bf16[8,256,256]{2,1,0:T(8,128)(2,1)S(1)} %all_to_all.31.own_ref.other_ref, bf16[8,256,256]{2,1,0:T(8,128)(2,1)S(1)} %all_to_all.31.own_ref.other_ref, bf16[16,2,144,512]{3,2,1,0:T(8,128)(2,1)S(1)} %bitcast.78, ...), custom_call_target="tpu_custom_call" | custom-call | flops 805306368 | bytes 5242880 | tf_op jit(solution)/shard_map/pallas_call | solution.py:269
  221.3 1.9 collective-permute-start.10
  223.9 4.0 %all-to-all-start.5 = ((f32[16,1,256]{2,1,0:T(1,128)}), f32[16,1,256]{2,1,0:T(1,128)S(1)}, u32[]{:S(2)}, u32[]{:S(2)}) async-start(f32[16,1,256]{2,1,0:T(1,128)} %broadcast_in_dim.194), calls=%async_computation.5 | async-start | bytes 32768 | tf_op jit(solution)/shard_map/all_to_all | solution.py:60
  228.0 5.7 %all-to-all-done.5 = f32[16,1,256]{2,1,0:T(1,128)S(1)} async-done(((f32[16,1,256]{2,1,0:T(1,128)}), f32[16,1,256]{2,1,0:T(1,128)S(1)}, u32[]{:S(2)}, u32[]{:S(2)}) %all-to-all-start.5) | async-done | bytes 16416 | tf_op jit(solution)/shard_map/all_to_all | solution.py:60
  (104 shorter events, 15.6 us)
Async XLA Ops:
  6.5 20.8 %slice-start.2 = ((bf16[32,672]{1,0:T(8,128)(2,1)}), bf16[32,160]{1,0:T(8,128)(2,1)S(1)}, s32[]{:S(2)}) async-start(bf16[32,672]{1,0:T(8,128)(2,1)} %param.26), calls=%async_computation.9 | async-start | bytes 32768 | tf_op jit(solution)/shard_map/slice | solution.py:319
  6.5 20.8 %copy-start.4 = (bf16[84,256]{1,0:T(8,128)(2,1)S(1)}, bf16[84,256]{1,0:T(8,128)(2,1)}, u32[]{:S(2)}) copy-start(bf16[84,256]{1,0:T(8,128)(2,1)} %param.21) | copy-start | bytes 129028
  6.5 20.9 %copy-start.6 = (bf16[84,128]{1,0:T(8,128)(2,1)S(1)}, bf16[84,128]{1,0:T(8,128)(2,1)}, u32[]{:S(2)}) copy-start(bf16[84,128]{1,0:T(8,128)(2,1)} %param.23) | copy-start | bytes 64516
  6.5 20.9 %copy-start.7 = (bf16[84,128]{1,0:T(8,128)(2,1)S(1)}, bf16[84,128]{1,0:T(8,128)(2,1)}, u32[]{:S(2)}) copy-start(bf16[84,128]{1,0:T(8,128)(2,1)} %param.22) | copy-start | bytes 64516
  9.0 18.4 %slice-start.3 = ((bf16[32,672]{1,0:T(8,128)(2,1)}), bf16[32,512]{1,0:T(8,128)(2,1)S(1)}, s32[]{:S(2)}) async-start(bf16[32,672]{1,0:T(8,128)(2,1)} %param.26), calls=%async_computation.10 | async-start | bytes 65536 | tf_op jit(solution)/shard_map/slice | solution.py:326
  9.1 40.6 %copy-start.12 = (bf16[256,672]{0,1:T(8,128)(2,1)S(1)}, bf16[256,672]{0,1:T(8,128)(2,1)}, u32[]{:S(2)}) copy-start(bf16[256,672]{0,1:T(8,128)(2,1)} %param.14) | copy-start | bytes 1032196
  9.1 42.6 %copy-start.8 = (s32[8]{0:T(128)S(1)}, s32[8]{0:T(128)}, u32[]{:S(2)}) copy-start(s32[8]{0:T(128)} %param.16) | copy-start | bytes 100
  9.1 42.6 %copy-start.10 = (s32[8]{0:T(128)S(1)}, s32[8]{0:T(128)}, u32[]{:S(2)}) copy-start(s32[8]{0:T(128)} %param.17) | copy-start | bytes 100
  9.6 31.0 %copy-start.11 = (bf16[1152,672]{0,1:T(8,128)(2,1)S(1)}, bf16[1152,672]{0,1:T(8,128)(2,1)}, u32[]{:S(2)}) copy-start(bf16[1152,672]{0,1:T(8,128)(2,1)} %param.19) | copy-start | bytes 4644868
  11.6 29.1 %all-to-all-start = ((bf16[16,32,144]{2,1,0:T(8,128)(2,1)}), bf16[16,32,144]{2,1,0:T(8,128)(2,1)S(1)}, u32[]{:S(2)}, u32[]{:S(2)}) async-start(bf16[16,32,144]{2,1,0:T(8,128)(2,1)} %broadcast_in_dim.100), calls=%async_computation | async-start | bytes 524288 | tf_op jit(solution)/shard_map/all_to_all | solution.py:60
  27.3 119.7 %all-gather.3.cloned.1.call-start = ((), (), s32[]{:S(2)}) async-start(), calls=%async_computation.6 | async-start | bytes 5013504 | tf_op jit(solution)/shard_map/all_gather | solution.py:359
  27.5 7.2 %collective-permute-start = (bf16[144,512]{1,0:T(8,128)(2,1)S(1)}, bf16[144,512]{1,0:T(8,128)(2,1)S(1)}, u32[]{:S(2)}, u32[]{:S(2)}) collective-permute-start(bf16[144,512]{1,0:T(8,128)(2,1)S(1)} %maximum_maximum_fusion), channel_id=1, source_target_pairs={{0,0},{1,128},{128,1},{129,129},{256,256},{257,384},{384,257},{385... | collective-permute-start | bytes 442376 | tf_op jit(solution)/shard_map/ppermute | solution.py:42
  31.4 8.4 %collective-permute-start.1 = (bf16[144,512]{1,0:T(8,128)(2,1)S(1)}, bf16[144,512]{1,0:T(8,128)(2,1)S(1)}, u32[]{:S(2)}, u32[]{:S(2)}) collective-permute-start(bf16[144,512]{1,0:T(8,128)(2,1)S(1)} %maximum_maximum_fusion), channel_id=1, source_target_pairs={{0,256},{1,384},{128,257},{129,385},{256,0},{257,128},{384,1},{385... | collective-permute-start | bytes 442376 | tf_op jit(solution)/shard_map/ppermute | solution.py:42
  40.7 30.9 %collective-permute-start.2 = (bf16[1152,672]{0,1:T(8,128)(2,1)S(1)}, bf16[1152,672]{0,1:T(8,128)(2,1)}, u32[]{:S(2)}, u32[]{:S(2)}) collective-permute-start(bf16[1152,672]{0,1:T(8,128)(2,1)S(1)} %copy-done.11), channel_id=1, source_target_pairs={{0,0},{1,128},{128,1},{129,129},{2,2},{3,130},{130,3},{131,131},{4... | collective-permute-start | bytes 4644872 | tf_op jit(solution)/shard_map/ppermute | solution.py:33
  49.7 21.9 %collective-permute-start.3 = (bf16[256,672]{0,1:T(8,128)(2,1)S(1)}, bf16[256,672]{0,1:T(8,128)(2,1)S(1)}, u32[]{:S(2)}, u32[]{:S(2)}) collective-permute-start(bf16[256,672]{0,1:T(8,128)(2,1)S(1)} %copy-done.12), channel_id=1, source_target_pairs={{0,0},{1,128},{128,1},{129,129},{2,2},{3,130},{130,3},{131,131},{4... | collective-permute-start | bytes 1032200 | tf_op jit(solution)/shard_map/ppermute | solution.py:33
  88.3 14.5 %all-to-all-start.2 = ((bf16[8,144,256]{2,1,0:T(8,128)(2,1)}), bf16[8,144,256]{2,1,0:T(8,128)(2,1)S(1)}, u32[]{:S(2)}, u32[]{:S(2)}) async-start(bf16[8,144,256]{2,1,0:T(8,128)(2,1)} %broadcast_in_dim.108), calls=%async_computation.2 | async-start | bytes 1179648 | tf_op jit(solution)/shard_map/all_to_all | solution.py:60
  106.6 42.4 %copy-start.5 = (f32[5376]{0:T(1024)S(1)}, f32[5376]{0:T(1024)}, u32[]{:S(2)}) copy-start(f32[5376]{0:T(1024)} %param.20) | copy-start | bytes 64516
  106.6 40.4 %all-to-all-start.3 = ((bf16[8,672,256]{2,1,0:T(8,128)(2,1)}), bf16[8,672,256]{2,1,0:T(8,128)(2,1)S(1)}, u32[]{:S(2)}, u32[]{:S(2)}) async-start(bf16[8,672,256]{2,1,0:T(8,128)(2,1)} %broadcast_in_dim.109), calls=%async_computation.3 | async-start | bytes 5505024 | tf_op jit(solution)/shard_map/all_to_all | solution.py:60
  110.3 36.7 %collective-permute-start.4 = (bf16[672,256]{1,0:T(8,128)(2,1)S(1)}, bf16[672,256]{1,0:T(8,128)(2,1)S(1)}, u32[]{:S(2)}, u32[]{:S(2)}) collective-permute-start(bf16[672,256]{1,0:T(8,128)(2,1)S(1)} %fusion.19), channel_id=1, source_target_pairs={{0,0},{1,128},{128,1},{129,129},{2,2},{3,130},{130,3},{131,131},{4... | collective-permute-start | bytes 1032200 | tf_op jit(solution)/shard_map/ppermute | solution.py:33
  147.0 13.8 %collective-permute-start.5 = (bf16[16,2,144,512]{3,2,1,0:T(8,128)(2,1)}, bf16[16,2,144,512]{3,2,1,0:T(8,128)(2,1)}, u32[]{:S(2)}, u32[]{:S(2)}) collective-permute-start(bf16[16,2,144,512]{3,2,1,0:T(8,128)(2,1)} %bitcast.74), channel_id=1, source_target_pairs={{0,1},{1,0},{2,3},{3,2},{4,5},{5,4},{6,7},{7,6},{8,9},{9,8},{10,11... | collective-permute-start | bytes 14155784 | tf_op jit(solution)/shard_map/ppermute | solution.py:397
  155.7 2.3 copy-start.1
  158.1 2.8 %copy-start.2 = (f32[128]{0:T(128)S(1)}, f32[128]{0:T(128)}, u32[]{:S(2)}) copy-start(f32[128]{0:T(128)} %param.24) | copy-start | bytes 1540
  158.1 2.8 %copy-start.3 = (f32[128]{0:T(128)S(1)}, f32[128]{0:T(128)}, u32[]{:S(2)}) copy-start(f32[128]{0:T(128)} %param.25) | copy-start | bytes 1540
  165.6 9.2 %collective-permute-start.6 = (bf16[256,256]{1,0:T(8,128)(2,1)S(1)}, bf16[256,256]{1,0:T(8,128)(2,1)S(1)}, u32[]{:S(2)}, u32[]{:S(2)}) collective-permute-start(bf16[256,256]{1,0:T(8,128)(2,1)S(1)} %get-tuple-element.29), channel_id=1, source_target_pairs={{0,16},{8,24},{16,32},{24,40},{32,48},{40,56},{48,64},{56,72},{64,... | collective-permute-start | bytes 393224 | tf_op jit(solution)/shard_map/ppermute | solution.py:55
  169.3 11.0 %collective-permute-start.7 = (bf16[256,256]{1,0:T(8,128)(2,1)S(1)}, bf16[256,256]{1,0:T(8,128)(2,1)S(1)}, u32[]{:S(2)}, u32[]{:S(2)}) collective-permute-start(bf16[256,256]{1,0:T(8,128)(2,1)S(1)} %get-tuple-element.29), channel_id=1, source_target_pairs={{0,8},{8,16},{16,24},{24,32},{32,40},{40,48},{48,56},{56,64},{64,7... | collective-permute-start | bytes 393224 | tf_op jit(solution)/shard_map/ppermute | solution.py:55
  180.3 18.0 %collective-permute-start.8 = (bf16[512,256]{1,0:T(8,128)(2,1)S(1)}, bf16[512,256]{1,0:T(8,128)(2,1)S(1)}, u32[]{:S(2)}, u32[]{:S(2)}) collective-permute-start(bf16[512,256]{1,0:T(8,128)(2,1)S(1)} %pad_maximum_fusion.1), channel_id=1, source_target_pairs={{0,16},{8,24},{16,32},{24,40},{32,48},{40,56},{48,64},{56,72},{64,... | collective-permute-start | bytes 786440 | tf_op jit(solution)/shard_map/ppermute | solution.py:55
  184.6 13.8 %collective-permute-start.9 = (bf16[256,256]{1,0:T(8,128)(2,1)S(1)}, bf16[256,256]{1,0:T(8,128)(2,1)S(1)}, u32[]{:S(2)}, u32[]{:S(2)}) collective-permute-start(bf16[256,256]{1,0:T(8,128)(2,1)S(1)} %get-tuple-element.29), channel_id=1, source_target_pairs={{8,0},{16,8},{24,16},{32,24},{40,32},{48,40},{56,48},{64,56},{72,6... | collective-permute-start | bytes 393224 | tf_op jit(solution)/shard_map/ppermute | solution.py:55
  198.4 19.2 %slice-start = ((s8[4718592]{0:T(1024)(128)(4,1)}), s8[4194304]{0:T(1024)(128)(4,1)S(1)}, s32[]{:S(2)}) async-start(s8[4718592]{0:T(1024)(128)(4,1)} %bitcast.76), calls=%async_computation.7 | async-start | bytes 8388608
  199.0 18.6 %slice-start.1 = ((s8[4718592]{0:T(1024)(128)(4,1)}), s8[524288]{0:T(1024)(128)(4,1)S(1)}, s32[]{:S(2)}) async-start(s8[4718592]{0:T(1024)(128)(4,1)} %bitcast.76), calls=%async_computation.8 | async-start | bytes 1048576
  217.6 16.1 %copy-start.9 = (f32[672]{0:T(1024)S(1)}, f32[672]{0:T(1024)}, u32[]{:S(2)}) copy-start(f32[672]{0:T(1024)} %param.27) | copy-start | bytes 8068
  221.3 12.4 %collective-permute-start.10 = (bf16[672,256]{1,0:T(8,128)(2,1)S(1)}, bf16[672,256]{1,0:T(8,128)(2,1)S(1)}, u32[]{:S(2)}, u32[]{:S(2)}) collective-permute-start(bf16[672,256]{1,0:T(8,128)(2,1)S(1)} %convert_element_type.60), channel_id=1, source_target_pairs={{0,0},{1,128},{128,1},{129,129},{2,2},{3,130},{130,3},{131,131},{4... | collective-permute-start | bytes 1032200 | tf_op jit(solution)/shard_map/ppermute | solution.py:33
  223.9 9.8 %all-to-all-start.5 = ((f32[16,1,256]{2,1,0:T(1,128)}), f32[16,1,256]{2,1,0:T(1,128)S(1)}, u32[]{:S(2)}, u32[]{:S(2)}) async-start(f32[16,1,256]{2,1,0:T(1,128)} %broadcast_in_dim.194), calls=%async_computation.5 | async-start | bytes 32768 | tf_op jit(solution)/shard_map/all_to_all | solution.py:60
  (1 other events, 1.8 us)
Sparse Core Ops, SparseCore 0:
  40.8 72.5 all-gather.2

commit v6 on v5

--- a/solution.py
+++ b/solution.py
@@ -345,20 +345,26 @@
     pool_rows = features.shape[0] // POOL
     block_rows = pool_rows * pooled_side
     shards_each = pooled_side // pool_rows
-    patch_grid = features.reshape(pool_rows, POOL, pooled_side, POOL, vis)
-    pooled = jnp.sum(patch_grid, axis=(1, 3), dtype=jnp.float32).reshape(block_rows, vis) / (
-        POOL * POOL
-    )
+    row = jnp.arange(block_rows, dtype=jnp.int32)
+    patch = jnp.arange(features.shape[0] * PATCH_SIDE, dtype=jnp.int32)
+    square = patch // (PATCH_SIDE * POOL) * pooled_side + patch % PATCH_SIDE // POOL
+    ones = (row[:, None] == square[None, :]).astype(jnp.bfloat16)
+    pooled = jnp.dot(
+        ones, features.reshape(-1, vis), preferred_element_type=jnp.float32
+    ) / (POOL * POOL)
     soft = rms_scale(pooled, soft_gain).astype(jnp.bfloat16)
     vis_part = vis // head_count
     soft_part = lax.dynamic_slice_in_dim(
         soft, lax.axis_index(GIVEN_HEAD) * vis_part, vis_part, 1
     )
     soft_z = exchange(soft_part, "z", Z).reshape(Z * block_rows, vis_part)
-    soft_z, both = lax.optimization_barrier((soft_z, both))
+    proj_other = lax.ppermute(proj_weight, ("a", "core"), [(0, 1), (3, 2)])
+    tokens = swapped(tokens)
+    soft_z, both, tokens, proj_other = lax.optimization_barrier(
+        (soft_z, both, tokens, proj_other)
+    )
     along = lax.all_gather(both, "z", axis=0)
-    proj_weight, tokens = swapped(proj_weight), swapped(tokens)
-    soft_z, proj_weight, tokens = lax.optimization_barrier((soft_z, proj_weight, tokens))
+    proj_weight = jnp.where(core_index == lax.axis_index("a"), proj_weight, proj_other)
     target = jnp.arange(8, dtype=jnp.int32)
     target_k, target_a, target_core = target // 4, target // 2 % 2, target % 2
     target_seq = (target_k * 2 + target_core) * Z + z_index

time: 243 us -> 219 us (0.901)
  waiting for transfers between devices: 90.5 us -> 70.6 us
  starting transfers between devices: 67.6 us -> 62.1 us
  blocking collectives: 31.8 us -> 35.3 us
  local copies, waits for them, and re-layouts: 16 us -> 13.3 us
    ppermute x4 -> x3, waiting for transfers between devices: 50.9 us -> 33.6 us  [swapped(): return lax.ppermute(value, ('a', 'core'), [(0, 0), (1, 2), (2, 1), (3, 3)])]
    ppermute x4 -> x3, starting transfers between devices: 18.1 us -> 10.3 us  [swapped(): return lax.ppermute(value, ('a', 'core'), [(0, 0), (1, 2), (2, 1), (3, 3)])]
    all_to_all x1, blocking collectives: 14.4 us -> 18 us  [body(): lax.all_to_all(frames.astype(jnp.bfloat16), ('k', 'a', 'core'), 0, 0, til...]
    convert_element_type x1 -> x0, local copies, waits for them, and re-layouts: 2.49 us -> none  [body(): jnp.sum(patch_grid, axis=(1, 3), dtype=jnp.float32).reshape(block_rows, vis)]
    ppermute x2, waiting for transfers between devices: 5.21 us -> 2.74 us  [from_half(): return lax.ppermute(value, ('k', 'a', 'core'), pairs)]
  transfers between devices with their start and end apart: 16 -> 16, of which waited for: 9 -> 8; matrix products, arithmetic and copies ran while one was open for 6% -> 8% of each run, Pallas kernels for 1% -> 2%
where the time goes in v6:
time: 219 us; the launch traced here: 218 us
  waiting for transfers between devices  70.6 us (32%)
  starting transfers between devices  62.1 us (28%)
  blocking collectives  35.3 us (16%)
  between operations  14 us (6%)
  local copies, waits for them, and re-layouts  13.3 us (6%)
  Pallas kernels  12.6 us (6%)
  other arithmetic  5.27 us (2%)
  matrix products  5.01 us (2%)
    ppermute x3, waiting for transfers between devices, swapped(): return lax.ppermute(value, ('a', 'core'), [(0, 0), (1, 2), (2, 1), (3, 3)])  33.6 us
    all_to_all x4, starting transfers between devices, exchange(): return lax.all_to_all(spread, axes, 0, 0, tiled=True)  28.5 us
    ppermute x4, waiting for transfers between devices, shifted(): return lax.ppermute(value, ('k', 'z', 'core'), pairs)  18.9 us
    all_to_all x1, blocking collectives, body(): lax.all_to_all(frames.astype(jnp.bfloat16), ('k', 'a', 'core'), 0, 0, til...  18 us
    all_to_all x1, blocking collectives, exchange(): return lax.all_to_all(spread, axes, 0, 0, tiled=True)  17.3 us
    all_to_all x4, waiting for transfers between devices, exchange(): return lax.all_to_all(spread, axes, 0, 0, tiled=True)  15.4 us
    ppermute x4, starting transfers between devices, shifted(): return lax.ppermute(value, ('k', 'z', 'core'), pairs)  12.5 us
    ppermute x3, starting transfers between devices, swapped(): return lax.ppermute(value, ('a', 'core'), [(0, 0), (1, 2), (2, 1), (3, 3)])  10.3 us
  transfers between devices with their start and end apart: 16, of which 8 were waited for; matrix products, arithmetic and copies ran while one was open for 8% of the time, Pallas kernels for 2%

profile of v6, /device:TPU:1, one launch (start us, length us, event | category | flops | bytes accessed | tf_op | source)
XLA Modules:
  0.0 218.2 jit_solution(15999237463388137402)
XLA Ops:
  10.1 15.7 %all-to-all-start = ((bf16[16,32,144]{2,1,0:T(8,128)(2,1)}), bf16[16,32,144]{2,1,0:T(8,128)(2,1)S(1)}, u32[]{:S(2)}, u32[]{:S(2)}) async-start(bf16[16,32,144]{2,1,0:T(8,128)(2,1)} %broadcast_in_dim.100), calls=%async_computation | async-start | bytes 524288 | tf_op jit(solution)/shard_map/all_to_all | solution.py:60
  26.0 4.0 %collective-permute-start = (bf16[144,512]{1,0:T(8,128)(2,1)S(1)}, bf16[144,512]{1,0:T(8,128)(2,1)S(1)}, u32[]{:S(2)}, u32[]{:S(2)}) collective-permute-start(bf16[144,512]{1,0:T(8,128)(2,1)S(1)} %maximum_maximum_fusion), channel_id=1, source_target_pairs={{0,0},{1,128},{128,1},{129,129},{256,256},{257,384},{384,257},{385... | collective-permute-start | bytes 442376 | tf_op jit(solution)/shard_map/ppermute | solution.py:42
  30.0 3.2 %collective-permute-start.1 = (bf16[144,512]{1,0:T(8,128)(2,1)S(1)}, bf16[144,512]{1,0:T(8,128)(2,1)S(1)}, u32[]{:S(2)}, u32[]{:S(2)}) collective-permute-start(bf16[144,512]{1,0:T(8,128)(2,1)S(1)} %maximum_maximum_fusion), channel_id=1, source_target_pairs={{0,256},{1,384},{128,257},{129,385},{256,0},{257,128},{384,1},{385... | collective-permute-start | bytes 442376 | tf_op jit(solution)/shard_map/ppermute | solution.py:42
  33.2 3.0 %collective-permute-start.2 = (bf16[256,672]{0,1:T(8,128)(2,1)S(1)}, bf16[256,672]{0,1:T(8,128)(2,1)S(1)}, u32[]{:S(2)}, u32[]{:S(2)}) collective-permute-start(bf16[256,672]{0,1:T(8,128)(2,1)S(1)} %copy-done.12), channel_id=1, source_target_pairs={{0,0},{1,128},{128,1},{129,129},{2,2},{3,130},{130,3},{131,131},{4... | collective-permute-start | bytes 1032200 | tf_op jit(solution)/shard_map/ppermute | solution.py:33
  36.2 2.7 %collective-permute-done.1 = bf16[144,512]{1,0:T(8,128)(2,1)S(1)} collective-permute-done((bf16[144,512]{1,0:T(8,128)(2,1)S(1)}, bf16[144,512]{1,0:T(8,128)(2,1)S(1)}, u32[]{:S(2)}, u32[]{:S(2)}) %collective-permute-start.1) | collective-permute-done | bytes 147488 | tf_op jit(solution)/shard_map/ppermute | solution.py:42
  39.7 2.3 %collective-permute-done.2 = bf16[256,672]{0,1:T(8,128)(2,1)S(1)} collective-permute-done((bf16[256,672]{0,1:T(8,128)(2,1)S(1)}, bf16[256,672]{0,1:T(8,128)(2,1)S(1)}, u32[]{:S(2)}, u32[]{:S(2)}) %collective-permute-start.2) | collective-permute-done | bytes 344096 | tf_op jit(solution)/shard_map/ppermute | solution.py:33
  43.9 18.0 %all_to_all.30 = bf16[8,144,256]{2,1,0:T(8,128)(2,1)S(1)} all-to-all(bf16[8,144,256]{2,1,0:T(8,128)(2,1)S(1)} %fusion.19), channel_id=1, replica_groups=mesh['k'=2,'a'=2,'z'=16,'y'=4,'core'=2] {'k','a','core'}, dimensions={0} | all-to-all | bytes 1179648 | tf_op jit(solution)/shard_map/all_to_all | solution.py:387
  62.8 4.2 %all-to-all-start.2 = ((bf16[8,144,256]{2,1,0:T(8,128)(2,1)}), bf16[8,144,256]{2,1,0:T(8,128)(2,1)S(1)}, u32[]{:S(2)}, u32[]{:S(2)}) async-start(bf16[8,144,256]{2,1,0:T(8,128)(2,1)} %broadcast_in_dim.108), calls=%async_computation.2 | async-start | bytes 1179648 | tf_op jit(solution)/shard_map/all_to_all | solution.py:60
  67.1 9.7 %all-to-all-done.2 = bf16[8,144,256]{2,1,0:T(8,128)(2,1)S(1)} async-done(((bf16[8,144,256]{2,1,0:T(8,128)(2,1)}), bf16[8,144,256]{2,1,0:T(8,128)(2,1)S(1)}, u32[]{:S(2)}, u32[]{:S(2)}) %all-to-all-start.2) | async-done | bytes 589856 | tf_op jit(solution)/shard_map/all_to_all | solution.py:60
  76.8 2.0 fusion.28
  78.9 1.7 broadcast_in_dim.109
  80.6 4.6 %all-to-all-start.3 = ((bf16[8,672,256]{2,1,0:T(8,128)(2,1)}), bf16[8,672,256]{2,1,0:T(8,128)(2,1)}, u32[]{:S(2)}, u32[]{:S(2)}) async-start(bf16[8,672,256]{2,1,0:T(8,128)(2,1)} %broadcast_in_dim.109), calls=%async_computation.3 | async-start | bytes 5505024 | tf_op jit(solution)/shard_map/all_to_all | solution.py:60
  85.2 5.3 %collective-permute-start.4 = (bf16[672,256]{1,0:T(8,128)(2,1)S(1)}, bf16[672,256]{1,0:T(8,128)(2,1)S(1)}, u32[]{:S(2)}, u32[]{:S(2)}) collective-permute-start(bf16[672,256]{1,0:T(8,128)(2,1)S(1)} %fusion.28), channel_id=1, source_target_pairs={{0,0},{1,128},{128,1},{129,129},{2,2},{3,130},{130,3},{131,131},{4... | collective-permute-start | bytes 1032200 | tf_op jit(solution)/shard_map/ppermute | solution.py:33
  90.5 31.3 %collective-permute-done.4 = bf16[672,256]{1,0:T(8,128)(2,1)S(1)} collective-permute-done((bf16[672,256]{1,0:T(8,128)(2,1)S(1)}, bf16[672,256]{1,0:T(8,128)(2,1)S(1)}, u32[]{:S(2)}, u32[]{:S(2)}) %collective-permute-start.4) | collective-permute-done | bytes 344096 | tf_op jit(solution)/shard_map/ppermute | solution.py:33
  121.8 2.2 %collective-permute-start.5 = (bf16[16,2,144,512]{3,2,1,0:T(8,128)(2,1)}, bf16[16,2,144,512]{3,2,1,0:T(8,128)(2,1)}, u32[]{:S(2)}, u32[]{:S(2)}) collective-permute-start(bf16[16,2,144,512]{3,2,1,0:T(8,128)(2,1)} %bitcast.75), channel_id=1, source_target_pairs={{0,1},{1,0},{2,3},{3,2},{4,5},{5,4},{6,7},{7,6},{8,9},{9,8},{10,11... | collective-permute-start | bytes 14155784 | tf_op jit(solution)/shard_map/ppermute | solution.py:403
  124.0 4.2 %reshape.364.gain_ref = f32[8,672,1]{2,1,0:T(8,128)} reshape(f32[5376]{0:T(1024)S(1)} %copy-done.6) | data formatting | bytes 43008 | tf_op jit(solution)/shard_map/reshape | solution.py:408
  129.1 1.8 copy-done.1
  130.8 2.3 %copy-done.2 = bf16[32,144,512]{2,1,0:T(8,128)(2,1)S(1)} copy-done((bf16[32,144,512]{2,1,0:T(8,128)(2,1)S(1)}, bf16[32,144,512]{2,1,0:T(8,128)(2,1)}, u32[]{:S(2)}) %copy-start.2) | copy-done | bytes 4718616
  133.2 4.0 %shard_map.136 = (f32[256,512]{1,0:T(8,128)S(1)}, f32[1,256]{1,0:T(1,128)S(1)}) custom-call(s32[1]{0:T(128)} %bitcast.9.core_ref, bf16[8,672,256]{2,1,0:T(8,128)(2,1)} %all-to-all-done.3.whole_ref, f32[8,672,1]{2,1,0:T(8,128)S(1)} %copy-done.1, bf16[16,2,144,512]{3,2,1,0:T(8,128)(2,1)S(1)} %bitcast.76), custom_call_target="tpu_custom_call" | custom-call | flops 704643072 | bytes 5242880 | tf_op jit(solution)/shard_map/pallas_call | solution.py:176
  137.2 5.0 %shard_map.137 = (bf16[256,256]{1,0:T(8,128)(2,1)S(1)}, bf16[256,256]{1,0:T(8,128)(2,1)S(1)}) custom-call(s32[1]{0:T(128)} %bitcast.9.core_ref, bf16[8,672,256]{2,1,0:T(8,128)(2,1)} %all-to-all-done.3.whole_ref, f32[8,672,1]{2,1,0:T(8,128)S(1)} %copy-done.1, bf16[16,2,144,512]{3,2,1,0:T(8,128)(2,1)} %collective-permute-done.5.weight_ref.across_ref, ...), custom_call_target="tpu_custom_call" | custom-call | flops 704643072 | bytes 5242880 | tf_op jit(solution)/shard_map/pallas_call | solution.py:201
  142.1 3.7 %collective-permute-start.6 = (bf16[256,256]{1,0:T(8,128)(2,1)S(1)}, bf16[256,256]{1,0:T(8,128)(2,1)S(1)}, u32[]{:S(2)}, u32[]{:S(2)}) collective-permute-start(bf16[256,256]{1,0:T(8,128)(2,1)S(1)} %get-tuple-element.27), channel_id=1, source_target_pairs={{0,16},{8,24},{16,32},{24,40},{32,48},{40,56},{48,64},{56,72},{64,... | collective-permute-start | bytes 393224 | tf_op jit(solution)/shard_map/ppermute | solution.py:55
  145.8 3.2 %collective-permute-start.7 = (bf16[256,256]{1,0:T(8,128)(2,1)S(1)}, bf16[256,256]{1,0:T(8,128)(2,1)S(1)}, u32[]{:S(2)}, u32[]{:S(2)}) collective-permute-start(bf16[256,256]{1,0:T(8,128)(2,1)S(1)} %get-tuple-element.27), channel_id=1, source_target_pairs={{0,8},{8,16},{16,24},{24,32},{32,40},{40,48},{48,56},{56,64},{64,7... | collective-permute-start | bytes 393224 | tf_op jit(solution)/shard_map/ppermute | solution.py:55
  149.1 1.6 collective-permute-done.6
  150.6 6.6 %collective-permute-done.7 = bf16[256,256]{1,0:T(8,128)(2,1)S(1)} collective-permute-done((bf16[256,256]{1,0:T(8,128)(2,1)S(1)}, bf16[256,256]{1,0:T(8,128)(2,1)S(1)}, u32[]{:S(2)}, u32[]{:S(2)}) %collective-permute-start.7) | collective-permute-done | bytes 131104 | tf_op jit(solution)/shard_map/ppermute | solution.py:55
  157.3 2.4 %collective-permute-start.8 = (bf16[512,256]{1,0:T(8,128)(2,1)S(1)}, bf16[512,256]{1,0:T(8,128)(2,1)S(1)}, u32[]{:S(2)}, u32[]{:S(2)}) collective-permute-start(bf16[512,256]{1,0:T(8,128)(2,1)S(1)} %pad_maximum_fusion.1), channel_id=1, source_target_pairs={{0,16},{8,24},{16,32},{24,40},{32,48},{40,56},{48,64},{56,72},{64,... | collective-permute-start | bytes 786440 | tf_op jit(solution)/shard_map/ppermute | solution.py:55
  161.2 3.2 %collective-permute-start.9 = (bf16[256,256]{1,0:T(8,128)(2,1)S(1)}, bf16[256,256]{1,0:T(8,128)(2,1)S(1)}, u32[]{:S(2)}, u32[]{:S(2)}) collective-permute-start(bf16[256,256]{1,0:T(8,128)(2,1)S(1)} %get-tuple-element.27), channel_id=1, source_target_pairs={{8,0},{16,8},{24,16},{32,24},{40,32},{48,40},{56,48},{64,56},{72,6... | collective-permute-start | bytes 393224 | tf_op jit(solution)/shard_map/ppermute | solution.py:55
  164.4 10.7 %collective-permute-done.8 = bf16[512,256]{1,0:T(8,128)(2,1)S(1)} collective-permute-done((bf16[512,256]{1,0:T(8,128)(2,1)S(1)}, bf16[512,256]{1,0:T(8,128)(2,1)S(1)}, u32[]{:S(2)}, u32[]{:S(2)}) %collective-permute-start.8) | collective-permute-done | bytes 262176 | tf_op jit(solution)/shard_map/ppermute | solution.py:55
  176.9 17.3 %all_to_all.31.own_ref.other_ref = bf16[8,256,256]{2,1,0:T(8,128)(2,1)S(1)} all-to-all(bf16[8,256,256]{2,1,0:T(8,128)(2,1)S(1)} %broadcast_in_dim.191), channel_id=1, replica_groups=mesh['k'=2,'a'=2,'z'=16,'y'=4,'core'=2] {'y','a'}, dimensions={0} | all-to-all | bytes 2097152 | tf_op jit(solution)/shard_map/all_to_all | solution.py:60
  194.3 3.7 %shard_map.138 = (f32[672,256]{1,0:T(8,128)S(1)}, f32[1,256]{1,0:T(1,128)S(1)}) custom-call(s32[1]{0:T(128)} %bitcast.9.core_ref, bf16[8,256,256]{2,1,0:T(8,128)(2,1)S(1)} %all_to_all.31.own_ref.other_ref, bf16[8,256,256]{2,1,0:T(8,128)(2,1)S(1)} %all_to_all.31.own_ref.other_ref, bf16[16,2,144,512]{3,2,1,0:T(8,128)(2,1)S(1)} %bitcast.79, ...), custom_call_target="tpu_custom_call" | custom-call | flops 805306368 | bytes 5242880 | tf_op jit(solution)/shard_map/pallas_call | solution.py:269
  198.0 1.9 collective-permute-start.10
  200.5 4.0 %all-to-all-start.5 = ((f32[16,1,256]{2,1,0:T(1,128)}), f32[16,1,256]{2,1,0:T(1,128)S(1)}, u32[]{:S(2)}, u32[]{:S(2)}) async-start(f32[16,1,256]{2,1,0:T(1,128)} %broadcast_in_dim.196), calls=%async_computation.5 | async-start | bytes 32768 | tf_op jit(solution)/shard_map/all_to_all | solution.py:60
  204.6 5.7 %all-to-all-done.5 = f32[16,1,256]{2,1,0:T(1,128)S(1)} async-done(((f32[16,1,256]{2,1,0:T(1,128)}), f32[16,1,256]{2,1,0:T(1,128)S(1)}, u32[]{:S(2)}, u32[]{:S(2)}) %all-to-all-start.5) | async-done | bytes 16416 | tf_op jit(solution)/shard_map/all_to_all | solution.py:60
  (102 shorter events, 13.1 us)
Async XLA Ops:
  6.5 2.3 %copy-start = (bf16[8,64,1152]{2,1,0:T(8,128)(2,1)S(1)}, bf16[8,64,1152]{2,1,0:T(8,128)(2,1)}, u32[]{:S(2)}) copy-start(bf16[8,64,1152]{2,1,0:T(8,128)(2,1)} %param.15) | copy-start | bytes 3538948
  6.5 19.3 %slice-start.2 = ((bf16[32,672]{1,0:T(8,128)(2,1)}), bf16[32,160]{1,0:T(8,128)(2,1)S(1)}, s32[]{:S(2)}) async-start(bf16[32,672]{1,0:T(8,128)(2,1)} %param.26), calls=%async_computation.9 | async-start | bytes 32768 | tf_op jit(solution)/shard_map/slice | solution.py:319
  6.5 19.4 %slice-start.3 = ((bf16[32,672]{1,0:T(8,128)(2,1)}), bf16[32,512]{1,0:T(8,128)(2,1)S(1)}, s32[]{:S(2)}) async-start(bf16[32,672]{1,0:T(8,128)(2,1)} %param.26), calls=%async_computation.10 | async-start | bytes 65536 | tf_op jit(solution)/shard_map/slice | solution.py:326
  6.5 19.4 %copy-start.5 = (bf16[84,256]{1,0:T(8,128)(2,1)S(1)}, bf16[84,256]{1,0:T(8,128)(2,1)}, u32[]{:S(2)}) copy-start(bf16[84,256]{1,0:T(8,128)(2,1)} %param.21) | copy-start | bytes 129028
  6.5 19.4 %copy-start.8 = (bf16[84,128]{1,0:T(8,128)(2,1)S(1)}, bf16[84,128]{1,0:T(8,128)(2,1)}, u32[]{:S(2)}) copy-start(bf16[84,128]{1,0:T(8,128)(2,1)} %param.22) | copy-start | bytes 64516
  6.5 19.4 %copy-start.7 = (bf16[84,128]{1,0:T(8,128)(2,1)S(1)}, bf16[84,128]{1,0:T(8,128)(2,1)}, u32[]{:S(2)}) copy-start(bf16[84,128]{1,0:T(8,128)(2,1)} %param.23) | copy-start | bytes 64516
  6.6 26.6 %copy-start.12 = (bf16[256,672]{0,1:T(8,128)(2,1)S(1)}, bf16[256,672]{0,1:T(8,128)(2,1)}, u32[]{:S(2)}) copy-start(bf16[256,672]{0,1:T(8,128)(2,1)} %param.14) | copy-start | bytes 1032196
  6.6 35.5 %collective-permute-start.3 = (bf16[1152,672]{0,1:T(8,128)(2,1)}, bf16[1152,672]{0,1:T(8,128)(2,1)}, u32[]{:S(2)}, u32[]{:S(2)}) collective-permute-start(bf16[1152,672]{0,1:T(8,128)(2,1)} %param.19), channel_id=1, source_target_pairs={{0,1},{129,128},{2,3},{131,130},{4,5},{133,132},{6,7},{135,134},{8... | collective-permute-start | bytes 4644872 | tf_op jit(solution)/shard_map/ppermute | solution.py:361
  9.2 32.9 %copy-start.9 = (s32[8]{0:T(128)S(1)}, s32[8]{0:T(128)}, u32[]{:S(2)}) copy-start(s32[8]{0:T(128)} %param.16) | copy-start | bytes 100
  9.2 32.9 %copy-start.11 = (s32[8]{0:T(128)S(1)}, s32[8]{0:T(128)}, u32[]{:S(2)}) copy-start(s32[8]{0:T(128)} %param.17) | copy-start | bytes 100
  10.1 31.9 %all-to-all-start = ((bf16[16,32,144]{2,1,0:T(8,128)(2,1)}), bf16[16,32,144]{2,1,0:T(8,128)(2,1)S(1)}, u32[]{:S(2)}, u32[]{:S(2)}) async-start(bf16[16,32,144]{2,1,0:T(8,128)(2,1)} %broadcast_in_dim.100), calls=%async_computation | async-start | bytes 524288 | tf_op jit(solution)/shard_map/all_to_all | solution.py:60
  25.8 96.0 %all-gather.3.cloned.1.call-start = ((), (), s32[]{:S(2)}) async-start(), calls=%async_computation.6 | async-start | bytes 5013504 | tf_op jit(solution)/shard_map/all_gather | solution.py:366
  26.0 10.2 %collective-permute-start = (bf16[144,512]{1,0:T(8,128)(2,1)S(1)}, bf16[144,512]{1,0:T(8,128)(2,1)S(1)}, u32[]{:S(2)}, u32[]{:S(2)}) collective-permute-start(bf16[144,512]{1,0:T(8,128)(2,1)S(1)} %maximum_maximum_fusion), channel_id=1, source_target_pairs={{0,0},{1,128},{128,1},{129,129},{256,256},{257,384},{384,257},{385... | collective-permute-start | bytes 442376 | tf_op jit(solution)/shard_map/ppermute | solution.py:42
  30.0 9.0 %collective-permute-start.1 = (bf16[144,512]{1,0:T(8,128)(2,1)S(1)}, bf16[144,512]{1,0:T(8,128)(2,1)S(1)}, u32[]{:S(2)}, u32[]{:S(2)}) collective-permute-start(bf16[144,512]{1,0:T(8,128)(2,1)S(1)} %maximum_maximum_fusion), channel_id=1, source_target_pairs={{0,256},{1,384},{128,257},{129,385},{256,0},{257,128},{384,1},{385... | collective-permute-start | bytes 442376 | tf_op jit(solution)/shard_map/ppermute | solution.py:42
  33.2 8.9 %collective-permute-start.2 = (bf16[256,672]{0,1:T(8,128)(2,1)S(1)}, bf16[256,672]{0,1:T(8,128)(2,1)S(1)}, u32[]{:S(2)}, u32[]{:S(2)}) collective-permute-start(bf16[256,672]{0,1:T(8,128)(2,1)S(1)} %copy-done.12), channel_id=1, source_target_pairs={{0,0},{1,128},{128,1},{129,129},{2,2},{3,130},{130,3},{131,131},{4... | collective-permute-start | bytes 1032200 | tf_op jit(solution)/shard_map/ppermute | solution.py:33
  62.8 14.0 %all-to-all-start.2 = ((bf16[8,144,256]{2,1,0:T(8,128)(2,1)}), bf16[8,144,256]{2,1,0:T(8,128)(2,1)S(1)}, u32[]{:S(2)}, u32[]{:S(2)}) async-start(bf16[8,144,256]{2,1,0:T(8,128)(2,1)} %broadcast_in_dim.108), calls=%async_computation.2 | async-start | bytes 1179648 | tf_op jit(solution)/shard_map/all_to_all | solution.py:60
  80.6 43.4 %copy-start.6 = (f32[5376]{0:T(1024)S(1)}, f32[5376]{0:T(1024)}, u32[]{:S(2)}) copy-start(f32[5376]{0:T(1024)} %param.20) | copy-start | bytes 64516
  80.6 41.2 %all-to-all-start.3 = ((bf16[8,672,256]{2,1,0:T(8,128)(2,1)}), bf16[8,672,256]{2,1,0:T(8,128)(2,1)}, u32[]{:S(2)}, u32[]{:S(2)}) async-start(bf16[8,672,256]{2,1,0:T(8,128)(2,1)} %broadcast_in_dim.109), calls=%async_computation.3 | async-start | bytes 5505024 | tf_op jit(solution)/shard_map/all_to_all | solution.py:60
  85.2 36.6 %collective-permute-start.4 = (bf16[672,256]{1,0:T(8,128)(2,1)S(1)}, bf16[672,256]{1,0:T(8,128)(2,1)S(1)}, u32[]{:S(2)}, u32[]{:S(2)}) collective-permute-start(bf16[672,256]{1,0:T(8,128)(2,1)S(1)} %fusion.28), channel_id=1, source_target_pairs={{0,0},{1,128},{128,1},{129,129},{2,2},{3,130},{130,3},{131,131},{4... | collective-permute-start | bytes 1032200 | tf_op jit(solution)/shard_map/ppermute | solution.py:33
  121.8 15.4 %collective-permute-start.5 = (bf16[16,2,144,512]{3,2,1,0:T(8,128)(2,1)}, bf16[16,2,144,512]{3,2,1,0:T(8,128)(2,1)}, u32[]{:S(2)}, u32[]{:S(2)}) collective-permute-start(bf16[16,2,144,512]{3,2,1,0:T(8,128)(2,1)} %bitcast.75), channel_id=1, source_target_pairs={{0,1},{1,0},{2,3},{3,2},{4,5},{5,4},{6,7},{7,6},{8,9},{9,8},{10,11... | collective-permute-start | bytes 14155784 | tf_op jit(solution)/shard_map/ppermute | solution.py:403
  130.8 2.3 %copy-start.2 = (bf16[32,144,512]{2,1,0:T(8,128)(2,1)S(1)}, bf16[32,144,512]{2,1,0:T(8,128)(2,1)}, u32[]{:S(2)}) copy-start(bf16[32,144,512]{2,1,0:T(8,128)(2,1)} %all-gather.3.cloned.1.call-done) | copy-start | bytes 14155780
  133.2 4.0 %copy-start.3 = (f32[128]{0:T(128)S(1)}, f32[128]{0:T(128)}, u32[]{:S(2)}) copy-start(f32[128]{0:T(128)} %param.24) | copy-start | bytes 1540
  133.2 4.0 %copy-start.4 = (f32[128]{0:T(128)S(1)}, f32[128]{0:T(128)}, u32[]{:S(2)}) copy-start(f32[128]{0:T(128)} %param.25) | copy-start | bytes 1540
  142.1 8.5 %collective-permute-start.6 = (bf16[256,256]{1,0:T(8,128)(2,1)S(1)}, bf16[256,256]{1,0:T(8,128)(2,1)S(1)}, u32[]{:S(2)}, u32[]{:S(2)}) collective-permute-start(bf16[256,256]{1,0:T(8,128)(2,1)S(1)} %get-tuple-element.27), channel_id=1, source_target_pairs={{0,16},{8,24},{16,32},{24,40},{32,48},{40,56},{48,64},{56,72},{64,... | collective-permute-start | bytes 393224 | tf_op jit(solution)/shard_map/ppermute | solution.py:55
  145.8 11.4 %collective-permute-start.7 = (bf16[256,256]{1,0:T(8,128)(2,1)S(1)}, bf16[256,256]{1,0:T(8,128)(2,1)S(1)}, u32[]{:S(2)}, u32[]{:S(2)}) collective-permute-start(bf16[256,256]{1,0:T(8,128)(2,1)S(1)} %get-tuple-element.27), channel_id=1, source_target_pairs={{0,8},{8,16},{16,24},{24,32},{32,40},{40,48},{48,56},{56,64},{64,7... | collective-permute-start | bytes 393224 | tf_op jit(solution)/shard_map/ppermute | solution.py:55
  157.3 17.8 %collective-permute-start.8 = (bf16[512,256]{1,0:T(8,128)(2,1)S(1)}, bf16[512,256]{1,0:T(8,128)(2,1)S(1)}, u32[]{:S(2)}, u32[]{:S(2)}) collective-permute-start(bf16[512,256]{1,0:T(8,128)(2,1)S(1)} %pad_maximum_fusion.1), channel_id=1, source_target_pairs={{0,16},{8,24},{16,32},{24,40},{32,48},{40,56},{48,64},{56,72},{64,... | collective-permute-start | bytes 786440 | tf_op jit(solution)/shard_map/ppermute | solution.py:55
  161.2 14.0 %collective-permute-start.9 = (bf16[256,256]{1,0:T(8,128)(2,1)S(1)}, bf16[256,256]{1,0:T(8,128)(2,1)S(1)}, u32[]{:S(2)}, u32[]{:S(2)}) collective-permute-start(bf16[256,256]{1,0:T(8,128)(2,1)S(1)} %get-tuple-element.27), channel_id=1, source_target_pairs={{8,0},{16,8},{24,16},{32,24},{40,32},{48,40},{56,48},{64,56},{72,6... | collective-permute-start | bytes 393224 | tf_op jit(solution)/shard_map/ppermute | solution.py:55
  175.2 19.1 %slice-start = ((s8[4718592]{0:T(1024)(128)(4,1)}), s8[4194304]{0:T(1024)(128)(4,1)S(1)}, s32[]{:S(2)}) async-start(s8[4718592]{0:T(1024)(128)(4,1)} %bitcast.77), calls=%async_computation.7 | async-start | bytes 8388608
  175.7 18.5 %slice-start.1 = ((s8[4718592]{0:T(1024)(128)(4,1)}), s8[524288]{0:T(1024)(128)(4,1)S(1)}, s32[]{:S(2)}) async-start(s8[4718592]{0:T(1024)(128)(4,1)} %bitcast.77), calls=%async_computation.8 | async-start | bytes 1048576
  194.3 16.1 %copy-start.10 = (f32[672]{0:T(1024)S(1)}, f32[672]{0:T(1024)}, u32[]{:S(2)}) copy-start(f32[672]{0:T(1024)} %param.27) | copy-start | bytes 8068
  198.0 12.4 %collective-permute-start.10 = (bf16[672,256]{1,0:T(8,128)(2,1)S(1)}, bf16[672,256]{1,0:T(8,128)(2,1)S(1)}, u32[]{:S(2)}, u32[]{:S(2)}) collective-permute-start(bf16[672,256]{1,0:T(8,128)(2,1)S(1)} %convert_element_type.53), channel_id=1, source_target_pairs={{0,0},{1,128},{128,1},{129,129},{2,2},{3,130},{130,3},{131,131},{4... | collective-permute-start | bytes 1032200 | tf_op jit(solution)/shard_map/ppermute | solution.py:33
  200.5 9.8 %all-to-all-start.5 = ((f32[16,1,256]{2,1,0:T(1,128)}), f32[16,1,256]{2,1,0:T(1,128)S(1)}, u32[]{:S(2)}, u32[]{:S(2)}) async-start(f32[16,1,256]{2,1,0:T(1,128)} %broadcast_in_dim.196), calls=%async_computation.5 | async-start | bytes 32768 | tf_op jit(solution)/shard_map/all_to_all | solution.py:60
  (1 other events, 1.8 us)
Sparse Core Ops, SparseCore 0:
  42.2 71.5 all-gather.2

commit v7 on v6

--- a/solution.py
+++ b/solution.py
@@ -100,7 +100,8 @@
     for shard in range(8):
         block[shard * ROWS_IN : (shard + 1) * ROWS_IN, :] = weight_ref[shard, 0, :ROWS_IN, :]
     part = whole_ref[0].astype(jnp.float32)
-    scaled = (part * gain_ref[0]).astype(jnp.bfloat16)
+    gain = jnp.concatenate([gain_ref[0], gain_ref[0]], axis=1)
+    scaled = (part * gain).astype(jnp.bfloat16)
     product = lax.dot_general(
         scaled, block[...], (((0,), (0,)), ((), ())), preferred_element_type=jnp.float32
     )
@@ -165,7 +166,7 @@
 def qkv_specs(block_of, width, rows):
     return [
         pl.BlockSpec((1, width, rows), lambda step, core: (block_of(step, core), 0, 0)),
-        pl.BlockSpec((1, width, 1), lambda step, core: (block_of(step, core), 0, 0)),
+        pl.BlockSpec((1, width, HEAD_DIM), lambda step, core: (block_of(step, core), 0, 0)),
         pl.BlockSpec((8, 1, PAD_IN, 512), lambda step, core: (step % 2, step // 2, 0, 0)),
     ]
 
@@ -256,8 +257,9 @@
     @pl.when(step == pl.num_programs(0) - 1)
     def _():
         result = total[:WIDTH, :]
-        result_ref[...] = result
-        squares_ref[...] = jnp.sum(result * result, axis=0, keepdims=True)
+        result_ref[...] = result.astype(jnp.bfloat16)
+        squares = jnp.sum(result * result, axis=0, keepdims=True)
+        squares_ref[...] = jnp.broadcast_to(squares[None], squares_ref.shape)
 
 
 def project_out(core, heads, along, across):
@@ -277,12 +279,15 @@
                 weights,
                 weights,
             ],
-            out_specs=[pl.BlockSpec((WIDTH, rows), fixed), pl.BlockSpec((1, rows), fixed)],
+            out_specs=[
+                pl.BlockSpec((WIDTH, rows), fixed),
+                pl.BlockSpec((16, 1, rows), lambda step, core: (0, 0, 0)),
+            ],
             scratch_shapes=[pltpu.VMEM((768, rows), jnp.float32)],
         ),
         out_shape=[
-            jax.ShapeDtypeStruct((WIDTH, rows), jnp.float32),
-            jax.ShapeDtypeStruct((1, rows), jnp.float32),
+            jax.ShapeDtypeStruct((WIDTH, rows), jnp.bfloat16),
+            jax.ShapeDtypeStruct((16, 1, rows), jnp.float32),
         ],
         compiler_params=pltpu.CompilerParams(vmem_limit_bytes=24 * 2**20),
         cost_estimate=pl.CostEstimate(
@@ -357,14 +362,6 @@
     soft_part = lax.dynamic_slice_in_dim(
         soft, lax.axis_index(GIVEN_HEAD) * vis_part, vis_part, 1
     )
-    soft_z = exchange(soft_part, "z", Z).reshape(Z * block_rows, vis_part)
-    proj_other = lax.ppermute(proj_weight, ("a", "core"), [(0, 1), (3, 2)])
-    tokens = swapped(tokens)
-    soft_z, both, tokens, proj_other = lax.optimization_barrier(
-        (soft_z, both, tokens, proj_other)
-    )
-    along = lax.all_gather(both, "z", axis=0)
-    proj_weight = jnp.where(core_index == lax.axis_index("a"), proj_weight, proj_other)
     target = jnp.arange(8, dtype=jnp.int32)
     target_k, target_a, target_core = target // 4, target // 2 % 2, target % 2
     target_seq = (target_k * 2 + target_core) * Z + z_index
@@ -381,6 +378,14 @@
     frame_row = jnp.where(wanted, frame_row + frame_pos, -1)
     x_index = lax.axis_index(("k", "a"))
     here = x_index * (Z * block_rows) + jnp.arange(Z * block_rows, dtype=jnp.int32)
+    soft_z = exchange(soft_part, "z", Z).reshape(Z * block_rows, vis_part)
+    tokens = swapped(tokens)
+    soft_z, both, tokens, proj_weight = lax.optimization_barrier(
+        (soft_z, both, tokens, proj_weight)
+    )
+    along = lax.all_gather(both, "z", axis=0)
+    proj_other = lax.ppermute(proj_weight, ("a", "core"), [(0, 1), (3, 2)])
+    proj_weight = jnp.where(core_index == lax.axis_index("a"), proj_weight, proj_other)
     chosen = (frame_row[:, None] == here[None, :]).astype(jnp.bfloat16)
     chosen = chosen.reshape(8, tok_rows, Z * block_rows)
     frames = jnp.einsum("sk,xps->xkp", soft_z, chosen, preferred_element_type=jnp.float32)
@@ -389,6 +394,10 @@
     )
     mine = jnp.sum(frames.astype(jnp.float32), axis=0).astype(jnp.bfloat16)
     soft_rows = exchange(mine, HEAD, head_count).reshape(vis, tok_rows)
+    gain_parts = jnp.broadcast_to(
+        input_gain.reshape(head_count, width, 1), (head_count, width, HEAD_DIM)
+    )
+    soft_rows, gain_parts = lax.optimization_barrier((soft_rows, gain_parts))
     embedded = lax.dot_general(
         proj_weight, soft_rows, (((0,), (0,)), ((), ())),
         preferred_element_type=jnp.float32,
@@ -398,14 +407,12 @@
     residual = jnp.where((my_image >= 0)[None, :], embedded, tokens.T)
 
     whole = exchange(residual, HEAD, head_count)
-    given_residual = swapped(residual)
-    along, whole, given_residual = lax.optimization_barrier((along, whole, given_residual))
+    along, whole = lax.optimization_barrier((along, whole))
     across = lax.ppermute(along, "core", [(0, 1), (1, 0)])
     half = HEAD_DIM // 2
     frequency = ROPE_BASE ** (-jnp.arange(half, dtype=jnp.float32) * 2.0 / HEAD_DIM)
     angles = my_pos.astype(jnp.float32)[:, None] * frequency[None, :]
     cosine, sine = jnp.cos(angles), jnp.sin(angles)
-    gain_parts = input_gain.reshape(head_count, width, 1)
     total, row_squares = project_first(core, whole, gain_parts, along)
     queries, own = project_second(
         core,
@@ -431,10 +438,13 @@
         allowed,
     )
     attended = attended.reshape(tok_rows, 2 * HEAD_DIM).T
+    attended, residual = lax.optimization_barrier((attended, residual))
+    given_residual = swapped(residual)
     heads_all = exchange(attended, HEAD, head_count)
     projected, squares = project_out(core, heads_all, along, across)
-    given = swapped(projected.astype(jnp.bfloat16)).astype(jnp.float32)
-    all_squares = exchange(squares, ("a", "y", "core"), 16).reshape(8, 2, tok_rows)
+    given = swapped(projected).astype(jnp.float32)
+    all_squares = lax.all_to_all(squares, ("a", "y", "core"), 0, 0, tiled=True)
+    all_squares = all_squares.reshape(8, 2, tok_rows)
     from_core = jnp.arange(2, dtype=jnp.int32) == lax.axis_index("a")
     squares = jnp.sum(jnp.where(from_core[None, :, None], all_squares, 0.0), axis=(0, 1))
     post = given * lax.rsqrt(squares[None, :] / D + EPSILON) * post_gain[:, None]

time: 219 us -> 219 us (level)
  waiting for transfers between devices: 70.6 us -> 48.2 us
  blocking collectives: 35.3 us -> 54.9 us
  local copies, waits for them, and re-layouts: 13.3 us -> 15.5 us
    ppermute x3, waiting for transfers between devices: 33.6 us -> 3.1 us  [swapped(): return lax.ppermute(value, ('a', 'core'), [(0, 0), (1, 2), (2, 1), (3, 3)])]
    all_to_all x1, blocking collectives: 17.3 us -> 35.9 us  [exchange(): return lax.all_to_all(spread, axes, 0, 0, tiled=True)]
    all_to_all x4 -> x3, waiting for transfers between devices: 15.4 us -> 22.2 us  [exchange(): return lax.all_to_all(spread, axes, 0, 0, tiled=True)]
    all_to_all x0 -> x1, waiting for transfers between devices: none -> 5.45 us  [body(): all_squares = lax.all_to_all(squares, ('a', 'y', 'core'), 0, 0, tiled=True)]
    unnamed x35, local copies, waits for them, and re-layouts: 4.22 us -> 9.6 us
    all_to_all x4 -> x3, starting transfers between devices: 28.5 us -> 24 us  [exchange(): return lax.all_to_all(spread, axes, 0, 0, tiled=True)]
    reshape x1 -> x0, local copies, waits for them, and re-layouts: 4.17 us -> none  [body(): gain_parts = input_gain.reshape(head_count, width, 1)]
    ppermute x4, waiting for transfers between devices: 18.9 us -> 15.3 us  [shifted(): return lax.ppermute(value, ('k', 'z', 'core'), pairs)]
  transfers between devices with their start and end apart: 16 -> 16, of which waited for: 8 -> 8; matrix products, arithmetic and copies ran while one was open for 8% -> 5% of each run, Pallas kernels for 2% -> 3%
where the time goes in v7:
time: 219 us; the launch traced here: 217 us
  starting transfers between devices  63.9 us (29%)
  blocking collectives  54.9 us (25%)
  waiting for transfers between devices  48.2 us (22%)
  local copies, waits for them, and re-layouts  15.5 us (7%)
  between operations  14 us (6%)
  Pallas kernels  10.5 us (5%)
  other arithmetic  5.23 us (2%)
  matrix products  5.03 us (2%)
    all_to_all x1, blocking collectives, exchange(): return lax.all_to_all(spread, axes, 0, 0, tiled=True)  35.9 us
    all_to_all x3, starting transfers between devices, exchange(): return lax.all_to_all(spread, axes, 0, 0, tiled=True)  24 us
    all_to_all x3, waiting for transfers between devices, exchange(): return lax.all_to_all(spread, axes, 0, 0, tiled=True)  22.2 us
    all_to_all x1, blocking collectives, body(): lax.all_to_all(frames.astype(jnp.bfloat16), ('k', 'a', 'core'), 0, 0, til...  19 us
    ppermute x4, waiting for transfers between devices, shifted(): return lax.ppermute(value, ('k', 'z', 'core'), pairs)  15.3 us
    ppermute x4, starting transfers between devices, shifted(): return lax.ppermute(value, ('k', 'z', 'core'), pairs)  14 us
    unnamed x35, local copies, waits for them, and re-layouts  9.6 us
    ppermute x3, starting transfers between devices, swapped(): return lax.ppermute(value, ('a', 'core'), [(0, 0), (1, 2), (2, 1), (3, 3)])  9.53 us
  transfers between devices with their start and end apart: 16, of which 8 were waited for; matrix products, arithmetic and copies ran while one was open for 5% of the time, Pallas kernels for 3%

profile of v7, /device:TPU:1, one launch (start us, length us, event | category | flops | bytes accessed | tf_op | source)
XLA Modules:
  0.0 217.2 jit_solution(521688083652154508)
XLA Ops:
  10.0 15.7 %all-to-all-start = ((bf16[16,32,144]{2,1,0:T(8,128)(2,1)}), bf16[16,32,144]{2,1,0:T(8,128)(2,1)S(1)}, u32[]{:S(2)}, u32[]{:S(2)}) async-start(bf16[16,32,144]{2,1,0:T(8,128)(2,1)} %broadcast_in_dim.101), calls=%async_computation | async-start | bytes 524288 | tf_op jit(solution)/shard_map/all_to_all | solution.py:60
  25.9 4.0 %collective-permute-start = (bf16[144,512]{1,0:T(8,128)(2,1)S(1)}, bf16[144,512]{1,0:T(8,128)(2,1)S(1)}, u32[]{:S(2)}, u32[]{:S(2)}) collective-permute-start(bf16[144,512]{1,0:T(8,128)(2,1)S(1)} %maximum_maximum_fusion), channel_id=1, source_target_pairs={{0,0},{1,128},{128,1},{129,129},{256,256},{257,384},{384,257},{385... | collective-permute-start | bytes 442376 | tf_op jit(solution)/shard_map/ppermute | solution.py:42
  29.9 3.2 %collective-permute-start.1 = (bf16[144,512]{1,0:T(8,128)(2,1)S(1)}, bf16[144,512]{1,0:T(8,128)(2,1)S(1)}, u32[]{:S(2)}, u32[]{:S(2)}) collective-permute-start(bf16[144,512]{1,0:T(8,128)(2,1)S(1)} %maximum_maximum_fusion), channel_id=1, source_target_pairs={{0,256},{1,384},{128,257},{129,385},{256,0},{257,128},{384,1},{385... | collective-permute-start | bytes 442376 | tf_op jit(solution)/shard_map/ppermute | solution.py:42
  33.1 3.0 %collective-permute-start.2 = (bf16[256,672]{0,1:T(8,128)(2,1)}, bf16[256,672]{0,1:T(8,128)(2,1)}, u32[]{:S(2)}, u32[]{:S(2)}) collective-permute-start(bf16[256,672]{0,1:T(8,128)(2,1)} %param.14), channel_id=1, source_target_pairs={{0,0},{1,128},{128,1},{129,129},{2,2},{3,130},{130,3},{131,131},{4... | collective-permute-start | bytes 1032200 | tf_op jit(solution)/shard_map/ppermute | solution.py:33
  36.2 2.1 collective-permute-done.1
  39.1 3.1 %collective-permute-done.2 = bf16[256,672]{0,1:T(8,128)(2,1)} collective-permute-done((bf16[256,672]{0,1:T(8,128)(2,1)}, bf16[256,672]{0,1:T(8,128)(2,1)}, u32[]{:S(2)}, u32[]{:S(2)}) %collective-permute-start.2) | collective-permute-done | bytes 344096 | tf_op jit(solution)/shard_map/ppermute | solution.py:33
  45.3 19.0 %all_to_all.30 = bf16[8,144,256]{2,1,0:T(8,128)(2,1)S(1)} all-to-all(bf16[8,144,256]{2,1,0:T(8,128)(2,1)S(1)} %fusion.19), channel_id=1, replica_groups=mesh['k'=2,'a'=2,'z'=16,'y'=4,'core'=2] {'k','a','core'}, dimensions={0} | all-to-all | bytes 1179648 | tf_op jit(solution)/shard_map/all_to_all | solution.py:392
  65.3 4.5 %all-to-all-start.2 = ((bf16[8,144,256]{2,1,0:T(8,128)(2,1)}), bf16[8,144,256]{2,1,0:T(8,128)(2,1)S(1)}, u32[]{:S(2)}, u32[]{:S(2)}) async-start(bf16[8,144,256]{2,1,0:T(8,128)(2,1)} %broadcast_in_dim.109), calls=%async_computation.2 | async-start | bytes 1179648 | tf_op jit(solution)/shard_map/all_to_all | solution.py:60
  70.0 9.7 %all-to-all-done.2 = bf16[8,144,256]{2,1,0:T(8,128)(2,1)S(1)} async-done(((bf16[8,144,256]{2,1,0:T(8,128)(2,1)}), bf16[8,144,256]{2,1,0:T(8,128)(2,1)S(1)}, u32[]{:S(2)}, u32[]{:S(2)}) %all-to-all-start.2) | async-done | bytes 589856 | tf_op jit(solution)/shard_map/all_to_all | solution.py:60
  79.8 2.0 broadcast_in_dim.115.gain_ref
  81.7 2.1 fusion.28
  84.0 35.9 %all_to_all.31.whole_ref = bf16[8,672,256]{2,1,0:T(8,128)(2,1)} all-to-all(bf16[8,672,256]{2,1,0:T(8,128)(2,1)S(1)} %broadcast_in_dim.116), channel_id=1, replica_groups=mesh['k'=2,'a'=2,'z'=16,'y'=4,'core'=2] {'y','a'}, dimensions={0} | all-to-all | bytes 5505024 | tf_op jit(solution)/shard_map/all_to_all | solution.py:60
  119.8 4.5 %collective-permute-start.4 = (bf16[16,2,144,512]{3,2,1,0:T(8,128)(2,1)}, bf16[16,2,144,512]{3,2,1,0:T(8,128)(2,1)}, u32[]{:S(2)}, u32[]{:S(2)}) collective-permute-start(bf16[16,2,144,512]{3,2,1,0:T(8,128)(2,1)} %bitcast.74), channel_id=1, source_target_pairs={{0,1},{1,0},{2,3},{3,2},{4,5},{5,4},{6,7},{7,6},{8,9},{9,8},{10,11... | collective-permute-start | bytes 14155784 | tf_op jit(solution)/shard_map/ppermute | solution.py:411
  125.3 1.8 copy-done.1
  127.1 1.8 copy-done.2
  128.8 2.3 %copy-done.3 = bf16[32,144,512]{2,1,0:T(8,128)(2,1)S(1)} copy-done((bf16[32,144,512]{2,1,0:T(8,128)(2,1)S(1)}, bf16[32,144,512]{2,1,0:T(8,128)(2,1)}, u32[]{:S(2)}) %copy-start.3) | copy-done | bytes 4718616
  131.2 2.1 shard_map.136
  133.3 4.2 %shard_map.137 = (bf16[256,256]{1,0:T(8,128)(2,1)S(1)}, bf16[256,256]{1,0:T(8,128)(2,1)S(1)}) custom-call(s32[1]{0:T(128)} %bitcast.core_ref, bf16[8,672,256]{2,1,0:T(8,128)(2,1)S(1)} %copy-done.2, f32[8,672,128]{2,1,0:T(8,128)S(1)} %copy-done.1, bf16[16,2,144,512]{3,2,1,0:T(8,128)(2,1)} %collective-permute-done.4.weight_ref.across_ref, ...), custom_call_target="tpu_custom_call" | custom-call | flops 704643072 | bytes 5242880 | tf_op jit(solution)/shard_map/pallas_call | solution.py:202
  137.5 3.6 %collective-permute-start.5 = (bf16[256,256]{1,0:T(8,128)(2,1)S(1)}, bf16[256,256]{1,0:T(8,128)(2,1)S(1)}, u32[]{:S(2)}, u32[]{:S(2)}) collective-permute-start(bf16[256,256]{1,0:T(8,128)(2,1)S(1)} %get-tuple-element.31), channel_id=1, source_target_pairs={{0,16},{8,24},{16,32},{24,40},{32,48},{40,56},{48,64},{56,72},{64,... | collective-permute-start | bytes 393224 | tf_op jit(solution)/shard_map/ppermute | solution.py:55
  141.1 3.4 %collective-permute-start.6 = (bf16[256,256]{1,0:T(8,128)(2,1)S(1)}, bf16[256,256]{1,0:T(8,128)(2,1)S(1)}, u32[]{:S(2)}, u32[]{:S(2)}) collective-permute-start(bf16[256,256]{1,0:T(8,128)(2,1)S(1)} %get-tuple-element.31), channel_id=1, source_target_pairs={{0,8},{8,16},{16,24},{24,32},{32,40},{40,48},{48,56},{56,64},{64,7... | collective-permute-start | bytes 393224 | tf_op jit(solution)/shard_map/ppermute | solution.py:55
  146.0 5.3 %collective-permute-done.6 = bf16[256,256]{1,0:T(8,128)(2,1)S(1)} collective-permute-done((bf16[256,256]{1,0:T(8,128)(2,1)S(1)}, bf16[256,256]{1,0:T(8,128)(2,1)S(1)}, u32[]{:S(2)}, u32[]{:S(2)}) %collective-permute-start.6) | collective-permute-done | bytes 131104 | tf_op jit(solution)/shard_map/ppermute | solution.py:55
  151.3 3.6 %collective-permute-start.7 = (bf16[512,256]{1,0:T(8,128)(2,1)S(1)}, bf16[512,256]{1,0:T(8,128)(2,1)S(1)}, u32[]{:S(2)}, u32[]{:S(2)}) collective-permute-start(bf16[512,256]{1,0:T(8,128)(2,1)S(1)} %pad_maximum_fusion.1), channel_id=1, source_target_pairs={{0,16},{8,24},{16,32},{24,40},{32,48},{40,56},{48,64},{56,72},{64,... | collective-permute-start | bytes 786440 | tf_op jit(solution)/shard_map/ppermute | solution.py:55
  156.4 3.4 %collective-permute-start.8 = (bf16[256,256]{1,0:T(8,128)(2,1)S(1)}, bf16[256,256]{1,0:T(8,128)(2,1)S(1)}, u32[]{:S(2)}, u32[]{:S(2)}) collective-permute-start(bf16[256,256]{1,0:T(8,128)(2,1)S(1)} %get-tuple-element.31), channel_id=1, source_target_pairs={{8,0},{16,8},{24,16},{32,24},{40,32},{48,40},{56,48},{64,56},{72,6... | collective-permute-start | bytes 393224 | tf_op jit(solution)/shard_map/ppermute | solution.py:55
  159.8 8.5 %collective-permute-done.7 = bf16[512,256]{1,0:T(8,128)(2,1)S(1)} collective-permute-done((bf16[512,256]{1,0:T(8,128)(2,1)S(1)}, bf16[512,256]{1,0:T(8,128)(2,1)S(1)}, u32[]{:S(2)}, u32[]{:S(2)}) %collective-permute-start.7) | collective-permute-done | bytes 262176 | tf_op jit(solution)/shard_map/ppermute | solution.py:55
  171.1 3.7 %all-to-all-start.4 = ((bf16[8,256,256]{2,1,0:T(8,128)(2,1)}), bf16[8,256,256]{2,1,0:T(8,128)(2,1)S(1)}, u32[]{:S(2)}, u32[]{:S(2)}) async-start(bf16[8,256,256]{2,1,0:T(8,128)(2,1)} %broadcast_in_dim.192), calls=%async_computation.4 | async-start | bytes 2097152 | tf_op jit(solution)/shard_map/all_to_all | solution.py:60
  174.8 3.5 %collective-permute-start.9 = (bf16[672,256]{1,0:T(8,128)(2,1)S(1)}, bf16[672,256]{1,0:T(8,128)(2,1)S(1)}, u32[]{:S(2)}, u32[]{:S(2)}) collective-permute-start(bf16[672,256]{1,0:T(8,128)(2,1)S(1)} %fusion.28), channel_id=1, source_target_pairs={{0,0},{1,128},{128,1},{129,129},{2,2},{3,130},{130,3},{131,131},{4... | collective-permute-start | bytes 1032200 | tf_op jit(solution)/shard_map/ppermute | solution.py:33
  178.3 12.5 %all-to-all-done.4.own_ref.other_ref = bf16[8,256,256]{2,1,0:T(8,128)(2,1)S(1)} async-done(((bf16[8,256,256]{2,1,0:T(8,128)(2,1)}), bf16[8,256,256]{2,1,0:T(8,128)(2,1)S(1)}, u32[]{:S(2)}, u32[]{:S(2)}) %all-to-all-start.4) | async-done | bytes 1048608 | tf_op jit(solution)/shard_map/all_to_all | solution.py:60
  190.8 2.3 %copy-done.4 = bf16[32,144,512]{2,1,0:T(8,128)(2,1)S(1)} copy-done((bf16[32,144,512]{2,1,0:T(8,128)(2,1)S(1)}, bf16[32,144,512]{2,1,0:T(8,128)(2,1)}, u32[]{:S(2)}) %copy-start.4) | copy-done | bytes 4718616
  193.1 4.2 %shard_map.138 = (bf16[672,256]{1,0:T(8,128)(2,1)S(1)}, f32[16,1,256]{2,1,0:T(1,128)}) custom-call(s32[1]{0:T(128)} %bitcast.core_ref, bf16[8,256,256]{2,1,0:T(8,128)(2,1)S(1)} %all-to-all-done.4.own_ref.other_ref, bf16[8,256,256]{2,1,0:T(8,128)(2,1)S(1)} %all-to-all-done.4.own_ref.other_ref, bf16[16,2,144,512]{3,2,1,0:T(8,128)(2,1)S(1)} %bitcast.76, ...), custom_call_target="tpu_custom_call" | custom-call | flops 805306368 | bytes 5242880 | tf_op jit(solution)/shard_map/pallas_call | solution.py:271
  197.3 3.0 %collective-permute-start.10 = (bf16[672,256]{1,0:T(8,128)(2,1)S(1)}, bf16[672,256]{1,0:T(8,128)(2,1)S(1)}, u32[]{:S(2)}, u32[]{:S(2)}) collective-permute-start(bf16[672,256]{1,0:T(8,128)(2,1)S(1)} %get-tuple-element.35), channel_id=1, source_target_pairs={{0,0},{1,128},{128,1},{129,129},{2,2},{3,130},{130,3},{131,131},{4... | collective-permute-start | bytes 1032200 | tf_op jit(solution)/shard_map/ppermute | solution.py:33
  200.4 3.4 %all-to-all-start.5 = ((f32[16,1,256]{2,1,0:T(1,128)}), f32[16,1,256]{2,1,0:T(1,128)S(1)}, u32[]{:S(2)}, u32[]{:S(2)}) async-start(f32[16,1,256]{2,1,0:T(1,128)} %get-tuple-element.36), calls=%async_computation.5 | async-start | bytes 32768 | tf_op jit(solution)/shard_map/all_to_all | solution.py:446
  203.9 5.5 %all-to-all-done.5 = f32[16,1,256]{2,1,0:T(1,128)S(1)} async-done(((f32[16,1,256]{2,1,0:T(1,128)}), f32[16,1,256]{2,1,0:T(1,128)S(1)}, u32[]{:S(2)}, u32[]{:S(2)}) %all-to-all-start.5) | async-done | bytes 16416 | tf_op jit(solution)/shard_map/all_to_all | solution.py:446
  (100 shorter events, 16.4 us)
Async XLA Ops:
  6.5 19.3 %slice-start = ((bf16[32,672]{1,0:T(8,128)(2,1)}), bf16[32,160]{1,0:T(8,128)(2,1)S(1)}, s32[]{:S(2)}) async-start(bf16[32,672]{1,0:T(8,128)(2,1)} %param.26), calls=%async_computation.7 | async-start | bytes 32768 | tf_op jit(solution)/shard_map/slice | solution.py:324
  6.5 19.4 %slice-start.1 = ((bf16[32,672]{1,0:T(8,128)(2,1)}), bf16[32,512]{1,0:T(8,128)(2,1)S(1)}, s32[]{:S(2)}) async-start(bf16[32,672]{1,0:T(8,128)(2,1)} %param.26), calls=%async_computation.8 | async-start | bytes 65536 | tf_op jit(solution)/shard_map/slice | solution.py:331
  6.5 19.3 %copy-start.7 = (bf16[84,256]{1,0:T(8,128)(2,1)S(1)}, bf16[84,256]{1,0:T(8,128)(2,1)}, u32[]{:S(2)}) copy-start(bf16[84,256]{1,0:T(8,128)(2,1)} %param.21) | copy-start | bytes 129028
  6.5 19.3 %copy-start.10 = (bf16[84,128]{1,0:T(8,128)(2,1)S(1)}, bf16[84,128]{1,0:T(8,128)(2,1)}, u32[]{:S(2)}) copy-start(bf16[84,128]{1,0:T(8,128)(2,1)} %param.22) | copy-start | bytes 64516
  6.5 19.3 %copy-start.9 = (bf16[84,128]{1,0:T(8,128)(2,1)S(1)}, bf16[84,128]{1,0:T(8,128)(2,1)}, u32[]{:S(2)}) copy-start(bf16[84,128]{1,0:T(8,128)(2,1)} %param.23) | copy-start | bytes 64516
  8.3 34.1 %copy-start.11 = (s32[8]{0:T(128)S(1)}, s32[8]{0:T(128)}, u32[]{:S(2)}) copy-start(s32[8]{0:T(128)} %param.16) | copy-start | bytes 100
  8.3 34.1 %copy-start.13 = (s32[8]{0:T(128)S(1)}, s32[8]{0:T(128)}, u32[]{:S(2)}) copy-start(s32[8]{0:T(128)} %param.17) | copy-start | bytes 100
  8.3 34.3 %copy-start.14 = (bf16[1152,672]{0,1:T(8,128)(2,1)S(1)}, bf16[1152,672]{0,1:T(8,128)(2,1)}, u32[]{:S(2)}) copy-start(bf16[1152,672]{0,1:T(8,128)(2,1)} %param.19) | copy-start | bytes 4644868
  10.0 32.2 %all-to-all-start = ((bf16[16,32,144]{2,1,0:T(8,128)(2,1)}), bf16[16,32,144]{2,1,0:T(8,128)(2,1)S(1)}, u32[]{:S(2)}, u32[]{:S(2)}) async-start(bf16[16,32,144]{2,1,0:T(8,128)(2,1)} %broadcast_in_dim.101), calls=%async_computation | async-start | bytes 524288 | tf_op jit(solution)/shard_map/all_to_all | solution.py:60
  25.8 94.1 %all-gather.3.cloned.1.call-start = ((), (), s32[]{:S(2)}) async-start(), calls=%async_computation.6 | async-start | bytes 5013504 | tf_op jit(solution)/shard_map/all_gather | solution.py:386
  25.9 10.2 %collective-permute-start = (bf16[144,512]{1,0:T(8,128)(2,1)S(1)}, bf16[144,512]{1,0:T(8,128)(2,1)S(1)}, u32[]{:S(2)}, u32[]{:S(2)}) collective-permute-start(bf16[144,512]{1,0:T(8,128)(2,1)S(1)} %maximum_maximum_fusion), channel_id=1, source_target_pairs={{0,0},{1,128},{128,1},{129,129},{256,256},{257,384},{384,257},{385... | collective-permute-start | bytes 442376 | tf_op jit(solution)/shard_map/ppermute | solution.py:42
  29.9 8.4 %collective-permute-start.1 = (bf16[144,512]{1,0:T(8,128)(2,1)S(1)}, bf16[144,512]{1,0:T(8,128)(2,1)S(1)}, u32[]{:S(2)}, u32[]{:S(2)}) collective-permute-start(bf16[144,512]{1,0:T(8,128)(2,1)S(1)} %maximum_maximum_fusion), channel_id=1, source_target_pairs={{0,256},{1,384},{128,257},{129,385},{256,0},{257,128},{384,1},{385... | collective-permute-start | bytes 442376 | tf_op jit(solution)/shard_map/ppermute | solution.py:42
  33.1 9.1 %collective-permute-start.2 = (bf16[256,672]{0,1:T(8,128)(2,1)}, bf16[256,672]{0,1:T(8,128)(2,1)}, u32[]{:S(2)}, u32[]{:S(2)}) collective-permute-start(bf16[256,672]{0,1:T(8,128)(2,1)} %param.14), channel_id=1, source_target_pairs={{0,0},{1,128},{128,1},{129,129},{2,2},{3,130},{130,3},{131,131},{4... | collective-permute-start | bytes 1032200 | tf_op jit(solution)/shard_map/ppermute | solution.py:33
  42.6 39.1 %collective-permute-start.3 = (bf16[1152,672]{0,1:T(8,128)(2,1)S(1)}, bf16[1152,672]{0,1:T(8,128)(2,1)}, u32[]{:S(2)}, u32[]{:S(2)}) collective-permute-start(bf16[1152,672]{0,1:T(8,128)(2,1)S(1)} %copy-done.14), channel_id=1, source_target_pairs={{0,1},{129,128},{2,3},{131,130},{4,5},{133,132},{6,7},{135,134},{8... | collective-permute-start | bytes 4644872 | tf_op jit(solution)/shard_map/ppermute | solution.py:387
  45.3 24.5 %copy-start.8 = (f32[5376]{0:T(1024)S(1)}, f32[5376]{0:T(1024)}, u32[]{:S(2)}) copy-start(f32[5376]{0:T(1024)} %param.20) | copy-start | bytes 64516
  65.3 14.5 %all-to-all-start.2 = ((bf16[8,144,256]{2,1,0:T(8,128)(2,1)}), bf16[8,144,256]{2,1,0:T(8,128)(2,1)S(1)}, u32[]{:S(2)}, u32[]{:S(2)}) async-start(bf16[8,144,256]{2,1,0:T(8,128)(2,1)} %broadcast_in_dim.109), calls=%async_computation.2 | async-start | bytes 1179648 | tf_op jit(solution)/shard_map/all_to_all | solution.py:60
  119.8 13.4 %collective-permute-start.4 = (bf16[16,2,144,512]{3,2,1,0:T(8,128)(2,1)}, bf16[16,2,144,512]{3,2,1,0:T(8,128)(2,1)}, u32[]{:S(2)}, u32[]{:S(2)}) collective-permute-start(bf16[16,2,144,512]{3,2,1,0:T(8,128)(2,1)} %bitcast.74), channel_id=1, source_target_pairs={{0,1},{1,0},{2,3},{3,2},{4,5},{5,4},{6,7},{7,6},{8,9},{9,8},{10,11... | collective-permute-start | bytes 14155784 | tf_op jit(solution)/shard_map/ppermute | solution.py:411
  125.3 1.8 copy-start.1
  127.1 1.8 copy-start.2
  128.8 2.3 %copy-start.3 = (bf16[32,144,512]{2,1,0:T(8,128)(2,1)S(1)}, bf16[32,144,512]{2,1,0:T(8,128)(2,1)}, u32[]{:S(2)}) copy-start(bf16[32,144,512]{2,1,0:T(8,128)(2,1)} %all-gather.3.cloned.1.call-done) | copy-start | bytes 14155780
  131.2 2.1 copy-start.5
  131.2 2.1 copy-start.6
  137.5 8.5 %collective-permute-start.5 = (bf16[256,256]{1,0:T(8,128)(2,1)S(1)}, bf16[256,256]{1,0:T(8,128)(2,1)S(1)}, u32[]{:S(2)}, u32[]{:S(2)}) collective-permute-start(bf16[256,256]{1,0:T(8,128)(2,1)S(1)} %get-tuple-element.31), channel_id=1, source_target_pairs={{0,16},{8,24},{16,32},{24,40},{32,48},{40,56},{48,64},{56,72},{64,... | collective-permute-start | bytes 393224 | tf_op jit(solution)/shard_map/ppermute | solution.py:55
  141.1 10.2 %collective-permute-start.6 = (bf16[256,256]{1,0:T(8,128)(2,1)S(1)}, bf16[256,256]{1,0:T(8,128)(2,1)S(1)}, u32[]{:S(2)}, u32[]{:S(2)}) collective-permute-start(bf16[256,256]{1,0:T(8,128)(2,1)S(1)} %get-tuple-element.31), channel_id=1, source_target_pairs={{0,8},{8,16},{16,24},{24,32},{32,40},{40,48},{48,56},{56,64},{64,7... | collective-permute-start | bytes 393224 | tf_op jit(solution)/shard_map/ppermute | solution.py:55
  151.3 17.0 %collective-permute-start.7 = (bf16[512,256]{1,0:T(8,128)(2,1)S(1)}, bf16[512,256]{1,0:T(8,128)(2,1)S(1)}, u32[]{:S(2)}, u32[]{:S(2)}) collective-permute-start(bf16[512,256]{1,0:T(8,128)(2,1)S(1)} %pad_maximum_fusion.1), channel_id=1, source_target_pairs={{0,16},{8,24},{16,32},{24,40},{32,48},{40,56},{48,64},{56,72},{64,... | collective-permute-start | bytes 786440 | tf_op jit(solution)/shard_map/ppermute | solution.py:55
  156.4 12.0 %collective-permute-start.8 = (bf16[256,256]{1,0:T(8,128)(2,1)S(1)}, bf16[256,256]{1,0:T(8,128)(2,1)S(1)}, u32[]{:S(2)}, u32[]{:S(2)}) collective-permute-start(bf16[256,256]{1,0:T(8,128)(2,1)S(1)} %get-tuple-element.31), channel_id=1, source_target_pairs={{8,0},{16,8},{24,16},{32,24},{40,32},{48,40},{56,48},{64,56},{72,6... | collective-permute-start | bytes 393224 | tf_op jit(solution)/shard_map/ppermute | solution.py:55
  171.1 38.3 %copy-start.12 = (f32[672]{0:T(1024)S(1)}, f32[672]{0:T(1024)}, u32[]{:S(2)}) copy-start(f32[672]{0:T(1024)} %param.27) | copy-start | bytes 8068
  171.1 19.6 %all-to-all-start.4 = ((bf16[8,256,256]{2,1,0:T(8,128)(2,1)}), bf16[8,256,256]{2,1,0:T(8,128)(2,1)S(1)}, u32[]{:S(2)}, u32[]{:S(2)}) async-start(bf16[8,256,256]{2,1,0:T(8,128)(2,1)} %broadcast_in_dim.192), calls=%async_computation.4 | async-start | bytes 2097152 | tf_op jit(solution)/shard_map/all_to_all | solution.py:60
  174.8 34.6 %collective-permute-start.9 = (bf16[672,256]{1,0:T(8,128)(2,1)S(1)}, bf16[672,256]{1,0:T(8,128)(2,1)S(1)}, u32[]{:S(2)}, u32[]{:S(2)}) collective-permute-start(bf16[672,256]{1,0:T(8,128)(2,1)S(1)} %fusion.28), channel_id=1, source_target_pairs={{0,0},{1,128},{128,1},{129,129},{2,2},{3,130},{130,3},{131,131},{4... | collective-permute-start | bytes 1032200 | tf_op jit(solution)/shard_map/ppermute | solution.py:33
  190.8 2.3 %copy-start.4 = (bf16[32,144,512]{2,1,0:T(8,128)(2,1)S(1)}, bf16[32,144,512]{2,1,0:T(8,128)(2,1)}, u32[]{:S(2)}) copy-start(bf16[32,144,512]{2,1,0:T(8,128)(2,1)} %all-gather.3.cloned.1.call-done) | copy-start | bytes 14155780
  197.3 12.2 %collective-permute-start.10 = (bf16[672,256]{1,0:T(8,128)(2,1)S(1)}, bf16[672,256]{1,0:T(8,128)(2,1)S(1)}, u32[]{:S(2)}, u32[]{:S(2)}) collective-permute-start(bf16[672,256]{1,0:T(8,128)(2,1)S(1)} %get-tuple-element.35), channel_id=1, source_target_pairs={{0,0},{1,128},{128,1},{129,129},{2,2},{3,130},{130,3},{131,131},{4... | collective-permute-start | bytes 1032200 | tf_op jit(solution)/shard_map/ppermute | solution.py:33
  200.4 9.0 %all-to-all-start.5 = ((f32[16,1,256]{2,1,0:T(1,128)}), f32[16,1,256]{2,1,0:T(1,128)S(1)}, u32[]{:S(2)}, u32[]{:S(2)}) async-start(f32[16,1,256]{2,1,0:T(1,128)} %get-tuple-element.36), calls=%async_computation.5 | async-start | bytes 32768 | tf_op jit(solution)/shard_map/all_to_all | solution.py:446
  (1 other events, 1.3 us)
Sparse Core Ops, SparseCore 0:
  42.3 71.8 all-gather.2

commit v8 on v7

--- a/solution.py
+++ b/solution.py
@@ -100,7 +100,7 @@
     for shard in range(8):
         block[shard * ROWS_IN : (shard + 1) * ROWS_IN, :] = weight_ref[shard, 0, :ROWS_IN, :]
     part = whole_ref[0].astype(jnp.float32)
-    gain = jnp.concatenate([gain_ref[0], gain_ref[0]], axis=1)
+    gain = jnp.transpose(gain_ref[0])[:WIDTH, :1]
     scaled = (part * gain).astype(jnp.bfloat16)
     product = lax.dot_general(
         scaled, block[...], (((0,), (0,)), ((), ())), preferred_element_type=jnp.float32
@@ -166,7 +166,7 @@
 def qkv_specs(block_of, width, rows):
     return [
         pl.BlockSpec((1, width, rows), lambda step, core: (block_of(step, core), 0, 0)),
-        pl.BlockSpec((1, width, HEAD_DIM), lambda step, core: (block_of(step, core), 0, 0)),
+        pl.BlockSpec((1, 8, 768), lambda step, core: (block_of(step, core), 0, 0)),
         pl.BlockSpec((8, 1, PAD_IN, 512), lambda step, core: (step % 2, step // 2, 0, 0)),
     ]
 
@@ -395,9 +395,9 @@
     mine = jnp.sum(frames.astype(jnp.float32), axis=0).astype(jnp.bfloat16)
     soft_rows = exchange(mine, HEAD, head_count).reshape(vis, tok_rows)
     gain_parts = jnp.broadcast_to(
-        input_gain.reshape(head_count, width, 1), (head_count, width, HEAD_DIM)
-    )
-    soft_rows, gain_parts = lax.optimization_barrier((soft_rows, gain_parts))
+        jnp.pad(input_gain.reshape(head_count, 1, width), ((0, 0), (0, 0), (0, 768 - width))),
+        (head_count, 8, 768),
+    )
     embedded = lax.dot_general(
         proj_weight, soft_rows, (((0,), (0,)), ((), ())),
         preferred_element_type=jnp.float32,
@@ -407,7 +407,8 @@
     residual = jnp.where((my_image >= 0)[None, :], embedded, tokens.T)
 
     whole = exchange(residual, HEAD, head_count)
-    along, whole = lax.optimization_barrier((along, whole))
+    given_residual = swapped(residual)
+    along, whole, given_residual = lax.optimization_barrier((along, whole, given_residual))
     across = lax.ppermute(along, "core", [(0, 1), (1, 0)])
     half = HEAD_DIM // 2
     frequency = ROPE_BASE ** (-jnp.arange(half, dtype=jnp.float32) * 2.0 / HEAD_DIM)
@@ -438,8 +439,6 @@
         allowed,
     )
     attended = attended.reshape(tok_rows, 2 * HEAD_DIM).T
-    attended, residual = lax.optimization_barrier((attended, residual))
-    given_residual = swapped(residual)
     heads_all = exchange(attended, HEAD, head_count)
     projected, squares = project_out(core, heads_all, along, across)
     given = swapped(projected).astype(jnp.float32)

time: 219 us -> 215 us (0.982)
  blocking collectives: 54.9 us -> 37.1 us
  waiting for transfers between devices: 48.2 us -> 59 us
  local copies, waits for them, and re-layouts: 15.5 us -> 8.13 us
  starting transfers between devices: 63.9 us -> 69.2 us
  Pallas kernels: 10.5 us -> 14.2 us
    ppermute x3, waiting for transfers between devices: 3.1 us -> 37.3 us  [swapped(): return lax.ppermute(value, ('a', 'core'), [(0, 0), (1, 2), (2, 1), (3, 3)])]
    all_to_all x1, blocking collectives: 35.9 us -> 17.8 us  [exchange(): return lax.all_to_all(spread, axes, 0, 0, tiled=True)]
    all_to_all x3, waiting for transfers between devices: 22.2 us -> 9.81 us  [exchange(): return lax.all_to_all(spread, axes, 0, 0, tiled=True)]
    ppermute x4, waiting for transfers between devices: 15.3 us -> 8.23 us  [shifted(): return lax.ppermute(value, ('k', 'z', 'core'), pairs)]
    unnamed x35 -> x33, local copies, waits for them, and re-layouts: 9.6 us -> 3.7 us
    all_to_all x1, waiting for transfers between devices: 5.45 us -> 2.16 us  [body(): all_squares = lax.all_to_all(squares, ('a', 'y', 'core'), 0, 0, tiled=True)]
    ppermute x3, starting transfers between devices: 9.53 us -> 12.4 us  [swapped(): return lax.ppermute(value, ('a', 'core'), [(0, 0), (1, 2), (2, 1), (3, 3)])]
    ppermute x1, starting transfers between devices: 4.53 us -> 1.91 us  [body(): across = lax.ppermute(along, 'core', [(0, 1), (1, 0)])]
  transfers between devices with their start and end apart: 16 -> 16, of which waited for: 8 -> 10; matrix products, arithmetic and copies ran while one was open for 5% -> 5% of each run, Pallas kernels for 3% -> 2%
where the time goes in v8:
time: 215 us; the launch traced here: 212 us
  starting transfers between devices  69.2 us (32%)
  waiting for transfers between devices  59 us (27%)
  blocking collectives  37.1 us (17%)
  Pallas kernels  14.2 us (7%)
  between operations  14 us (7%)
  local copies, waits for them, and re-layouts  8.13 us (4%)
  other arithmetic  5.22 us (2%)
  matrix products  5 us (2%)
    ppermute x3, waiting for transfers between devices, swapped(): return lax.ppermute(value, ('a', 'core'), [(0, 0), (1, 2), (2, 1), (3, 3)])  37.3 us
    all_to_all x3, starting transfers between devices, exchange(): return lax.all_to_all(spread, axes, 0, 0, tiled=True)  24.8 us
    all_to_all x1, blocking collectives, body(): lax.all_to_all(frames.astype(jnp.bfloat16), ('k', 'a', 'core'), 0, 0, til...  19.2 us
    all_to_all x1, blocking collectives, exchange(): return lax.all_to_all(spread, axes, 0, 0, tiled=True)  17.8 us
    ppermute x4, starting transfers between devices, shifted(): return lax.ppermute(value, ('k', 'z', 'core'), pairs)  15.9 us
    ppermute x3, starting transfers between devices, swapped(): return lax.ppermute(value, ('a', 'core'), [(0, 0), (1, 2), (2, 1), (3, 3)])  12.4 us
    all_to_all x3, waiting for transfers between devices, exchange(): return lax.all_to_all(spread, axes, 0, 0, tiled=True)  9.81 us
    ppermute x4, waiting for transfers between devices, shifted(): return lax.ppermute(value, ('k', 'z', 'core'), pairs)  8.23 us
  transfers between devices with their start and end apart: 16, of which 10 were waited for; matrix products, arithmetic and copies ran while one was open for 5% of the time, Pallas kernels for 2%

profile of v8, /device:TPU:1, one launch (start us, length us, event | category | flops | bytes accessed | tf_op | source)
XLA Modules:
  0.0 211.8 jit_solution(8745507604908166056)
XLA Ops:
  9.9 15.7 %all-to-all-start = ((bf16[16,32,144]{2,1,0:T(8,128)(2,1)}), bf16[16,32,144]{2,1,0:T(8,128)(2,1)S(1)}, u32[]{:S(2)}, u32[]{:S(2)}) async-start(bf16[16,32,144]{2,1,0:T(8,128)(2,1)} %broadcast_in_dim.100), calls=%async_computation | async-start | bytes 524288 | tf_op jit(solution)/shard_map/all_to_all | solution.py:60
  25.8 5.2 %collective-permute-start.1 = (bf16[144,512]{1,0:T(8,128)(2,1)S(1)}, bf16[144,512]{1,0:T(8,128)(2,1)S(1)}, u32[]{:S(2)}, u32[]{:S(2)}) collective-permute-start(bf16[144,512]{1,0:T(8,128)(2,1)S(1)} %maximum_maximum_fusion), channel_id=1, source_target_pairs={{0,256},{1,384},{128,257},{129,385},{256,0},{257,128},{384,1},{385... | collective-permute-start | bytes 442376 | tf_op jit(solution)/shard_map/ppermute | solution.py:42
  31.0 1.9 collective-permute-start
  33.0 3.6 %collective-permute-start.2 = (bf16[256,672]{0,1:T(8,128)(2,1)S(1)}, bf16[256,672]{0,1:T(8,128)(2,1)S(1)}, u32[]{:S(2)}, u32[]{:S(2)}) collective-permute-start(bf16[256,672]{0,1:T(8,128)(2,1)S(1)} %copy-done.11), channel_id=1, source_target_pairs={{0,0},{1,128},{128,1},{129,129},{2,2},{3,130},{130,3},{131,131},{4... | collective-permute-start | bytes 1032200 | tf_op jit(solution)/shard_map/ppermute | solution.py:33
  38.6 3.3 %collective-permute-done.2 = bf16[256,672]{0,1:T(8,128)(2,1)S(1)} collective-permute-done((bf16[256,672]{0,1:T(8,128)(2,1)S(1)}, bf16[256,672]{0,1:T(8,128)(2,1)S(1)}, u32[]{:S(2)}, u32[]{:S(2)}) %collective-permute-start.2) | collective-permute-done | bytes 344096 | tf_op jit(solution)/shard_map/ppermute | solution.py:33
  43.6 1.3 fusion.19
  45.0 19.2 %all_to_all.30 = bf16[8,144,256]{2,1,0:T(8,128)(2,1)S(1)} all-to-all(bf16[8,144,256]{2,1,0:T(8,128)(2,1)S(1)} %fusion.19), channel_id=1, replica_groups=mesh['k'=2,'a'=2,'z'=16,'y'=4,'core'=2] {'k','a','core'}, dimensions={0} | all-to-all | bytes 1179648 | tf_op jit(solution)/shard_map/all_to_all | solution.py:392
  65.1 4.5 %all-to-all-start.2 = ((bf16[8,144,256]{2,1,0:T(8,128)(2,1)}), bf16[8,144,256]{2,1,0:T(8,128)(2,1)S(1)}, u32[]{:S(2)}, u32[]{:S(2)}) async-start(bf16[8,144,256]{2,1,0:T(8,128)(2,1)} %broadcast_in_dim.108), calls=%async_computation.2 | async-start | bytes 1179648 | tf_op jit(solution)/shard_map/all_to_all | solution.py:60
  69.8 9.8 %all-to-all-done.2 = bf16[8,144,256]{2,1,0:T(8,128)(2,1)S(1)} async-done(((bf16[8,144,256]{2,1,0:T(8,128)(2,1)}), bf16[8,144,256]{2,1,0:T(8,128)(2,1)S(1)}, u32[]{:S(2)}, u32[]{:S(2)}) %all-to-all-start.2) | async-done | bytes 589856 | tf_op jit(solution)/shard_map/all_to_all | solution.py:60
  79.6 2.0 fusion.28
  81.6 1.7 broadcast_in_dim.109
  83.4 4.6 %all-to-all-start.3 = ((bf16[8,672,256]{2,1,0:T(8,128)(2,1)}), bf16[8,672,256]{2,1,0:T(8,128)(2,1)}, u32[]{:S(2)}, u32[]{:S(2)}) async-start(bf16[8,672,256]{2,1,0:T(8,128)(2,1)} %broadcast_in_dim.109), calls=%async_computation.3 | async-start | bytes 5505024 | tf_op jit(solution)/shard_map/all_to_all | solution.py:60
  87.9 5.2 %collective-permute-start.4 = (bf16[672,256]{1,0:T(8,128)(2,1)S(1)}, bf16[672,256]{1,0:T(8,128)(2,1)S(1)}, u32[]{:S(2)}, u32[]{:S(2)}) collective-permute-start(bf16[672,256]{1,0:T(8,128)(2,1)S(1)} %fusion.28), channel_id=1, source_target_pairs={{0,0},{1,128},{128,1},{129,129},{2,2},{3,130},{130,3},{131,131},{4... | collective-permute-start | bytes 1032200 | tf_op jit(solution)/shard_map/ppermute | solution.py:33
  93.2 31.4 %collective-permute-done.4 = bf16[672,256]{1,0:T(8,128)(2,1)S(1)} collective-permute-done((bf16[672,256]{1,0:T(8,128)(2,1)S(1)}, bf16[672,256]{1,0:T(8,128)(2,1)S(1)}, u32[]{:S(2)}, u32[]{:S(2)}) %collective-permute-start.4) | collective-permute-done | bytes 344096 | tf_op jit(solution)/shard_map/ppermute | solution.py:33
  124.6 1.9 collective-permute-start.5
  127.5 2.3 %copy-done.1 = bf16[32,144,512]{2,1,0:T(8,128)(2,1)S(1)} copy-done((bf16[32,144,512]{2,1,0:T(8,128)(2,1)S(1)}, bf16[32,144,512]{2,1,0:T(8,128)(2,1)}, u32[]{:S(2)}) %copy-start.1) | copy-done | bytes 4718616
  129.9 4.5 %shard_map.136 = (f32[256,512]{1,0:T(8,128)S(1)}, f32[1,256]{1,0:T(1,128)S(1)}) custom-call(s32[1]{0:T(128)} %bitcast.9.core_ref, bf16[8,672,256]{2,1,0:T(8,128)(2,1)} %all-to-all-done.3.whole_ref, f32[8,8,768]{2,1,0:T(8,128)S(1)} %broadcast_in_dim.116.gain_ref, bf16[16,2,144,512]{3,2,1,0:T(8,128)(2,1)S(1)} %bitcast.77), custom_call_target="tpu_custom_call" | custom-call | flops 704643072 | bytes 5242880 | tf_op jit(solution)/shard_map/pallas_call | solution.py:177
  134.7 5.5 %shard_map.137 = (bf16[256,256]{1,0:T(8,128)(2,1)S(1)}, bf16[256,256]{1,0:T(8,128)(2,1)S(1)}) custom-call(s32[1]{0:T(128)} %bitcast.9.core_ref, bf16[8,672,256]{2,1,0:T(8,128)(2,1)} %all-to-all-done.3.whole_ref, f32[8,8,768]{2,1,0:T(8,128)S(1)} %broadcast_in_dim.116.gain_ref, bf16[16,2,144,512]{3,2,1,0:T(8,128)(2,1)} %collective-permute-done.5.weight_ref.across_ref, ...), custom_call_target="tpu_custom_call" | custom-call | flops 704643072 | bytes 5242880 | tf_op jit(solution)/shard_map/pallas_call | solution.py:202
  140.2 2.6 %collective-permute-start.7 = (bf16[256,256]{1,0:T(8,128)(2,1)S(1)}, bf16[256,256]{1,0:T(8,128)(2,1)S(1)}, u32[]{:S(2)}, u32[]{:S(2)}) collective-permute-start(bf16[256,256]{1,0:T(8,128)(2,1)S(1)} %get-tuple-element.27), channel_id=1, source_target_pairs={{0,8},{8,16},{16,24},{24,32},{32,40},{40,48},{48,56},{56,64},{64,7... | collective-permute-start | bytes 393224 | tf_op jit(solution)/shard_map/ppermute | solution.py:55
  142.8 4.3 %collective-permute-start.6 = (bf16[256,256]{1,0:T(8,128)(2,1)S(1)}, bf16[256,256]{1,0:T(8,128)(2,1)S(1)}, u32[]{:S(2)}, u32[]{:S(2)}) collective-permute-start(bf16[256,256]{1,0:T(8,128)(2,1)S(1)} %get-tuple-element.27), channel_id=1, source_target_pairs={{0,16},{8,24},{16,32},{24,40},{32,48},{40,56},{48,64},{56,72},{64,... | collective-permute-start | bytes 393224 | tf_op jit(solution)/shard_map/ppermute | solution.py:55
  147.2 1.5 collective-permute-done.7
  148.7 4.9 %collective-permute-done.6 = bf16[256,256]{1,0:T(8,128)(2,1)S(1)} collective-permute-done((bf16[256,256]{1,0:T(8,128)(2,1)S(1)}, bf16[256,256]{1,0:T(8,128)(2,1)S(1)}, u32[]{:S(2)}, u32[]{:S(2)}) %collective-permute-start.6) | collective-permute-done | bytes 131104 | tf_op jit(solution)/shard_map/ppermute | solution.py:55
  153.6 1.9 collective-permute-start.8
  155.5 1.4 fusion.12
  156.9 7.1 %collective-permute-start.9 = (bf16[256,256]{1,0:T(8,128)(2,1)S(1)}, bf16[256,256]{1,0:T(8,128)(2,1)S(1)}, u32[]{:S(2)}, u32[]{:S(2)}) collective-permute-start(bf16[256,256]{1,0:T(8,128)(2,1)S(1)} %get-tuple-element.27), channel_id=1, source_target_pairs={{8,0},{16,8},{24,16},{32,24},{40,32},{48,40},{56,48},{64,56},{72,6... | collective-permute-start | bytes 393224 | tf_op jit(solution)/shard_map/ppermute | solution.py:55
  164.1 1.8 collective-permute-done.9
  167.8 17.8 %all_to_all.31.own_ref.other_ref = bf16[8,256,256]{2,1,0:T(8,128)(2,1)S(1)} all-to-all(bf16[8,256,256]{2,1,0:T(8,128)(2,1)S(1)} %broadcast_in_dim.192), channel_id=1, replica_groups=mesh['k'=2,'a'=2,'z'=16,'y'=4,'core'=2] {'y','a'}, dimensions={0} | all-to-all | bytes 2097152 | tf_op jit(solution)/shard_map/all_to_all | solution.py:60
  185.6 4.2 %shard_map.138 = (bf16[672,256]{1,0:T(8,128)(2,1)S(1)}, f32[16,1,256]{2,1,0:T(1,128)}) custom-call(s32[1]{0:T(128)} %bitcast.9.core_ref, bf16[8,256,256]{2,1,0:T(8,128)(2,1)S(1)} %all_to_all.31.own_ref.other_ref, bf16[8,256,256]{2,1,0:T(8,128)(2,1)S(1)} %all_to_all.31.own_ref.other_ref, bf16[16,2,144,512]{3,2,1,0:T(8,128)(2,1)S(1)} %bitcast.80, ...), custom_call_target="tpu_custom_call" | custom-call | flops 805306368 | bytes 5242880 | tf_op jit(solution)/shard_map/pallas_call | solution.py:271
  189.9 5.6 %all-to-all-start.5 = ((f32[16,1,256]{2,1,0:T(1,128)}), f32[16,1,256]{2,1,0:T(1,128)S(1)}, u32[]{:S(2)}, u32[]{:S(2)}) async-start(f32[16,1,256]{2,1,0:T(1,128)} %get-tuple-element.30), calls=%async_computation.5 | async-start | bytes 32768 | tf_op jit(solution)/shard_map/all_to_all | solution.py:445
  195.5 3.6 %collective-permute-start.10 = (bf16[672,256]{1,0:T(8,128)(2,1)S(1)}, bf16[672,256]{1,0:T(8,128)(2,1)S(1)}, u32[]{:S(2)}, u32[]{:S(2)}) collective-permute-start(bf16[672,256]{1,0:T(8,128)(2,1)S(1)} %get-tuple-element.29), channel_id=1, source_target_pairs={{0,0},{1,128},{128,1},{129,129},{2,2},{3,130},{130,3},{131,131},{4... | collective-permute-start | bytes 1032200 | tf_op jit(solution)/shard_map/ppermute | solution.py:33
  199.2 2.2 %all-to-all-done.5 = f32[16,1,256]{2,1,0:T(1,128)S(1)} async-done(((f32[16,1,256]{2,1,0:T(1,128)}), f32[16,1,256]{2,1,0:T(1,128)S(1)}, u32[]{:S(2)}, u32[]{:S(2)}) %all-to-all-start.5) | async-done | bytes 16416 | tf_op jit(solution)/shard_map/all_to_all | solution.py:445
  201.5 2.6 %collective-permute-done.10 = bf16[672,256]{1,0:T(8,128)(2,1)S(1)} collective-permute-done((bf16[672,256]{1,0:T(8,128)(2,1)S(1)}, bf16[672,256]{1,0:T(8,128)(2,1)S(1)}, u32[]{:S(2)}, u32[]{:S(2)}) %collective-permute-start.10) | collective-permute-done | bytes 344096 | tf_op jit(solution)/shard_map/ppermute | solution.py:33
  (100 shorter events, 12.4 us)
Async XLA Ops:
  6.5 1.3 copy-start
  6.5 19.2 %slice-start.2 = ((bf16[32,672]{1,0:T(8,128)(2,1)}), bf16[32,160]{1,0:T(8,128)(2,1)S(1)}, s32[]{:S(2)}) async-start(bf16[32,672]{1,0:T(8,128)(2,1)} %param.26), calls=%async_computation.9 | async-start | bytes 32768 | tf_op jit(solution)/shard_map/slice | solution.py:324
  6.5 19.2 %slice-start.3 = ((bf16[32,672]{1,0:T(8,128)(2,1)}), bf16[32,512]{1,0:T(8,128)(2,1)S(1)}, s32[]{:S(2)}) async-start(bf16[32,672]{1,0:T(8,128)(2,1)} %param.26), calls=%async_computation.10 | async-start | bytes 65536 | tf_op jit(solution)/shard_map/slice | solution.py:331
  6.5 19.2 %copy-start.6 = (bf16[84,128]{1,0:T(8,128)(2,1)S(1)}, bf16[84,128]{1,0:T(8,128)(2,1)}, u32[]{:S(2)}) copy-start(bf16[84,128]{1,0:T(8,128)(2,1)} %param.23) | copy-start | bytes 64516
  6.5 19.2 %copy-start.7 = (bf16[84,128]{1,0:T(8,128)(2,1)S(1)}, bf16[84,128]{1,0:T(8,128)(2,1)}, u32[]{:S(2)}) copy-start(bf16[84,128]{1,0:T(8,128)(2,1)} %param.22) | copy-start | bytes 64516
  6.5 19.2 %copy-start.4 = (bf16[84,256]{1,0:T(8,128)(2,1)S(1)}, bf16[84,256]{1,0:T(8,128)(2,1)}, u32[]{:S(2)}) copy-start(bf16[84,256]{1,0:T(8,128)(2,1)} %param.21) | copy-start | bytes 129028
  6.6 26.4 %copy-start.11 = (bf16[256,672]{0,1:T(8,128)(2,1)S(1)}, bf16[256,672]{0,1:T(8,128)(2,1)}, u32[]{:S(2)}) copy-start(bf16[256,672]{0,1:T(8,128)(2,1)} %param.14) | copy-start | bytes 1032196
  8.3 33.7 %copy-start.8 = (s32[8]{0:T(128)S(1)}, s32[8]{0:T(128)}, u32[]{:S(2)}) copy-start(s32[8]{0:T(128)} %param.16) | copy-start | bytes 100
  8.3 33.7 %copy-start.10 = (s32[8]{0:T(128)S(1)}, s32[8]{0:T(128)}, u32[]{:S(2)}) copy-start(s32[8]{0:T(128)} %param.17) | copy-start | bytes 100
  9.9 32.0 %all-to-all-start = ((bf16[16,32,144]{2,1,0:T(8,128)(2,1)}), bf16[16,32,144]{2,1,0:T(8,128)(2,1)S(1)}, u32[]{:S(2)}, u32[]{:S(2)}) async-start(bf16[16,32,144]{2,1,0:T(8,128)(2,1)} %broadcast_in_dim.100), calls=%async_computation | async-start | bytes 524288 | tf_op jit(solution)/shard_map/all_to_all | solution.py:60
  25.7 98.9 %all-gather.3.cloned.1.call-start = ((), (), s32[]{:S(2)}) async-start(), calls=%async_computation.6 | async-start | bytes 5013504 | tf_op jit(solution)/shard_map/all_gather | solution.py:386
  25.8 10.8 %collective-permute-start.1 = (bf16[144,512]{1,0:T(8,128)(2,1)S(1)}, bf16[144,512]{1,0:T(8,128)(2,1)S(1)}, u32[]{:S(2)}, u32[]{:S(2)}) collective-permute-start(bf16[144,512]{1,0:T(8,128)(2,1)S(1)} %maximum_maximum_fusion), channel_id=1, source_target_pairs={{0,256},{1,384},{128,257},{129,385},{256,0},{257,128},{384,1},{385... | collective-permute-start | bytes 442376 | tf_op jit(solution)/shard_map/ppermute | solution.py:42
  31.0 6.8 %collective-permute-start = (bf16[144,512]{1,0:T(8,128)(2,1)S(1)}, bf16[144,512]{1,0:T(8,128)(2,1)S(1)}, u32[]{:S(2)}, u32[]{:S(2)}) collective-permute-start(bf16[144,512]{1,0:T(8,128)(2,1)S(1)} %maximum_maximum_fusion), channel_id=1, source_target_pairs={{0,0},{1,128},{128,1},{129,129},{256,256},{257,384},{384,257},{385... | collective-permute-start | bytes 442376 | tf_op jit(solution)/shard_map/ppermute | solution.py:42
  33.0 8.9 %collective-permute-start.2 = (bf16[256,672]{0,1:T(8,128)(2,1)S(1)}, bf16[256,672]{0,1:T(8,128)(2,1)S(1)}, u32[]{:S(2)}, u32[]{:S(2)}) collective-permute-start(bf16[256,672]{0,1:T(8,128)(2,1)S(1)} %copy-done.11), channel_id=1, source_target_pairs={{0,0},{1,128},{128,1},{129,129},{2,2},{3,130},{130,3},{131,131},{4... | collective-permute-start | bytes 1032200 | tf_op jit(solution)/shard_map/ppermute | solution.py:33
  42.2 37.4 %collective-permute-start.3 = (bf16[1152,672]{0,1:T(8,128)(2,1)}, bf16[1152,672]{0,1:T(8,128)(2,1)}, u32[]{:S(2)}, u32[]{:S(2)}) collective-permute-start(bf16[1152,672]{0,1:T(8,128)(2,1)} %param.19), channel_id=1, source_target_pairs={{0,1},{129,128},{2,3},{131,130},{4,5},{133,132},{6,7},{135,134},{8... | collective-permute-start | bytes 4644872 | tf_op jit(solution)/shard_map/ppermute | solution.py:387
  65.1 14.4 %all-to-all-start.2 = ((bf16[8,144,256]{2,1,0:T(8,128)(2,1)}), bf16[8,144,256]{2,1,0:T(8,128)(2,1)S(1)}, u32[]{:S(2)}, u32[]{:S(2)}) async-start(bf16[8,144,256]{2,1,0:T(8,128)(2,1)} %broadcast_in_dim.108), calls=%async_computation.2 | async-start | bytes 1179648 | tf_op jit(solution)/shard_map/all_to_all | solution.py:60
  83.4 43.1 %copy-start.5 = (f32[5376]{0:T(1024)S(1)}, f32[5376]{0:T(1024)}, u32[]{:S(2)}) copy-start(f32[5376]{0:T(1024)} %param.20) | copy-start | bytes 64516
  83.4 41.2 %all-to-all-start.3 = ((bf16[8,672,256]{2,1,0:T(8,128)(2,1)}), bf16[8,672,256]{2,1,0:T(8,128)(2,1)}, u32[]{:S(2)}, u32[]{:S(2)}) async-start(bf16[8,672,256]{2,1,0:T(8,128)(2,1)} %broadcast_in_dim.109), calls=%async_computation.3 | async-start | bytes 5505024 | tf_op jit(solution)/shard_map/all_to_all | solution.py:60
  87.9 36.6 %collective-permute-start.4 = (bf16[672,256]{1,0:T(8,128)(2,1)S(1)}, bf16[672,256]{1,0:T(8,128)(2,1)S(1)}, u32[]{:S(2)}, u32[]{:S(2)}) collective-permute-start(bf16[672,256]{1,0:T(8,128)(2,1)S(1)} %fusion.28), channel_id=1, source_target_pairs={{0,0},{1,128},{128,1},{129,129},{2,2},{3,130},{130,3},{131,131},{4... | collective-permute-start | bytes 1032200 | tf_op jit(solution)/shard_map/ppermute | solution.py:33
  124.6 10.1 %collective-permute-start.5 = (bf16[16,2,144,512]{3,2,1,0:T(8,128)(2,1)}, bf16[16,2,144,512]{3,2,1,0:T(8,128)(2,1)}, u32[]{:S(2)}, u32[]{:S(2)}) collective-permute-start(bf16[16,2,144,512]{3,2,1,0:T(8,128)(2,1)} %bitcast.76), channel_id=1, source_target_pairs={{0,1},{1,0},{2,3},{3,2},{4,5},{5,4},{6,7},{7,6},{8,9},{9,8},{10,11... | collective-permute-start | bytes 14155784 | tf_op jit(solution)/shard_map/ppermute | solution.py:412
  127.5 2.3 %copy-start.1 = (bf16[32,144,512]{2,1,0:T(8,128)(2,1)S(1)}, bf16[32,144,512]{2,1,0:T(8,128)(2,1)}, u32[]{:S(2)}) copy-start(bf16[32,144,512]{2,1,0:T(8,128)(2,1)} %all-gather.3.cloned.1.call-done) | copy-start | bytes 14155780
  129.9 4.9 %copy-start.2 = (f32[128]{0:T(128)S(1)}, f32[128]{0:T(128)}, u32[]{:S(2)}) copy-start(f32[128]{0:T(128)} %param.24) | copy-start | bytes 1540
  129.9 4.9 %copy-start.3 = (f32[128]{0:T(128)S(1)}, f32[128]{0:T(128)}, u32[]{:S(2)}) copy-start(f32[128]{0:T(128)} %param.25) | copy-start | bytes 1540
  140.2 8.4 %collective-permute-start.7 = (bf16[256,256]{1,0:T(8,128)(2,1)S(1)}, bf16[256,256]{1,0:T(8,128)(2,1)S(1)}, u32[]{:S(2)}, u32[]{:S(2)}) collective-permute-start(bf16[256,256]{1,0:T(8,128)(2,1)S(1)} %get-tuple-element.27), channel_id=1, source_target_pairs={{0,8},{8,16},{16,24},{24,32},{32,40},{40,48},{48,56},{56,64},{64,7... | collective-permute-start | bytes 393224 | tf_op jit(solution)/shard_map/ppermute | solution.py:55
  142.8 10.7 %collective-permute-start.6 = (bf16[256,256]{1,0:T(8,128)(2,1)S(1)}, bf16[256,256]{1,0:T(8,128)(2,1)S(1)}, u32[]{:S(2)}, u32[]{:S(2)}) collective-permute-start(bf16[256,256]{1,0:T(8,128)(2,1)S(1)} %get-tuple-element.27), channel_id=1, source_target_pairs={{0,16},{8,24},{16,32},{24,40},{32,48},{40,56},{48,64},{56,72},{64,... | collective-permute-start | bytes 393224 | tf_op jit(solution)/shard_map/ppermute | solution.py:55
  153.6 10.5 %collective-permute-start.8 = (bf16[512,256]{1,0:T(8,128)(2,1)S(1)}, bf16[512,256]{1,0:T(8,128)(2,1)S(1)}, u32[]{:S(2)}, u32[]{:S(2)}) collective-permute-start(bf16[512,256]{1,0:T(8,128)(2,1)S(1)} %pad_maximum_fusion.1), channel_id=1, source_target_pairs={{0,16},{8,24},{16,32},{24,40},{32,48},{40,56},{48,64},{56,72},{64,... | collective-permute-start | bytes 786440 | tf_op jit(solution)/shard_map/ppermute | solution.py:55
  156.9 9.0 %collective-permute-start.9 = (bf16[256,256]{1,0:T(8,128)(2,1)S(1)}, bf16[256,256]{1,0:T(8,128)(2,1)S(1)}, u32[]{:S(2)}, u32[]{:S(2)}) collective-permute-start(bf16[256,256]{1,0:T(8,128)(2,1)S(1)} %get-tuple-element.27), channel_id=1, source_target_pairs={{8,0},{16,8},{24,16},{32,24},{40,32},{48,40},{56,48},{64,56},{72,6... | collective-permute-start | bytes 393224 | tf_op jit(solution)/shard_map/ppermute | solution.py:55
  166.0 19.6 %slice-start = ((s8[4718592]{0:T(1024)(128)(4,1)}), s8[4194304]{0:T(1024)(128)(4,1)S(1)}, s32[]{:S(2)}) async-start(s8[4718592]{0:T(1024)(128)(4,1)} %bitcast.78), calls=%async_computation.7 | async-start | bytes 8388608
  166.6 19.0 %slice-start.1 = ((s8[4718592]{0:T(1024)(128)(4,1)}), s8[524288]{0:T(1024)(128)(4,1)S(1)}, s32[]{:S(2)}) async-start(s8[4718592]{0:T(1024)(128)(4,1)} %bitcast.78), calls=%async_computation.8 | async-start | bytes 1048576
  185.6 18.4 %copy-start.9 = (f32[672]{0:T(1024)S(1)}, f32[672]{0:T(1024)}, u32[]{:S(2)}) copy-start(f32[672]{0:T(1024)} %param.27) | copy-start | bytes 8068
  189.9 11.5 %all-to-all-start.5 = ((f32[16,1,256]{2,1,0:T(1,128)}), f32[16,1,256]{2,1,0:T(1,128)S(1)}, u32[]{:S(2)}, u32[]{:S(2)}) async-start(f32[16,1,256]{2,1,0:T(1,128)} %get-tuple-element.30), calls=%async_computation.5 | async-start | bytes 32768 | tf_op jit(solution)/shard_map/all_to_all | solution.py:445
  195.5 8.6 %collective-permute-start.10 = (bf16[672,256]{1,0:T(8,128)(2,1)S(1)}, bf16[672,256]{1,0:T(8,128)(2,1)S(1)}, u32[]{:S(2)}, u32[]{:S(2)}) collective-permute-start(bf16[672,256]{1,0:T(8,128)(2,1)S(1)} %get-tuple-element.29), channel_id=1, source_target_pairs={{0,0},{1,128},{128,1},{129,129},{2,2},{3,130},{130,3},{131,131},{4... | collective-permute-start | bytes 1032200 | tf_op jit(solution)/shard_map/ppermute | solution.py:33
Sparse Core Ops, SparseCore 0:
  42.0 72.0 all-gather.2

commit v9 on v7

--- a/solution.py
+++ b/solution.py
@@ -397,7 +397,6 @@
     gain_parts = jnp.broadcast_to(
         input_gain.reshape(head_count, width, 1), (head_count, width, HEAD_DIM)
     )
-    soft_rows, gain_parts = lax.optimization_barrier((soft_rows, gain_parts))
     embedded = lax.dot_general(
         proj_weight, soft_rows, (((0,), (0,)), ((), ())),
         preferred_element_type=jnp.float32,
@@ -407,7 +406,8 @@
     residual = jnp.where((my_image >= 0)[None, :], embedded, tokens.T)
 
     whole = exchange(residual, HEAD, head_count)
-    along, whole = lax.optimization_barrier((along, whole))
+    given_residual = swapped(residual)
+    along, whole, given_residual = lax.optimization_barrier((along, whole, given_residual))
     across = lax.ppermute(along, "core", [(0, 1), (1, 0)])
     half = HEAD_DIM // 2
     frequency = ROPE_BASE ** (-jnp.arange(half, dtype=jnp.float32) * 2.0 / HEAD_DIM)
@@ -438,8 +438,6 @@
         allowed,
     )
     attended = attended.reshape(tok_rows, 2 * HEAD_DIM).T
-    attended, residual = lax.optimization_barrier((attended, residual))
-    given_residual = swapped(residual)
     heads_all = exchange(attended, HEAD, head_count)
     projected, squares = project_out(core, heads_all, along, across)
     given = swapped(projected).astype(jnp.float32)

time: 219 us -> 216 us (0.986)
  waiting for transfers between devices: 48.2 us -> 68.3 us
  blocking collectives: 54.9 us -> 38.4 us
  local copies, waits for them, and re-layouts: 15.5 us -> 8.88 us
    ppermute x3, waiting for transfers between devices: 3.1 us -> 34.3 us  [swapped(): return lax.ppermute(value, ('a', 'core'), [(0, 0), (1, 2), (2, 1), (3, 3)])]
    all_to_all x1, blocking collectives: 35.9 us -> 19.2 us  [exchange(): return lax.all_to_all(spread, axes, 0, 0, tiled=True)]
    all_to_all x3, waiting for transfers between devices: 22.2 us -> 9.81 us  [exchange(): return lax.all_to_all(spread, axes, 0, 0, tiled=True)]
    unnamed x35 -> x33, local copies, waits for them, and re-layouts: 9.6 us -> 3.71 us
    ppermute x1, starting transfers between devices: 4.53 us -> 1.91 us  [body(): across = lax.ppermute(along, 'core', [(0, 1), (1, 0)])]
  transfers between devices with their start and end apart: 16 -> 16, of which waited for: 8 -> 9; matrix products, arithmetic and copies ran while one was open for 5% -> 5% of each run, Pallas kernels for 3% -> 2%
where the time goes in v9:
time: 216 us; the launch traced here: 215 us
  waiting for transfers between devices  68.3 us (32%)
  starting transfers between devices  63 us (29%)
  blocking collectives  38.4 us (18%)
  between operations  14 us (6%)
  Pallas kernels  12.2 us (6%)
  local copies, waits for them, and re-layouts  8.88 us (4%)
  other arithmetic  5.23 us (2%)
  matrix products  4.98 us (2%)
    ppermute x3, waiting for transfers between devices, swapped(): return lax.ppermute(value, ('a', 'core'), [(0, 0), (1, 2), (2, 1), (3, 3)])  34.3 us
    all_to_all x3, starting transfers between devices, exchange(): return lax.all_to_all(spread, axes, 0, 0, tiled=True)  24.8 us
    all_to_all x1, blocking collectives, body(): lax.all_to_all(frames.astype(jnp.bfloat16), ('k', 'a', 'core'), 0, 0, til...  19.2 us
    all_to_all x1, blocking collectives, exchange(): return lax.all_to_all(spread, axes, 0, 0, tiled=True)  19.2 us
    ppermute x4, waiting for transfers between devices, shifted(): return lax.ppermute(value, ('k', 'z', 'core'), pairs)  16.1 us
    ppermute x4, starting transfers between devices, shifted(): return lax.ppermute(value, ('k', 'z', 'core'), pairs)  13.4 us
    ppermute x3, starting transfers between devices, swapped(): return lax.ppermute(value, ('a', 'core'), [(0, 0), (1, 2), (2, 1), (3, 3)])  11 us
    all_to_all x3, waiting for transfers between devices, exchange(): return lax.all_to_all(spread, axes, 0, 0, tiled=True)  9.81 us
  transfers between devices with their start and end apart: 16, of which 9 were waited for; matrix products, arithmetic and copies ran while one was open for 5% of the time, Pallas kernels for 2%

profile of v9, /device:TPU:1, one launch (start us, length us, event | category | flops | bytes accessed | tf_op | source)
XLA Modules:
  0.0 215.0 jit_solution(6514218883557046558)
XLA Ops:
  9.9 15.7 %all-to-all-start = ((bf16[16,32,144]{2,1,0:T(8,128)(2,1)}), bf16[16,32,144]{2,1,0:T(8,128)(2,1)S(1)}, u32[]{:S(2)}, u32[]{:S(2)}) async-start(bf16[16,32,144]{2,1,0:T(8,128)(2,1)} %broadcast_in_dim.100), calls=%async_computation | async-start | bytes 524288 | tf_op jit(solution)/shard_map/all_to_all | solution.py:60
  25.8 4.0 %collective-permute-start = (bf16[144,512]{1,0:T(8,128)(2,1)S(1)}, bf16[144,512]{1,0:T(8,128)(2,1)S(1)}, u32[]{:S(2)}, u32[]{:S(2)}) collective-permute-start(bf16[144,512]{1,0:T(8,128)(2,1)S(1)} %maximum_maximum_fusion), channel_id=1, source_target_pairs={{0,0},{1,128},{128,1},{129,129},{256,256},{257,384},{384,257},{385... | collective-permute-start | bytes 442376 | tf_op jit(solution)/shard_map/ppermute | solution.py:42
  29.8 3.2 %collective-permute-start.1 = (bf16[144,512]{1,0:T(8,128)(2,1)S(1)}, bf16[144,512]{1,0:T(8,128)(2,1)S(1)}, u32[]{:S(2)}, u32[]{:S(2)}) collective-permute-start(bf16[144,512]{1,0:T(8,128)(2,1)S(1)} %maximum_maximum_fusion), channel_id=1, source_target_pairs={{0,256},{1,384},{128,257},{129,385},{256,0},{257,128},{384,1},{385... | collective-permute-start | bytes 442376 | tf_op jit(solution)/shard_map/ppermute | solution.py:42
  33.0 3.0 %collective-permute-start.2 = (bf16[256,672]{0,1:T(8,128)(2,1)S(1)}, bf16[256,672]{0,1:T(8,128)(2,1)S(1)}, u32[]{:S(2)}, u32[]{:S(2)}) collective-permute-start(bf16[256,672]{0,1:T(8,128)(2,1)S(1)} %copy-done.11), channel_id=1, source_target_pairs={{0,0},{1,128},{128,1},{129,129},{2,2},{3,130},{130,3},{131,131},{4... | collective-permute-start | bytes 1032200 | tf_op jit(solution)/shard_map/ppermute | solution.py:33
  36.0 2.1 collective-permute-done.1
  39.0 2.9 %collective-permute-done.2 = bf16[256,672]{0,1:T(8,128)(2,1)S(1)} collective-permute-done((bf16[256,672]{0,1:T(8,128)(2,1)S(1)}, bf16[256,672]{0,1:T(8,128)(2,1)S(1)}, u32[]{:S(2)}, u32[]{:S(2)}) %collective-permute-start.2) | collective-permute-done | bytes 344096 | tf_op jit(solution)/shard_map/ppermute | solution.py:33
  43.6 1.3 fusion.19
  45.0 19.2 %all_to_all.30 = bf16[8,144,256]{2,1,0:T(8,128)(2,1)S(1)} all-to-all(bf16[8,144,256]{2,1,0:T(8,128)(2,1)S(1)} %fusion.19), channel_id=1, replica_groups=mesh['k'=2,'a'=2,'z'=16,'y'=4,'core'=2] {'k','a','core'}, dimensions={0} | all-to-all | bytes 1179648 | tf_op jit(solution)/shard_map/all_to_all | solution.py:392
  65.1 4.5 %all-to-all-start.2 = ((bf16[8,144,256]{2,1,0:T(8,128)(2,1)}), bf16[8,144,256]{2,1,0:T(8,128)(2,1)S(1)}, u32[]{:S(2)}, u32[]{:S(2)}) async-start(bf16[8,144,256]{2,1,0:T(8,128)(2,1)} %broadcast_in_dim.108), calls=%async_computation.2 | async-start | bytes 1179648 | tf_op jit(solution)/shard_map/all_to_all | solution.py:60
  69.8 9.8 %all-to-all-done.2 = bf16[8,144,256]{2,1,0:T(8,128)(2,1)S(1)} async-done(((bf16[8,144,256]{2,1,0:T(8,128)(2,1)}), bf16[8,144,256]{2,1,0:T(8,128)(2,1)S(1)}, u32[]{:S(2)}, u32[]{:S(2)}) %all-to-all-start.2) | async-done | bytes 589856 | tf_op jit(solution)/shard_map/all_to_all | solution.py:60
  79.6 2.0 fusion.28
  81.6 1.7 broadcast_in_dim.109
  83.4 4.6 %all-to-all-start.3 = ((bf16[8,672,256]{2,1,0:T(8,128)(2,1)}), bf16[8,672,256]{2,1,0:T(8,128)(2,1)}, u32[]{:S(2)}, u32[]{:S(2)}) async-start(bf16[8,672,256]{2,1,0:T(8,128)(2,1)} %broadcast_in_dim.109), calls=%async_computation.3 | async-start | bytes 5505024 | tf_op jit(solution)/shard_map/all_to_all | solution.py:60
  87.9 5.2 %collective-permute-start.4 = (bf16[672,256]{1,0:T(8,128)(2,1)S(1)}, bf16[672,256]{1,0:T(8,128)(2,1)S(1)}, u32[]{:S(2)}, u32[]{:S(2)}) collective-permute-start(bf16[672,256]{1,0:T(8,128)(2,1)S(1)} %fusion.28), channel_id=1, source_target_pairs={{0,0},{1,128},{128,1},{129,129},{2,2},{3,130},{130,3},{131,131},{4... | collective-permute-start | bytes 1032200 | tf_op jit(solution)/shard_map/ppermute | solution.py:33
  93.2 31.4 %collective-permute-done.4 = bf16[672,256]{1,0:T(8,128)(2,1)S(1)} collective-permute-done((bf16[672,256]{1,0:T(8,128)(2,1)S(1)}, bf16[672,256]{1,0:T(8,128)(2,1)S(1)}, u32[]{:S(2)}, u32[]{:S(2)}) %collective-permute-start.4) | collective-permute-done | bytes 344096 | tf_op jit(solution)/shard_map/ppermute | solution.py:33
  124.5 1.9 collective-permute-start.5
  128.2 2.3 %copy-done.1 = bf16[32,144,512]{2,1,0:T(8,128)(2,1)S(1)} copy-done((bf16[32,144,512]{2,1,0:T(8,128)(2,1)S(1)}, bf16[32,144,512]{2,1,0:T(8,128)(2,1)}, u32[]{:S(2)}) %copy-start.1) | copy-done | bytes 4718616
  130.6 3.5 %shard_map.136 = (f32[256,512]{1,0:T(8,128)S(1)}, f32[1,256]{1,0:T(1,128)S(1)}) custom-call(s32[1]{0:T(128)} %bitcast.9.core_ref, bf16[8,672,256]{2,1,0:T(8,128)(2,1)} %all-to-all-done.3.whole_ref, f32[8,672,128]{2,1,0:T(8,128)S(1)} %broadcast_in_dim.116.gain_ref, bf16[16,2,144,512]{3,2,1,0:T(8,128)(2,1)S(1)} %bitcast.75), custom_call_target="tpu_custom_call" | custom-call | flops 704643072 | bytes 5242880 | tf_op jit(solution)/shard_map/pallas_call | solution.py:177
  134.7 4.5 %shard_map.137 = (bf16[256,256]{1,0:T(8,128)(2,1)S(1)}, bf16[256,256]{1,0:T(8,128)(2,1)S(1)}) custom-call(s32[1]{0:T(128)} %bitcast.9.core_ref, bf16[8,672,256]{2,1,0:T(8,128)(2,1)} %all-to-all-done.3.whole_ref, f32[8,672,128]{2,1,0:T(8,128)S(1)} %broadcast_in_dim.116.gain_ref, bf16[16,2,144,512]{3,2,1,0:T(8,128)(2,1)} %collective-permute-done.5.weight_ref.across_ref, ...), custom_call_target="tpu_custom_call" | custom-call | flops 704643072 | bytes 5242880 | tf_op jit(solution)/shard_map/pallas_call | solution.py:202
  139.2 3.8 %collective-permute-start.6 = (bf16[256,256]{1,0:T(8,128)(2,1)S(1)}, bf16[256,256]{1,0:T(8,128)(2,1)S(1)}, u32[]{:S(2)}, u32[]{:S(2)}) collective-permute-start(bf16[256,256]{1,0:T(8,128)(2,1)S(1)} %get-tuple-element.27), channel_id=1, source_target_pairs={{0,16},{8,24},{16,32},{24,40},{32,48},{40,56},{48,64},{56,72},{64,... | collective-permute-start | bytes 393224 | tf_op jit(solution)/shard_map/ppermute | solution.py:55
  143.0 3.2 %collective-permute-start.7 = (bf16[256,256]{1,0:T(8,128)(2,1)S(1)}, bf16[256,256]{1,0:T(8,128)(2,1)S(1)}, u32[]{:S(2)}, u32[]{:S(2)}) collective-permute-start(bf16[256,256]{1,0:T(8,128)(2,1)S(1)} %get-tuple-element.27), channel_id=1, source_target_pairs={{0,8},{8,16},{16,24},{24,32},{32,40},{40,48},{48,56},{56,64},{64,7... | collective-permute-start | bytes 393224 | tf_op jit(solution)/shard_map/ppermute | solution.py:55
  146.2 2.6 %collective-permute-done.6 = bf16[256,256]{1,0:T(8,128)(2,1)S(1)} collective-permute-done((bf16[256,256]{1,0:T(8,128)(2,1)S(1)}, bf16[256,256]{1,0:T(8,128)(2,1)S(1)}, u32[]{:S(2)}, u32[]{:S(2)}) %collective-permute-start.6) | collective-permute-done | bytes 131104 | tf_op jit(solution)/shard_map/ppermute | solution.py:55
  148.7 4.8 %collective-permute-done.7 = bf16[256,256]{1,0:T(8,128)(2,1)S(1)} collective-permute-done((bf16[256,256]{1,0:T(8,128)(2,1)S(1)}, bf16[256,256]{1,0:T(8,128)(2,1)S(1)}, u32[]{:S(2)}, u32[]{:S(2)}) %collective-permute-start.7) | collective-permute-done | bytes 131104 | tf_op jit(solution)/shard_map/ppermute | solution.py:55
  153.6 3.3 %collective-permute-start.8 = (bf16[512,256]{1,0:T(8,128)(2,1)S(1)}, bf16[512,256]{1,0:T(8,128)(2,1)S(1)}, u32[]{:S(2)}, u32[]{:S(2)}) collective-permute-start(bf16[512,256]{1,0:T(8,128)(2,1)S(1)} %pad_maximum_fusion.1), channel_id=1, source_target_pairs={{0,16},{8,24},{16,32},{24,40},{32,48},{40,56},{48,64},{56,72},{64,... | collective-permute-start | bytes 786440 | tf_op jit(solution)/shard_map/ppermute | solution.py:55
  156.9 1.4 fusion.12
  158.3 3.1 %collective-permute-start.9 = (bf16[256,256]{1,0:T(8,128)(2,1)S(1)}, bf16[256,256]{1,0:T(8,128)(2,1)S(1)}, u32[]{:S(2)}, u32[]{:S(2)}) collective-permute-start(bf16[256,256]{1,0:T(8,128)(2,1)S(1)} %get-tuple-element.27), channel_id=1, source_target_pairs={{8,0},{16,8},{24,16},{32,24},{40,32},{48,40},{56,48},{64,56},{72,6... | collective-permute-start | bytes 393224 | tf_op jit(solution)/shard_map/ppermute | solution.py:55
  161.5 8.7 %collective-permute-done.8 = bf16[512,256]{1,0:T(8,128)(2,1)S(1)} collective-permute-done((bf16[512,256]{1,0:T(8,128)(2,1)S(1)}, bf16[512,256]{1,0:T(8,128)(2,1)S(1)}, u32[]{:S(2)}, u32[]{:S(2)}) %collective-permute-start.8) | collective-permute-done | bytes 262176 | tf_op jit(solution)/shard_map/ppermute | solution.py:55
  172.0 19.2 %all_to_all.31.own_ref.other_ref = bf16[8,256,256]{2,1,0:T(8,128)(2,1)S(1)} all-to-all(bf16[8,256,256]{2,1,0:T(8,128)(2,1)S(1)} %broadcast_in_dim.192), channel_id=1, replica_groups=mesh['k'=2,'a'=2,'z'=16,'y'=4,'core'=2] {'y','a'}, dimensions={0} | all-to-all | bytes 2097152 | tf_op jit(solution)/shard_map/all_to_all | solution.py:60
  191.2 4.2 %shard_map.138 = (bf16[672,256]{1,0:T(8,128)(2,1)S(1)}, f32[16,1,256]{2,1,0:T(1,128)}) custom-call(s32[1]{0:T(128)} %bitcast.9.core_ref, bf16[8,256,256]{2,1,0:T(8,128)(2,1)S(1)} %all_to_all.31.own_ref.other_ref, bf16[8,256,256]{2,1,0:T(8,128)(2,1)S(1)} %all_to_all.31.own_ref.other_ref, bf16[16,2,144,512]{3,2,1,0:T(8,128)(2,1)S(1)} %bitcast.78, ...), custom_call_target="tpu_custom_call" | custom-call | flops 805306368 | bytes 5242880 | tf_op jit(solution)/shard_map/pallas_call | solution.py:271
  195.5 2.7 %collective-permute-start.10 = (bf16[672,256]{1,0:T(8,128)(2,1)S(1)}, bf16[672,256]{1,0:T(8,128)(2,1)S(1)}, u32[]{:S(2)}, u32[]{:S(2)}) collective-permute-start(bf16[672,256]{1,0:T(8,128)(2,1)S(1)} %get-tuple-element.29), channel_id=1, source_target_pairs={{0,0},{1,128},{128,1},{129,129},{2,2},{3,130},{130,3},{131,131},{4... | collective-permute-start | bytes 1032200 | tf_op jit(solution)/shard_map/ppermute | solution.py:33
  198.2 3.4 %all-to-all-start.5 = ((f32[16,1,256]{2,1,0:T(1,128)}), f32[16,1,256]{2,1,0:T(1,128)S(1)}, u32[]{:S(2)}, u32[]{:S(2)}) async-start(f32[16,1,256]{2,1,0:T(1,128)} %get-tuple-element.30), calls=%async_computation.5 | async-start | bytes 32768 | tf_op jit(solution)/shard_map/all_to_all | solution.py:444
  201.7 5.4 %all-to-all-done.5 = f32[16,1,256]{2,1,0:T(1,128)S(1)} async-done(((f32[16,1,256]{2,1,0:T(1,128)}), f32[16,1,256]{2,1,0:T(1,128)S(1)}, u32[]{:S(2)}, u32[]{:S(2)}) %all-to-all-start.5) | async-done | bytes 16416 | tf_op jit(solution)/shard_map/all_to_all | solution.py:444
  (99 shorter events, 12.3 us)
Async XLA Ops:
  6.5 1.3 copy-start
  6.5 19.2 %slice-start.2 = ((bf16[32,672]{1,0:T(8,128)(2,1)}), bf16[32,160]{1,0:T(8,128)(2,1)S(1)}, s32[]{:S(2)}) async-start(bf16[32,672]{1,0:T(8,128)(2,1)} %param.26), calls=%async_computation.9 | async-start | bytes 32768 | tf_op jit(solution)/shard_map/slice | solution.py:324
  6.5 19.2 %slice-start.3 = ((bf16[32,672]{1,0:T(8,128)(2,1)}), bf16[32,512]{1,0:T(8,128)(2,1)S(1)}, s32[]{:S(2)}) async-start(bf16[32,672]{1,0:T(8,128)(2,1)} %param.26), calls=%async_computation.10 | async-start | bytes 65536 | tf_op jit(solution)/shard_map/slice | solution.py:331
  6.5 19.2 %copy-start.4 = (bf16[84,256]{1,0:T(8,128)(2,1)S(1)}, bf16[84,256]{1,0:T(8,128)(2,1)}, u32[]{:S(2)}) copy-start(bf16[84,256]{1,0:T(8,128)(2,1)} %param.21) | copy-start | bytes 129028
  6.5 19.2 %copy-start.7 = (bf16[84,128]{1,0:T(8,128)(2,1)S(1)}, bf16[84,128]{1,0:T(8,128)(2,1)}, u32[]{:S(2)}) copy-start(bf16[84,128]{1,0:T(8,128)(2,1)} %param.22) | copy-start | bytes 64516
  6.5 19.2 %copy-start.6 = (bf16[84,128]{1,0:T(8,128)(2,1)S(1)}, bf16[84,128]{1,0:T(8,128)(2,1)}, u32[]{:S(2)}) copy-start(bf16[84,128]{1,0:T(8,128)(2,1)} %param.23) | copy-start | bytes 64516
  6.6 26.4 %copy-start.11 = (bf16[256,672]{0,1:T(8,128)(2,1)S(1)}, bf16[256,672]{0,1:T(8,128)(2,1)}, u32[]{:S(2)}) copy-start(bf16[256,672]{0,1:T(8,128)(2,1)} %param.14) | copy-start | bytes 1032196
  8.3 33.7 %copy-start.8 = (s32[8]{0:T(128)S(1)}, s32[8]{0:T(128)}, u32[]{:S(2)}) copy-start(s32[8]{0:T(128)} %param.16) | copy-start | bytes 100
  8.3 33.7 %copy-start.10 = (s32[8]{0:T(128)S(1)}, s32[8]{0:T(128)}, u32[]{:S(2)}) copy-start(s32[8]{0:T(128)} %param.17) | copy-start | bytes 100
  9.9 32.0 %all-to-all-start = ((bf16[16,32,144]{2,1,0:T(8,128)(2,1)}), bf16[16,32,144]{2,1,0:T(8,128)(2,1)S(1)}, u32[]{:S(2)}, u32[]{:S(2)}) async-start(bf16[16,32,144]{2,1,0:T(8,128)(2,1)} %broadcast_in_dim.100), calls=%async_computation | async-start | bytes 524288 | tf_op jit(solution)/shard_map/all_to_all | solution.py:60
  25.7 98.9 %all-gather.3.cloned.1.call-start = ((), (), s32[]{:S(2)}) async-start(), calls=%async_computation.6 | async-start | bytes 5013504 | tf_op jit(solution)/shard_map/all_gather | solution.py:386
  25.8 10.2 %collective-permute-start = (bf16[144,512]{1,0:T(8,128)(2,1)S(1)}, bf16[144,512]{1,0:T(8,128)(2,1)S(1)}, u32[]{:S(2)}, u32[]{:S(2)}) collective-permute-start(bf16[144,512]{1,0:T(8,128)(2,1)S(1)} %maximum_maximum_fusion), channel_id=1, source_target_pairs={{0,0},{1,128},{128,1},{129,129},{256,256},{257,384},{384,257},{385... | collective-permute-start | bytes 442376 | tf_op jit(solution)/shard_map/ppermute | solution.py:42
  29.8 8.4 %collective-permute-start.1 = (bf16[144,512]{1,0:T(8,128)(2,1)S(1)}, bf16[144,512]{1,0:T(8,128)(2,1)S(1)}, u32[]{:S(2)}, u32[]{:S(2)}) collective-permute-start(bf16[144,512]{1,0:T(8,128)(2,1)S(1)} %maximum_maximum_fusion), channel_id=1, source_target_pairs={{0,256},{1,384},{128,257},{129,385},{256,0},{257,128},{384,1},{385... | collective-permute-start | bytes 442376 | tf_op jit(solution)/shard_map/ppermute | solution.py:42
  33.0 8.9 %collective-permute-start.2 = (bf16[256,672]{0,1:T(8,128)(2,1)S(1)}, bf16[256,672]{0,1:T(8,128)(2,1)S(1)}, u32[]{:S(2)}, u32[]{:S(2)}) collective-permute-start(bf16[256,672]{0,1:T(8,128)(2,1)S(1)} %copy-done.11), channel_id=1, source_target_pairs={{0,0},{1,128},{128,1},{129,129},{2,2},{3,130},{130,3},{131,131},{4... | collective-permute-start | bytes 1032200 | tf_op jit(solution)/shard_map/ppermute | solution.py:33
  42.2 37.4 %collective-permute-start.3 = (bf16[1152,672]{0,1:T(8,128)(2,1)}, bf16[1152,672]{0,1:T(8,128)(2,1)}, u32[]{:S(2)}, u32[]{:S(2)}) collective-permute-start(bf16[1152,672]{0,1:T(8,128)(2,1)} %param.19), channel_id=1, source_target_pairs={{0,1},{129,128},{2,3},{131,130},{4,5},{133,132},{6,7},{135,134},{8... | collective-permute-start | bytes 4644872 | tf_op jit(solution)/shard_map/ppermute | solution.py:387
  65.1 14.5 %all-to-all-start.2 = ((bf16[8,144,256]{2,1,0:T(8,128)(2,1)}), bf16[8,144,256]{2,1,0:T(8,128)(2,1)S(1)}, u32[]{:S(2)}, u32[]{:S(2)}) async-start(bf16[8,144,256]{2,1,0:T(8,128)(2,1)} %broadcast_in_dim.108), calls=%async_computation.2 | async-start | bytes 1179648 | tf_op jit(solution)/shard_map/all_to_all | solution.py:60
  83.4 43.1 %copy-start.5 = (f32[5376]{0:T(1024)S(1)}, f32[5376]{0:T(1024)}, u32[]{:S(2)}) copy-start(f32[5376]{0:T(1024)} %param.20) | copy-start | bytes 64516
  83.4 41.2 %all-to-all-start.3 = ((bf16[8,672,256]{2,1,0:T(8,128)(2,1)}), bf16[8,672,256]{2,1,0:T(8,128)(2,1)}, u32[]{:S(2)}, u32[]{:S(2)}) async-start(bf16[8,672,256]{2,1,0:T(8,128)(2,1)} %broadcast_in_dim.109), calls=%async_computation.3 | async-start | bytes 5505024 | tf_op jit(solution)/shard_map/all_to_all | solution.py:60
  87.9 36.6 %collective-permute-start.4 = (bf16[672,256]{1,0:T(8,128)(2,1)S(1)}, bf16[672,256]{1,0:T(8,128)(2,1)S(1)}, u32[]{:S(2)}, u32[]{:S(2)}) collective-permute-start(bf16[672,256]{1,0:T(8,128)(2,1)S(1)} %fusion.28), channel_id=1, source_target_pairs={{0,0},{1,128},{128,1},{129,129},{2,2},{3,130},{130,3},{131,131},{4... | collective-permute-start | bytes 1032200 | tf_op jit(solution)/shard_map/ppermute | solution.py:33
  124.5 10.1 %collective-permute-start.5 = (bf16[16,2,144,512]{3,2,1,0:T(8,128)(2,1)}, bf16[16,2,144,512]{3,2,1,0:T(8,128)(2,1)}, u32[]{:S(2)}, u32[]{:S(2)}) collective-permute-start(bf16[16,2,144,512]{3,2,1,0:T(8,128)(2,1)} %bitcast.74), channel_id=1, source_target_pairs={{0,1},{1,0},{2,3},{3,2},{4,5},{5,4},{6,7},{7,6},{8,9},{9,8},{10,11... | collective-permute-start | bytes 14155784 | tf_op jit(solution)/shard_map/ppermute | solution.py:411
  128.2 2.3 %copy-start.1 = (bf16[32,144,512]{2,1,0:T(8,128)(2,1)S(1)}, bf16[32,144,512]{2,1,0:T(8,128)(2,1)}, u32[]{:S(2)}) copy-start(bf16[32,144,512]{2,1,0:T(8,128)(2,1)} %all-gather.3.cloned.1.call-done) | copy-start | bytes 14155780
  130.6 4.1 %copy-start.2 = (f32[128]{0:T(128)S(1)}, f32[128]{0:T(128)}, u32[]{:S(2)}) copy-start(f32[128]{0:T(128)} %param.24) | copy-start | bytes 1540
  130.6 4.1 %copy-start.3 = (f32[128]{0:T(128)S(1)}, f32[128]{0:T(128)}, u32[]{:S(2)}) copy-start(f32[128]{0:T(128)} %param.25) | copy-start | bytes 1540
  139.2 9.6 %collective-permute-start.6 = (bf16[256,256]{1,0:T(8,128)(2,1)S(1)}, bf16[256,256]{1,0:T(8,128)(2,1)S(1)}, u32[]{:S(2)}, u32[]{:S(2)}) collective-permute-start(bf16[256,256]{1,0:T(8,128)(2,1)S(1)} %get-tuple-element.27), channel_id=1, source_target_pairs={{0,16},{8,24},{16,32},{24,40},{32,48},{40,56},{48,64},{56,72},{64,... | collective-permute-start | bytes 393224 | tf_op jit(solution)/shard_map/ppermute | solution.py:55
  143.0 10.6 %collective-permute-start.7 = (bf16[256,256]{1,0:T(8,128)(2,1)S(1)}, bf16[256,256]{1,0:T(8,128)(2,1)S(1)}, u32[]{:S(2)}, u32[]{:S(2)}) collective-permute-start(bf16[256,256]{1,0:T(8,128)(2,1)S(1)} %get-tuple-element.27), channel_id=1, source_target_pairs={{0,8},{8,16},{16,24},{24,32},{32,40},{40,48},{48,56},{56,64},{64,7... | collective-permute-start | bytes 393224 | tf_op jit(solution)/shard_map/ppermute | solution.py:55
  153.6 16.5 %collective-permute-start.8 = (bf16[512,256]{1,0:T(8,128)(2,1)S(1)}, bf16[512,256]{1,0:T(8,128)(2,1)S(1)}, u32[]{:S(2)}, u32[]{:S(2)}) collective-permute-start(bf16[512,256]{1,0:T(8,128)(2,1)S(1)} %pad_maximum_fusion.1), channel_id=1, source_target_pairs={{0,16},{8,24},{16,32},{24,40},{32,48},{40,56},{48,64},{56,72},{64,... | collective-permute-start | bytes 786440 | tf_op jit(solution)/shard_map/ppermute | solution.py:55
  158.3 11.9 %collective-permute-start.9 = (bf16[256,256]{1,0:T(8,128)(2,1)S(1)}, bf16[256,256]{1,0:T(8,128)(2,1)S(1)}, u32[]{:S(2)}, u32[]{:S(2)}) collective-permute-start(bf16[256,256]{1,0:T(8,128)(2,1)S(1)} %get-tuple-element.27), channel_id=1, source_target_pairs={{8,0},{16,8},{24,16},{32,24},{40,32},{48,40},{56,48},{64,56},{72,6... | collective-permute-start | bytes 393224 | tf_op jit(solution)/shard_map/ppermute | solution.py:55
  170.2 21.0 %slice-start = ((s8[4718592]{0:T(1024)(128)(4,1)}), s8[4194304]{0:T(1024)(128)(4,1)S(1)}, s32[]{:S(2)}) async-start(s8[4718592]{0:T(1024)(128)(4,1)} %bitcast.76), calls=%async_computation.7 | async-start | bytes 8388608
  170.8 20.4 %slice-start.1 = ((s8[4718592]{0:T(1024)(128)(4,1)}), s8[524288]{0:T(1024)(128)(4,1)S(1)}, s32[]{:S(2)}) async-start(s8[4718592]{0:T(1024)(128)(4,1)} %bitcast.76), calls=%async_computation.8 | async-start | bytes 1048576
  191.2 16.0 %copy-start.9 = (f32[672]{0:T(1024)S(1)}, f32[672]{0:T(1024)}, u32[]{:S(2)}) copy-start(f32[672]{0:T(1024)} %param.27) | copy-start | bytes 8068
  195.5 11.8 %collective-permute-start.10 = (bf16[672,256]{1,0:T(8,128)(2,1)S(1)}, bf16[672,256]{1,0:T(8,128)(2,1)S(1)}, u32[]{:S(2)}, u32[]{:S(2)}) collective-permute-start(bf16[672,256]{1,0:T(8,128)(2,1)S(1)} %get-tuple-element.29), channel_id=1, source_target_pairs={{0,0},{1,128},{128,1},{129,129},{2,2},{3,130},{130,3},{131,131},{4... | collective-permute-start | bytes 1032200 | tf_op jit(solution)/shard_map/ppermute | solution.py:33
  198.2 8.9 %all-to-all-start.5 = ((f32[16,1,256]{2,1,0:T(1,128)}), f32[16,1,256]{2,1,0:T(1,128)S(1)}, u32[]{:S(2)}, u32[]{:S(2)}) async-start(f32[16,1,256]{2,1,0:T(1,128)} %get-tuple-element.30), calls=%async_computation.5 | async-start | bytes 32768 | tf_op jit(solution)/shard_map/all_to_all | solution.py:444
Sparse Core Ops, SparseCore 0:
  42.0 72.0 all-gather.2

commit v10 on v8

--- a/solution.py
+++ b/solution.py
@@ -429,7 +429,8 @@
     )
     past_count = WINDOW // tok_rows
     near = jnp.concatenate([shifted(own, 2), shifted(own, 1)], axis=0)
-    window = jnp.concatenate([shifted(near, 2), near, own, shifted(own, -1)], axis=0)
+    near, later = lax.optimization_barrier((near, shifted(own, -1)))
+    window = jnp.concatenate([shifted(near, 2), near, own, later], axis=0)
     key_pos = (seq_index - past_count) * tok_rows + jnp.arange(window.shape[0], dtype=jnp.int32)
     allowed = allowed_keys(my_pos, key_pos, starts, total_rows)
     attended = attend(

time: 215 us -> 215 us (level)
  the two profiles are of different devices: /device:TPU:1 before, /device:TPU:6 now
where the time goes in v10:
time: 215 us; the launch traced here: 214 us
  waiting for transfers between devices  75.1 us (35%)
  starting transfers between devices  61.4 us (29%)
  blocking collectives  31.1 us (14%)
  Pallas kernels  14.3 us (7%)
  between operations  14 us (7%)
  local copies, waits for them, and re-layouts  8.13 us (4%)
  other arithmetic  5.23 us (2%)
  matrix products  5 us (2%)
    ppermute x3, waiting for transfers between devices, swapped(): return lax.ppermute(value, ('a', 'core'), [(0, 0), (1, 2), (2, 1), (3, 3)])  38.9 us
    all_to_all x3, starting transfers between devices, exchange(): return lax.all_to_all(spread, axes, 0, 0, tiled=True)  26.7 us
    ppermute x4, waiting for transfers between devices, shifted(): return lax.ppermute(value, ('k', 'z', 'core'), pairs)  17.8 us
    all_to_all x1, blocking collectives, exchange(): return lax.all_to_all(spread, axes, 0, 0, tiled=True)  15.9 us
    ppermute x4, starting transfers between devices, shifted(): return lax.ppermute(value, ('k', 'z', 'core'), pairs)  15.6 us
    all_to_all x1, blocking collectives, body(): lax.all_to_all(frames.astype(jnp.bfloat16), ('k', 'a', 'core'), 0, 0, til...  15.2 us
    all_to_all x3, waiting for transfers between devices, exchange(): return lax.all_to_all(spread, axes, 0, 0, tiled=True)  14.2 us
    ppermute x3, starting transfers between devices, swapped(): return lax.ppermute(value, ('a', 'core'), [(0, 0), (1, 2), (2, 1), (3, 3)])  6.45 us
  transfers between devices with their start and end apart: 16, of which 10 were waited for; matrix products, arithmetic and copies ran while one was open for 5% of the time, Pallas kernels for 2%

profile of v10, /device:TPU:6, one launch (start us, length us, event | category | flops | bytes accessed | tf_op | source)
XLA Modules:
  0.0 214.3 jit_solution(17192226893702669084)
XLA Ops:
  9.9 15.2 %all-to-all-start = ((bf16[16,32,144]{2,1,0:T(8,128)(2,1)}), bf16[16,32,144]{2,1,0:T(8,128)(2,1)S(1)}, u32[]{:S(2)}, u32[]{:S(2)}) async-start(bf16[16,32,144]{2,1,0:T(8,128)(2,1)} %broadcast_in_dim.100), calls=%async_computation | async-start | bytes 524288 | tf_op jit(solution)/shard_map/all_to_all | solution.py:60
  25.3 1.9 collective-permute-start.1
  27.2 3.0 %collective-permute-start = (bf16[144,512]{1,0:T(8,128)(2,1)S(1)}, bf16[144,512]{1,0:T(8,128)(2,1)S(1)}, u32[]{:S(2)}, u32[]{:S(2)}) collective-permute-start(bf16[144,512]{1,0:T(8,128)(2,1)S(1)} %maximum_maximum_fusion), channel_id=1, source_target_pairs={{0,0},{1,128},{128,1},{129,129},{256,256},{257,384},{384,257},{385... | collective-permute-start | bytes 442376 | tf_op jit(solution)/shard_map/ppermute | solution.py:42
  30.2 2.6 %collective-permute-start.2 = (bf16[256,672]{0,1:T(8,128)(2,1)S(1)}, bf16[256,672]{0,1:T(8,128)(2,1)S(1)}, u32[]{:S(2)}, u32[]{:S(2)}) collective-permute-start(bf16[256,672]{0,1:T(8,128)(2,1)S(1)} %copy-done.11), channel_id=1, source_target_pairs={{0,0},{1,128},{128,1},{129,129},{2,2},{3,130},{130,3},{131,131},{4... | collective-permute-start | bytes 1032200 | tf_op jit(solution)/shard_map/ppermute | solution.py:33
  34.7 4.0 %collective-permute-done.2 = bf16[256,672]{0,1:T(8,128)(2,1)S(1)} collective-permute-done((bf16[256,672]{0,1:T(8,128)(2,1)S(1)}, bf16[256,672]{0,1:T(8,128)(2,1)S(1)}, u32[]{:S(2)}, u32[]{:S(2)}) %collective-permute-start.2) | collective-permute-done | bytes 344096 | tf_op jit(solution)/shard_map/ppermute | solution.py:33
  38.8 4.7 %all-to-all-done = bf16[16,32,144]{2,1,0:T(8,128)(2,1)S(1)} async-done(((bf16[16,32,144]{2,1,0:T(8,128)(2,1)}), bf16[16,32,144]{2,1,0:T(8,128)(2,1)S(1)}, u32[]{:S(2)}, u32[]{:S(2)}) %all-to-all-start) | async-done | bytes 147488 | tf_op jit(solution)/shard_map/all_to_all | solution.py:60
  45.3 1.3 fusion.19
  46.6 15.2 %all_to_all.30 = bf16[8,144,256]{2,1,0:T(8,128)(2,1)S(1)} all-to-all(bf16[8,144,256]{2,1,0:T(8,128)(2,1)S(1)} %fusion.19), channel_id=1, replica_groups=mesh['k'=2,'a'=2,'z'=16,'y'=4,'core'=2] {'k','a','core'}, dimensions={0} | all-to-all | bytes 1179648 | tf_op jit(solution)/shard_map/all_to_all | solution.py:392
  62.8 5.9 %all-to-all-start.2 = ((bf16[8,144,256]{2,1,0:T(8,128)(2,1)}), bf16[8,144,256]{2,1,0:T(8,128)(2,1)S(1)}, u32[]{:S(2)}, u32[]{:S(2)}) async-start(bf16[8,144,256]{2,1,0:T(8,128)(2,1)} %broadcast_in_dim.108), calls=%async_computation.2 | async-start | bytes 1179648 | tf_op jit(solution)/shard_map/all_to_all | solution.py:60
  68.8 9.4 %all-to-all-done.2 = bf16[8,144,256]{2,1,0:T(8,128)(2,1)S(1)} async-done(((bf16[8,144,256]{2,1,0:T(8,128)(2,1)}), bf16[8,144,256]{2,1,0:T(8,128)(2,1)S(1)}, u32[]{:S(2)}, u32[]{:S(2)}) %all-to-all-start.2) | async-done | bytes 589856 | tf_op jit(solution)/shard_map/all_to_all | solution.py:60
  78.2 2.0 fusion.28
  80.3 1.7 broadcast_in_dim.109
  82.0 5.6 %all-to-all-start.3 = ((bf16[8,672,256]{2,1,0:T(8,128)(2,1)}), bf16[8,672,256]{2,1,0:T(8,128)(2,1)}, u32[]{:S(2)}, u32[]{:S(2)}) async-start(bf16[8,672,256]{2,1,0:T(8,128)(2,1)} %broadcast_in_dim.109), calls=%async_computation.3 | async-start | bytes 5505024 | tf_op jit(solution)/shard_map/all_to_all | solution.py:60
  87.6 1.9 collective-permute-start.4
  89.5 31.2 %collective-permute-done.4 = bf16[672,256]{1,0:T(8,128)(2,1)S(1)} collective-permute-done((bf16[672,256]{1,0:T(8,128)(2,1)S(1)}, bf16[672,256]{1,0:T(8,128)(2,1)S(1)}, u32[]{:S(2)}, u32[]{:S(2)}) %collective-permute-start.4) | collective-permute-done | bytes 344096 | tf_op jit(solution)/shard_map/ppermute | solution.py:33
  120.8 1.9 collective-permute-start.5
  123.7 2.3 %copy-done.1 = bf16[32,144,512]{2,1,0:T(8,128)(2,1)S(1)} copy-done((bf16[32,144,512]{2,1,0:T(8,128)(2,1)S(1)}, bf16[32,144,512]{2,1,0:T(8,128)(2,1)}, u32[]{:S(2)}) %copy-start.1) | copy-done | bytes 4718616
  126.1 4.5 %shard_map.136 = (f32[256,512]{1,0:T(8,128)S(1)}, f32[1,256]{1,0:T(1,128)S(1)}) custom-call(s32[1]{0:T(128)} %bitcast.9.core_ref, bf16[8,672,256]{2,1,0:T(8,128)(2,1)} %all-to-all-done.3.whole_ref, f32[8,8,768]{2,1,0:T(8,128)S(1)} %broadcast_in_dim.116.gain_ref, bf16[16,2,144,512]{3,2,1,0:T(8,128)(2,1)S(1)} %bitcast.77), custom_call_target="tpu_custom_call" | custom-call | flops 704643072 | bytes 5242880 | tf_op jit(solution)/shard_map/pallas_call | solution.py:177
  130.9 5.5 %shard_map.137 = (bf16[256,256]{1,0:T(8,128)(2,1)S(1)}, bf16[256,256]{1,0:T(8,128)(2,1)S(1)}) custom-call(s32[1]{0:T(128)} %bitcast.9.core_ref, bf16[8,672,256]{2,1,0:T(8,128)(2,1)} %all-to-all-done.3.whole_ref, f32[8,8,768]{2,1,0:T(8,128)S(1)} %broadcast_in_dim.116.gain_ref, bf16[16,2,144,512]{3,2,1,0:T(8,128)(2,1)} %collective-permute-done.5.weight_ref.across_ref, ...), custom_call_target="tpu_custom_call" | custom-call | flops 704643072 | bytes 5242880 | tf_op jit(solution)/shard_map/pallas_call | solution.py:202
  136.4 3.4 %collective-permute-start.7 = (bf16[256,256]{1,0:T(8,128)(2,1)S(1)}, bf16[256,256]{1,0:T(8,128)(2,1)S(1)}, u32[]{:S(2)}, u32[]{:S(2)}) collective-permute-start(bf16[256,256]{1,0:T(8,128)(2,1)S(1)} %get-tuple-element.29), channel_id=1, source_target_pairs={{0,8},{8,16},{16,24},{24,32},{32,40},{40,48},{48,56},{56,64},{64,7... | collective-permute-start | bytes 393224 | tf_op jit(solution)/shard_map/ppermute | solution.py:55
  139.8 4.1 %collective-permute-start.6 = (bf16[256,256]{1,0:T(8,128)(2,1)S(1)}, bf16[256,256]{1,0:T(8,128)(2,1)S(1)}, u32[]{:S(2)}, u32[]{:S(2)}) collective-permute-start(bf16[256,256]{1,0:T(8,128)(2,1)S(1)} %get-tuple-element.29), channel_id=1, source_target_pairs={{0,16},{8,24},{16,32},{24,40},{32,48},{40,56},{48,64},{56,72},{64,... | collective-permute-start | bytes 393224 | tf_op jit(solution)/shard_map/ppermute | solution.py:55
  144.0 6.2 %collective-permute-start.8 = (bf16[256,256]{1,0:T(8,128)(2,1)S(1)}, bf16[256,256]{1,0:T(8,128)(2,1)S(1)}, u32[]{:S(2)}, u32[]{:S(2)}) collective-permute-start(bf16[256,256]{1,0:T(8,128)(2,1)S(1)} %get-tuple-element.29), channel_id=1, source_target_pairs={{8,0},{16,8},{24,16},{32,24},{40,32},{48,40},{56,48},{64,56},{72,6... | collective-permute-start | bytes 393224 | tf_op jit(solution)/shard_map/ppermute | solution.py:55
  150.2 3.4 %collective-permute-done.6 = bf16[256,256]{1,0:T(8,128)(2,1)S(1)} collective-permute-done((bf16[256,256]{1,0:T(8,128)(2,1)S(1)}, bf16[256,256]{1,0:T(8,128)(2,1)S(1)}, u32[]{:S(2)}, u32[]{:S(2)}) %collective-permute-start.6) | collective-permute-done | bytes 131104 | tf_op jit(solution)/shard_map/ppermute | solution.py:55
  153.6 1.9 collective-permute-start.9
  155.5 1.4 fusion.12
  157.0 14.5 %collective-permute-done.9 = bf16[512,256]{1,0:T(8,128)(2,1)S(1)} collective-permute-done((bf16[512,256]{1,0:T(8,128)(2,1)S(1)}, bf16[512,256]{1,0:T(8,128)(2,1)S(1)}, u32[]{:S(2)}, u32[]{:S(2)}) %collective-permute-start.9) | collective-permute-done | bytes 262176 | tf_op jit(solution)/shard_map/ppermute | solution.py:55
  173.3 15.9 %all_to_all.31.own_ref.other_ref = bf16[8,256,256]{2,1,0:T(8,128)(2,1)S(1)} all-to-all(bf16[8,256,256]{2,1,0:T(8,128)(2,1)S(1)} %broadcast_in_dim.192), channel_id=1, replica_groups=mesh['k'=2,'a'=2,'z'=16,'y'=4,'core'=2] {'y','a'}, dimensions={0} | all-to-all | bytes 2097152 | tf_op jit(solution)/shard_map/all_to_all | solution.py:60
  189.2 4.2 %shard_map.138 = (bf16[672,256]{1,0:T(8,128)(2,1)S(1)}, f32[16,1,256]{2,1,0:T(1,128)}) custom-call(s32[1]{0:T(128)} %bitcast.9.core_ref, bf16[8,256,256]{2,1,0:T(8,128)(2,1)S(1)} %all_to_all.31.own_ref.other_ref, bf16[8,256,256]{2,1,0:T(8,128)(2,1)S(1)} %all_to_all.31.own_ref.other_ref, bf16[16,2,144,512]{3,2,1,0:T(8,128)(2,1)S(1)} %bitcast.80, ...), custom_call_target="tpu_custom_call" | custom-call | flops 805306368 | bytes 5242880 | tf_op jit(solution)/shard_map/pallas_call | solution.py:271
  193.4 4.5 %all-to-all-start.5 = ((f32[16,1,256]{2,1,0:T(1,128)}), f32[16,1,256]{2,1,0:T(1,128)S(1)}, u32[]{:S(2)}, u32[]{:S(2)}) async-start(f32[16,1,256]{2,1,0:T(1,128)} %get-tuple-element.34), calls=%async_computation.5 | async-start | bytes 32768 | tf_op jit(solution)/shard_map/all_to_all | solution.py:446
  197.9 2.0 collective-permute-start.10
  200.0 2.7 %all-to-all-done.5 = f32[16,1,256]{2,1,0:T(1,128)S(1)} async-done(((f32[16,1,256]{2,1,0:T(1,128)}), f32[16,1,256]{2,1,0:T(1,128)S(1)}, u32[]{:S(2)}, u32[]{:S(2)}) %all-to-all-start.5) | async-done | bytes 16416 | tf_op jit(solution)/shard_map/all_to_all | solution.py:446
  202.8 3.7 %collective-permute-done.10 = bf16[672,256]{1,0:T(8,128)(2,1)S(1)} collective-permute-done((bf16[672,256]{1,0:T(8,128)(2,1)S(1)}, bf16[672,256]{1,0:T(8,128)(2,1)S(1)}, u32[]{:S(2)}, u32[]{:S(2)}) %collective-permute-start.10) | collective-permute-done | bytes 344096 | tf_op jit(solution)/shard_map/ppermute | solution.py:33
  (99 shorter events, 12.4 us)
Async XLA Ops:
  6.5 1.3 copy-start
  6.5 18.6 %slice-start.2 = ((bf16[32,672]{1,0:T(8,128)(2,1)}), bf16[32,160]{1,0:T(8,128)(2,1)S(1)}, s32[]{:S(2)}) async-start(bf16[32,672]{1,0:T(8,128)(2,1)} %param.26), calls=%async_computation.9 | async-start | bytes 32768 | tf_op jit(solution)/shard_map/slice | solution.py:324
  6.5 18.7 %slice-start.3 = ((bf16[32,672]{1,0:T(8,128)(2,1)}), bf16[32,512]{1,0:T(8,128)(2,1)S(1)}, s32[]{:S(2)}) async-start(bf16[32,672]{1,0:T(8,128)(2,1)} %param.26), calls=%async_computation.10 | async-start | bytes 65536 | tf_op jit(solution)/shard_map/slice | solution.py:331
  6.5 18.6 %copy-start.6 = (bf16[84,128]{1,0:T(8,128)(2,1)S(1)}, bf16[84,128]{1,0:T(8,128)(2,1)}, u32[]{:S(2)}) copy-start(bf16[84,128]{1,0:T(8,128)(2,1)} %param.23) | copy-start | bytes 64516
  6.5 18.6 %copy-start.7 = (bf16[84,128]{1,0:T(8,128)(2,1)S(1)}, bf16[84,128]{1,0:T(8,128)(2,1)}, u32[]{:S(2)}) copy-start(bf16[84,128]{1,0:T(8,128)(2,1)} %param.22) | copy-start | bytes 64516
  6.5 18.6 %copy-start.4 = (bf16[84,256]{1,0:T(8,128)(2,1)S(1)}, bf16[84,256]{1,0:T(8,128)(2,1)}, u32[]{:S(2)}) copy-start(bf16[84,256]{1,0:T(8,128)(2,1)} %param.21) | copy-start | bytes 129028
  6.6 23.6 %copy-start.11 = (bf16[256,672]{0,1:T(8,128)(2,1)S(1)}, bf16[256,672]{0,1:T(8,128)(2,1)}, u32[]{:S(2)}) copy-start(bf16[256,672]{0,1:T(8,128)(2,1)} %param.14) | copy-start | bytes 1032196
  8.3 35.3 %copy-start.8 = (s32[8]{0:T(128)S(1)}, s32[8]{0:T(128)}, u32[]{:S(2)}) copy-start(s32[8]{0:T(128)} %param.16) | copy-start | bytes 100
  8.3 35.3 %copy-start.10 = (s32[8]{0:T(128)S(1)}, s32[8]{0:T(128)}, u32[]{:S(2)}) copy-start(s32[8]{0:T(128)} %param.17) | copy-start | bytes 100
  9.9 33.6 %all-to-all-start = ((bf16[16,32,144]{2,1,0:T(8,128)(2,1)}), bf16[16,32,144]{2,1,0:T(8,128)(2,1)S(1)}, u32[]{:S(2)}, u32[]{:S(2)}) async-start(bf16[16,32,144]{2,1,0:T(8,128)(2,1)} %broadcast_in_dim.100), calls=%async_computation | async-start | bytes 524288 | tf_op jit(solution)/shard_map/all_to_all | solution.py:60
  25.1 95.7 %all-gather.3.cloned.1.call-start = ((), (), s32[]{:S(2)}) async-start(), calls=%async_computation.6 | async-start | bytes 5013504 | tf_op jit(solution)/shard_map/all_gather | solution.py:386
  25.3 8.7 %collective-permute-start.1 = (bf16[144,512]{1,0:T(8,128)(2,1)S(1)}, bf16[144,512]{1,0:T(8,128)(2,1)S(1)}, u32[]{:S(2)}, u32[]{:S(2)}) collective-permute-start(bf16[144,512]{1,0:T(8,128)(2,1)S(1)} %maximum_maximum_fusion), channel_id=1, source_target_pairs={{0,256},{1,384},{128,257},{129,385},{256,0},{257,128},{384,1},{385... | collective-permute-start | bytes 442376 | tf_op jit(solution)/shard_map/ppermute | solution.py:42
  27.2 6.8 %collective-permute-start = (bf16[144,512]{1,0:T(8,128)(2,1)S(1)}, bf16[144,512]{1,0:T(8,128)(2,1)S(1)}, u32[]{:S(2)}, u32[]{:S(2)}) collective-permute-start(bf16[144,512]{1,0:T(8,128)(2,1)S(1)} %maximum_maximum_fusion), channel_id=1, source_target_pairs={{0,0},{1,128},{128,1},{129,129},{256,256},{257,384},{384,257},{385... | collective-permute-start | bytes 442376 | tf_op jit(solution)/shard_map/ppermute | solution.py:42
  30.2 8.6 %collective-permute-start.2 = (bf16[256,672]{0,1:T(8,128)(2,1)S(1)}, bf16[256,672]{0,1:T(8,128)(2,1)S(1)}, u32[]{:S(2)}, u32[]{:S(2)}) collective-permute-start(bf16[256,672]{0,1:T(8,128)(2,1)S(1)} %copy-done.11), channel_id=1, source_target_pairs={{0,0},{1,128},{128,1},{129,129},{2,2},{3,130},{130,3},{131,131},{4... | collective-permute-start | bytes 1032200 | tf_op jit(solution)/shard_map/ppermute | solution.py:33
  43.9 34.4 %collective-permute-start.3 = (bf16[1152,672]{0,1:T(8,128)(2,1)}, bf16[1152,672]{0,1:T(8,128)(2,1)}, u32[]{:S(2)}, u32[]{:S(2)}) collective-permute-start(bf16[1152,672]{0,1:T(8,128)(2,1)} %param.19), channel_id=1, source_target_pairs={{0,1},{129,128},{2,3},{131,130},{4,5},{133,132},{6,7},{135,134},{8... | collective-permute-start | bytes 4644872 | tf_op jit(solution)/shard_map/ppermute | solution.py:387
  62.8 15.5 %all-to-all-start.2 = ((bf16[8,144,256]{2,1,0:T(8,128)(2,1)}), bf16[8,144,256]{2,1,0:T(8,128)(2,1)S(1)}, u32[]{:S(2)}, u32[]{:S(2)}) async-start(bf16[8,144,256]{2,1,0:T(8,128)(2,1)} %broadcast_in_dim.108), calls=%async_computation.2 | async-start | bytes 1179648 | tf_op jit(solution)/shard_map/all_to_all | solution.py:60
  82.0 40.7 %copy-start.5 = (f32[5376]{0:T(1024)S(1)}, f32[5376]{0:T(1024)}, u32[]{:S(2)}) copy-start(f32[5376]{0:T(1024)} %param.20) | copy-start | bytes 64516
  82.0 38.7 %all-to-all-start.3 = ((bf16[8,672,256]{2,1,0:T(8,128)(2,1)}), bf16[8,672,256]{2,1,0:T(8,128)(2,1)}, u32[]{:S(2)}, u32[]{:S(2)}) async-start(bf16[8,672,256]{2,1,0:T(8,128)(2,1)} %broadcast_in_dim.109), calls=%async_computation.3 | async-start | bytes 5505024 | tf_op jit(solution)/shard_map/all_to_all | solution.py:60
  87.6 33.1 %collective-permute-start.4 = (bf16[672,256]{1,0:T(8,128)(2,1)S(1)}, bf16[672,256]{1,0:T(8,128)(2,1)S(1)}, u32[]{:S(2)}, u32[]{:S(2)}) collective-permute-start(bf16[672,256]{1,0:T(8,128)(2,1)S(1)} %fusion.28), channel_id=1, source_target_pairs={{0,0},{1,128},{128,1},{129,129},{2,2},{3,130},{130,3},{131,131},{4... | collective-permute-start | bytes 1032200 | tf_op jit(solution)/shard_map/ppermute | solution.py:33
  120.8 10.1 %collective-permute-start.5 = (bf16[16,2,144,512]{3,2,1,0:T(8,128)(2,1)}, bf16[16,2,144,512]{3,2,1,0:T(8,128)(2,1)}, u32[]{:S(2)}, u32[]{:S(2)}) collective-permute-start(bf16[16,2,144,512]{3,2,1,0:T(8,128)(2,1)} %bitcast.76), channel_id=1, source_target_pairs={{0,1},{1,0},{2,3},{3,2},{4,5},{5,4},{6,7},{7,6},{8,9},{9,8},{10,11... | collective-permute-start | bytes 14155784 | tf_op jit(solution)/shard_map/ppermute | solution.py:412
  123.7 2.3 %copy-start.1 = (bf16[32,144,512]{2,1,0:T(8,128)(2,1)S(1)}, bf16[32,144,512]{2,1,0:T(8,128)(2,1)}, u32[]{:S(2)}) copy-start(bf16[32,144,512]{2,1,0:T(8,128)(2,1)} %all-gather.3.cloned.1.call-done) | copy-start | bytes 14155780
  126.1 4.9 %copy-start.2 = (f32[128]{0:T(128)S(1)}, f32[128]{0:T(128)}, u32[]{:S(2)}) copy-start(f32[128]{0:T(128)} %param.24) | copy-start | bytes 1540
  126.1 4.9 %copy-start.3 = (f32[128]{0:T(128)S(1)}, f32[128]{0:T(128)}, u32[]{:S(2)}) copy-start(f32[128]{0:T(128)} %param.25) | copy-start | bytes 1540
  136.4 13.8 %collective-permute-start.7 = (bf16[256,256]{1,0:T(8,128)(2,1)S(1)}, bf16[256,256]{1,0:T(8,128)(2,1)S(1)}, u32[]{:S(2)}, u32[]{:S(2)}) collective-permute-start(bf16[256,256]{1,0:T(8,128)(2,1)S(1)} %get-tuple-element.29), channel_id=1, source_target_pairs={{0,8},{8,16},{16,24},{24,32},{32,40},{40,48},{48,56},{56,64},{64,7... | collective-permute-start | bytes 393224 | tf_op jit(solution)/shard_map/ppermute | solution.py:55
  139.8 13.8 %collective-permute-start.6 = (bf16[256,256]{1,0:T(8,128)(2,1)S(1)}, bf16[256,256]{1,0:T(8,128)(2,1)S(1)}, u32[]{:S(2)}, u32[]{:S(2)}) collective-permute-start(bf16[256,256]{1,0:T(8,128)(2,1)S(1)} %get-tuple-element.29), channel_id=1, source_target_pairs={{0,16},{8,24},{16,32},{24,40},{32,48},{40,56},{48,64},{56,72},{64,... | collective-permute-start | bytes 393224 | tf_op jit(solution)/shard_map/ppermute | solution.py:55
  144.0 9.6 %collective-permute-start.8 = (bf16[256,256]{1,0:T(8,128)(2,1)S(1)}, bf16[256,256]{1,0:T(8,128)(2,1)S(1)}, u32[]{:S(2)}, u32[]{:S(2)}) collective-permute-start(bf16[256,256]{1,0:T(8,128)(2,1)S(1)} %get-tuple-element.29), channel_id=1, source_target_pairs={{8,0},{16,8},{24,16},{32,24},{40,32},{48,40},{56,48},{64,56},{72,6... | collective-permute-start | bytes 393224 | tf_op jit(solution)/shard_map/ppermute | solution.py:55
  153.6 17.8 %collective-permute-start.9 = (bf16[512,256]{1,0:T(8,128)(2,1)S(1)}, bf16[512,256]{1,0:T(8,128)(2,1)S(1)}, u32[]{:S(2)}, u32[]{:S(2)}) collective-permute-start(bf16[512,256]{1,0:T(8,128)(2,1)S(1)} %pad_maximum_fusion.1), channel_id=1, source_target_pairs={{0,16},{8,24},{16,32},{24,40},{32,48},{40,56},{48,64},{56,72},{64,... | collective-permute-start | bytes 786440 | tf_op jit(solution)/shard_map/ppermute | solution.py:55
  171.5 17.7 %slice-start = ((s8[4718592]{0:T(1024)(128)(4,1)}), s8[4194304]{0:T(1024)(128)(4,1)S(1)}, s32[]{:S(2)}) async-start(s8[4718592]{0:T(1024)(128)(4,1)} %bitcast.78), calls=%async_computation.7 | async-start | bytes 8388608
  172.1 17.1 %slice-start.1 = ((s8[4718592]{0:T(1024)(128)(4,1)}), s8[524288]{0:T(1024)(128)(4,1)S(1)}, s32[]{:S(2)}) async-start(s8[4718592]{0:T(1024)(128)(4,1)} %bitcast.78), calls=%async_computation.8 | async-start | bytes 1048576
  189.2 17.3 %copy-start.9 = (f32[672]{0:T(1024)S(1)}, f32[672]{0:T(1024)}, u32[]{:S(2)}) copy-start(f32[672]{0:T(1024)} %param.27) | copy-start | bytes 8068
  193.4 9.2 %all-to-all-start.5 = ((f32[16,1,256]{2,1,0:T(1,128)}), f32[16,1,256]{2,1,0:T(1,128)S(1)}, u32[]{:S(2)}, u32[]{:S(2)}) async-start(f32[16,1,256]{2,1,0:T(1,128)} %get-tuple-element.34), calls=%async_computation.5 | async-start | bytes 32768 | tf_op jit(solution)/shard_map/all_to_all | solution.py:446
  197.9 8.6 %collective-permute-start.10 = (bf16[672,256]{1,0:T(8,128)(2,1)S(1)}, bf16[672,256]{1,0:T(8,128)(2,1)S(1)}, u32[]{:S(2)}, u32[]{:S(2)}) collective-permute-start(bf16[672,256]{1,0:T(8,128)(2,1)S(1)} %get-tuple-element.33), channel_id=1, source_target_pairs={{0,0},{1,128},{128,1},{129,129},{2,2},{3,130},{130,3},{131,131},{4... | collective-permute-start | bytes 1032200 | tf_op jit(solution)/shard_map/ppermute | solution.py:33
Sparse Core Ops, SparseCore 0:
  43.6 76.9 all-gather.2
